TPU v7x, 256 devices: a whole 4x4x8 slice. The times are simulated.
256 devices in a mesh: replica: 32 (over y, z_hi, core), fsdp: 2 (over z_lo), tensor: 4 (over x).
Axes of the slice: x: 4, y: 4, z: 8 (z_hi: 4, z_lo: 2; z = z_hi * 2 + z_lo), core: 2. Of those that a mesh axis runs over, the one named last changes fastest.
Arguments:
- anchor: float32 [256, 28672], P('fsdp', 'tensor')
- local_weights: float32 [32, 256, 28672], P('replica', 'fsdp', 'tensor')
- momentum: float32 [256, 4, 7168], P('fsdp', 'tensor', 'replica'), may hold values from -3 to 3
Outputs:
- new_anchor: float32 [256, 28672], P('fsdp', 'tensor')
- new_momentum: float32 [256, 4, 7168], P('fsdp', 'tensor', 'replica')
All inputs are finite; a program needn't handle non-finite values.
Results may differ from a plain program's by a relative error of at most 0.00013.
Values sent between devices are 32-bit elements; how exact they have to be, the bound alone decides.
No kernel may reach another device: no remote copies, remote signals or barrier semaphores. Data moves between devices by JAX's collectives and lax.ppermute only.
A program may use at most 64 MiB of HBM per device.

v0:
```python
import math

import jax
import jax.numpy as jnp
from jax import lax
from jax.sharding import PartitionSpec as P

momentum_decay = 0.9
outer_rate = 0.7
clip_rms = 0.25


def on_device(anchor, local_weights, momentum):
    drift_term = anchor - local_weights[0]
    replicas = lax.axis_size("replica")
    elements = anchor.shape[0] * anchor.shape[1] * lax.axis_size("fsdp") * lax.axis_size("tensor")
    ceiling = clip_rms * math.sqrt(elements)
    summed = lax.psum(drift_term, "replica")
    pseudo_grad = summed / replicas
    squares = lax.psum(jnp.sum(pseudo_grad * pseudo_grad), ("fsdp", "tensor"))
    gathered = lax.all_gather(momentum, "replica", axis=2, tiled=True)
    moment_whole = gathered[:, 0, :]
    scaling = ceiling / jnp.maximum(jnp.sqrt(squares), ceiling)
    clipped = pseudo_grad * scaling
    moment_next = momentum_decay * moment_whole + clipped
    update = clipped + momentum_decay * moment_next
    new_anchor = anchor - outer_rate * update
    own_width = momentum.shape[2]
    own_cols = lax.dynamic_slice_in_dim(
        moment_next, lax.axis_index("replica") * own_width, own_width, 1
    )
    return (new_anchor, own_cols[:, None, :])


def solution(mesh):
    in_specs = (P("fsdp", "tensor"), P("replica", "fsdp", "tensor"), P("fsdp", "tensor", "replica"))
    out_specs = (P("fsdp", "tensor"), P("fsdp", "tensor", "replica"))
    return jax.shard_map(
        on_device, mesh=mesh, in_specs=in_specs, out_specs=out_specs, check_vma=False
    )
```

profile of v0, /device:TPU:1, one launch (start us, length us, event | category | flops | bytes accessed | tf_op | source)
XLA Modules:
  0.0 409.2 jit_solution(14211219817070265154)
XLA Ops:
  7.2 0.0 all-reduce.2.cloned.1.call-start
  7.2 5.3 %copy.10 = f32[128,7168]{0,1:T(8,128)} copy(f32[128,7168]{1,0:T(8,128)} %param.3) | data formatting | bytes 7340032 | tf_op args[0]
  12.5 5.3 %copy.7 = f32[1,128,7168]{1,2,0:T(8,128)} copy(f32[1,128,7168]{2,1,0:T(8,128)} %param.4) | data formatting | bytes 7340032 | tf_op args[1]
  17.7 5.4 %bitcast_subtract_fusion = f32[128,7168]{0,1:T(8,128)} fusion(f32[128,7168]{0,1:T(8,128)} %copy.10, f32[1,128,7168]{1,2,0:T(8,128)} %copy.7), kind=kLoop, calls=%fused_computation | loop fusion | flops 917504 | bytes 11010048 | tf_op jit(solution)/shard_map/sub | solution.py:14
  23.2 0.0 all-reduce.2.cloned.1.call-update
  23.2 0.0 all-gather.2.cloned.1.call-start
  23.2 0.7 all-gather.2.cloned.1.call-update
  24.0 299.1 %all-reduce.2.cloned.1.call-done = f32[128,7168]{0,1:T(8,128)} async-done(((f32[128,7168]{0,1:T(8,128)}), f32[128,7168]{0,1:T(8,128)}) %all-reduce.2.cloned.1.call-update) | async-done | bytes 3670032 | tf_op jit(solution)/shard_map/psum | solution.py:18
  323.0 3.6 multiply_reduce_fusion
  326.6 16.1 %psum.15 = f32[]{:T(128)} all-reduce(f32[]{:T(128)} %multiply_reduce_fusion), channel_id=1, replica_groups=mesh['replica'=32,'fsdp'=2,'tensor'=4] {'fsdp','tensor'}, use_global_device_ids=true, to_apply=%region_2.0 | all-reduce | flops 1 | bytes 8 | tf_op jit(solution)/shard_map/psum | solution.py:20
  343.5 41.1 %all-gather.2.cloned.1.call-done = f32[128,1,7168]{0,1,2:T(1,128)} async-done(((f32[128,1,224]{0,1,2:T(1,128)}), f32[128,1,7168]{0,1,2:T(1,128)}) %all-gather.2.cloned.1.call-update) | async-done | bytes 3670032 | tf_op jit(solution)/shard_map/all_gather | solution.py:21
  384.6 0.0 copy-start
  384.6 0.0 copy-start.1
  384.6 7.2 %broadcast_multiply_fusion = f32[128,1,7168]{0,1,2:T(1,128)S(1)} fusion(f32[128,1,7168]{0,1,2:T(1,128)} %all-gather.2.cloned.1.call-done), kind=kLoop, calls=%fused_computation.4 | loop fusion | flops 917504 | bytes 7340032 | tf_op jit(solution)/shard_map/mul | solution.py:25
  391.8 0.0 copy-done
  391.8 0.0 copy-done.1
  391.9 3.7 multiply_add_fusion
  395.5 5.2 %copy.11 = f32[128,7168]{1,0:T(8,128)} copy(f32[128,7168]{0,1:T(8,128)} %get-tuple-element.5) | data formatting | bytes 7340032
  400.8 1.6 dynamic-slice_bitcast_fusion
Async XLA Ops:
  7.2 315.9 %all-reduce.2.cloned.1.call-start = ((), (), s32[]{:S(2)}) async-start(), calls=%async_computation | async-start | bytes 7340032 | tf_op jit(solution)/shard_map/psum | solution.py:18
  23.2 361.4 %all-gather.2.cloned.1.call-start = ((), (), s32[]{:S(2)}) async-start(), calls=%async_computation.1 | async-start | bytes 3784704 | tf_op jit(solution)/shard_map/all_gather | solution.py:21
  384.6 7.2 %copy-start = (f32[128,7168]{0,1:T(8,128)S(1)}, f32[128,7168]{0,1:T(8,128)}, u32[]{:S(2)}) copy-start(f32[128,7168]{0,1:T(8,128)} %copy.10) | copy-start | bytes 11010052
  384.6 7.3 %copy-start.1 = (f32[128,7168]{0,1:T(8,128)S(1)}, f32[128,7168]{0,1:T(8,128)}, u32[]{:S(2)}) copy-start(f32[128,7168]{0,1:T(8,128)} %all-reduce.2.cloned.1.call-done) | copy-start | bytes 11010052
Sparse Core Ops, SparseCore 0:
  23.3 299.6 all-reduce.1
  325.9 58.6 all-gather.1
where the time goes:
time: 410 us; the launch traced here: 409 us
  waiting for transfers between devices  341 us (83%)
  other arithmetic  19.9 us (5%)
  local copies, waits for them, and re-layouts  17.3 us (4%)
  blocking collectives  16.1 us (4%)
  between operations  14.8 us (4%)
    psum x1, waiting for transfers between devices, on_device(): summed = lax.psum(drift_term, 'replica')  299 us
    all_gather x1, waiting for transfers between devices, on_device(): gathered = lax.all_gather(momentum, 'replica', axis=2, tiled=True)  41.1 us
    psum x1, blocking collectives, on_device(): squares = lax.psum(jnp.sum(pseudo_grad * pseudo_grad), ('fsdp', 'tensor'))  16.1 us
    unnamed x7, local copies, waits for them, and re-layouts  15.8 us
  transfers between devices with their start and end apart: 2, of which 2 were waited for; matrix products, arithmetic and copies ran while one was open for 1% of the time, Pallas kernels for 0%

commit v1 on v0

v1 whole, which is shorter than its diff:
```python
import math

import jax
import jax.numpy as jnp
from jax import lax
from jax.sharding import Mesh, PartitionSpec as P

momentum_decay = 0.9
outer_rate = 0.7
clip_rms = 0.25

REPLICA = ("y", "zh", "core")
SUB = 8
LANE = 128


def swap(x, axis, mask):
    n = lax.axis_size(axis)
    return lax.ppermute(x, axis, [(i, i ^ mask) for i in range(n)])


def shift(x, axis, by):
    n = lax.axis_size(axis)
    return lax.ppermute(x, axis, [(i, (i + by) % n) for i in range(n)])


def tiles(x):
    rows, cols = x.shape
    return x.reshape(rows // SUB, SUB, cols // LANE, LANE).transpose(0, 2, 1, 3)


def untiles(x):
    blocks, lanes = x.shape[:2]
    return x.transpose(0, 2, 1, 3).reshape(blocks * SUB, lanes * LANE)


def gather4(x, axis):
    me = lax.axis_index(axis)
    parts = [(0, x)] + [(by, shift(x, axis, by)) for by in (1, 3, 2)]
    whole = jnp.zeros((4,) + x.shape, x.dtype)
    for by, part in parts:
        whole = lax.dynamic_update_index_in_dim(whole, part, (me - by) % 4, 0)
    return whole


def on_device(anchor, local_weights, momentum):
    y, zh, core = (lax.axis_index(a) for a in REPLICA)
    replicas = math.prod(lax.axis_size(a) for a in REPLICA)
    elements = anchor.shape[0] * anchor.shape[1] * lax.axis_size("zl") * lax.axis_size("x")
    ceiling = clip_rms * math.sqrt(elements)

    a_tiles, l_tiles = tiles(anchor), tiles(local_weights[0])
    blocks, lanes = a_tiles.shape[:2]
    quarter = lanes // 4

    gray_y, gray_z = (y ^ (y >> 1)) & 1, (zh ^ (zh >> 1)) & 1
    streams = (
        (("y", 1, gray_y), ("y", 3, y >> 1), ("zh", 1, gray_z), ("zh", 3, zh >> 1)),
        (("y", 3, y >> 1), ("y", 1, y & 1), ("zh", 3, zh >> 1), ("zh", 1, zh & 1)),
    )

    def drift(stream, of_core, row, count):
        at = (row, (2 * stream + of_core) * quarter, 0, 0)
        size = (count, quarter, SUB, LANE)
        return lax.dynamic_slice(a_tiles, at, size) - lax.dynamic_slice(l_tiles, at, size)

    received = [[(0, swap(drift(s, 1 - core, 0, blocks), "core", 1))] for s in (0, 1)]
    first = [0, 0]
    count = blocks

    def total(s, row, n):
        value = drift(s, core, row, n)
        for origin, part in received[s]:
            value = value + lax.dynamic_slice_in_dim(part, row - origin, n, 0)
        return value

    for step in range(4):
        count //= 2
        for s in (0, 1):
            axis, mask, bit = streams[s][step]
            sent = total(s, first[s] + (1 - bit) * count, count)
            first[s] = first[s] + bit * count
            received[s].append((first[s], swap(sent, axis, mask)))
    own = [total(s, first[s], count) * (1.0 / replicas) for s in (0, 1)]

    squares = sum(jnp.sum(p * p, axis=(0, 1)) for p in own)
    for axis, mask in (("x", 1), ("x", 2), ("zl", 1), ("core", 1), ("y", 1), ("zh", 1), ("y", 3), ("zh", 3)):
        squares = squares + swap(squares, axis, mask)
    norm = jnp.sqrt(jnp.sum(squares))
    scaling = ceiling / jnp.maximum(norm, ceiling)

    own_moment = momentum[:, 0, :].T
    shard = own_moment.shape[0]
    gathered = own_moment.reshape(shard // SUB, SUB, LANE)
    gathered = gather4(gathered, "zh")
    gathered = gather4(gathered, "y")
    other = swap(gathered, "core", 1)
    moment = jnp.stack([jnp.where(core == 0, gathered, other), jnp.where(core == 0, other, gathered)], 2)
    moment = tiles(moment.reshape(replicas * shard, LANE).T)
    rest = a_tiles - outer_rate * momentum_decay * momentum_decay * moment

    for step in (3, 2, 1, 0):
        for s in (0, 1):
            axis, mask, bit = streams[s][step]
            other = swap(own[s], axis, mask)
            low, high = jnp.where(bit == 0, own[s], other), jnp.where(bit == 0, other, own[s])
            own[s] = jnp.concatenate([low, high], 0)
    pieces = []
    for s in (0, 1):
        other = swap(own[s], "core", 1)
        pieces += [jnp.where(core == 0, own[s], other), jnp.where(core == 0, other, own[s])]
    pseudo_grad = jnp.concatenate(pieces, 1)

    new_anchor = rest - (outer_rate * (1.0 + momentum_decay)) * scaling * pseudo_grad

    at = (y * 8 + zh * 2 + core) * shard
    tile_at = jnp.minimum(at // LANE, lanes - 3)
    cols = lax.dynamic_slice_in_dim(pseudo_grad, tile_at, 3, 1)
    cols = cols.transpose(1, 3, 0, 2).reshape(3 * LANE // SUB, SUB, LANE)
    cols = lax.dynamic_slice_in_dim(cols, (at - tile_at * LANE) // SUB, shard // SUB, 0)
    new_moment = momentum_decay * own_moment + scaling * cols.reshape(shard, LANE)
    return untiles(new_anchor), new_moment.T[:, None, :]


def solution(mesh):
    fine = Mesh(mesh.devices.reshape(4, 4, 2, 2, 4), ("y", "zh", "core", "zl", "x"))
    in_specs = (P("zl", "x"), P(REPLICA, "zl", "x"), P("zl", "x", REPLICA))
    out_specs = (P("zl", "x"), P("zl", "x", REPLICA))
    return jax.shard_map(on_device, mesh=fine, in_specs=in_specs, out_specs=out_specs, check_vma=False)
```

time: 410 us -> 184 us (0.45)
  waiting for transfers between devices: 341 us -> 58.1 us
  starting transfers between devices: 0.08 us -> 71.8 us
  blocking collectives: 16.1 us -> 0 us
  between operations: 14.8 us -> 2.02 us
  local copies, waits for them, and re-layouts: 17.3 us -> 27.4 us
    psum x1 -> x0, waiting for transfers between devices: 299 us -> none  [on_device(): summed = lax.psum(drift_term, 'replica')]
    ppermute x0 -> x35, starting transfers between devices: none -> 71.8 us  [the longest x29 59.4 us: swap(): return lax.ppermute(x, axis, [(i, i ^ mask) for i in range(n)])]
    ppermute x0 -> x35, waiting for transfers between devices: none -> 58.1 us  [the longest x29 49.7 us: swap(): return lax.ppermute(x, axis, [(i, i ^ mask) for i in range(n)])]
    all_gather x1 -> x0, waiting for transfers between devices: 41.1 us -> none  [on_device(): gathered = lax.all_gather(momentum, 'replica', axis=2, tiled=True)]
    psum x1 -> x0, blocking collectives: 16.1 us -> none  [on_device(): squares = lax.psum(jnp.sum(pseudo_grad * pseudo_grad), ('fsdp', 'tensor'))]
    unnamed x7 -> x24, local copies, waits for them, and re-layouts: 15.8 us -> 7.79 us
    select_n x0 -> x10, other arithmetic: none -> 6.2 us  [the longest x2 3.8 us: on_device(): jnp.where(core == 0, own[s], other)]
    mul x0 -> x1, local copies, waits for them, and re-layouts: none -> 5.31 us  [on_device(): rest = a_tiles - outer_rate * momentum_decay * momentum_decay * moment]
  transfers between devices with their start and end apart: 2 -> 35, of which waited for: 2 -> 17; matrix products, arithmetic and copies ran while one was open for 1% -> 16% of each run, Pallas kernels for 0% -> 0%
where the time goes in v1:
time: 184 us; the launch traced here: 183 us
  starting transfers between devices  71.8 us (39%)
  waiting for transfers between devices  58.1 us (32%)
  local copies, waits for them, and re-layouts  27.4 us (15%)
  other arithmetic  23.8 us (13%)
  between operations  2.02 us (1%)
    ppermute x29, starting transfers between devices, swap(): return lax.ppermute(x, axis, [(i, i ^ mask) for i in range(n)])  59.4 us
    ppermute x29, waiting for transfers between devices, swap(): return lax.ppermute(x, axis, [(i, i ^ mask) for i in range(n)])  49.7 us
    ppermute x6, starting transfers between devices, shift(): return lax.ppermute(x, axis, [(i, (i + by) % n) for i in range(n)])  12.4 us
    ppermute x6, waiting for transfers between devices, shift(): return lax.ppermute(x, axis, [(i, (i + by) % n) for i in range(n)])  8.34 us
    unnamed x24, local copies, waits for them, and re-layouts  7.79 us
    add x5, other arithmetic, total(): value = value + lax.dynamic_slice_in_dim(part, row - origin, n, 0)  6.89 us
    mul x1, local copies, waits for them, and re-layouts, on_device(): rest = a_tiles - outer_rate * momentum_decay * momentum_decay * moment  5.31 us
    another operation x1, local copies, waits for them, and re-layouts, tiles(): return x.reshape(rows // SUB, SUB, cols // LANE, LANE).transpose(0, 2, 1, 3)  4.48 us
  transfers between devices with their start and end apart: 35, of which 17 were waited for; matrix products, arithmetic and copies ran while one was open for 16% of the time, Pallas kernels for 0%

profile of v1, /device:TPU:1, one launch (start us, length us, event | category | flops | bytes accessed | tf_op | source)
XLA Modules:
  0.0 183.1 jit_solution(2380781185323461082)
XLA Ops:
  0.6 4.5 %copy_bitcast_fusion.1 = (f32[16,8,56,128]{3,2,1,0:T(8,128)S(1)}, f32[16,8,56,128]{3,2,1,0:T(8,128)S(1)}) fusion(f32[16,8,56,128]{3,1,2,0:T(8,128)} %bitcast.110, f32[16,8,56,128]{3,1,2,0:T(8,128)} %bitcast.107), kind=kLoop, calls=%fused_computation.1 | loop fusion | bytes 14680064 | tf_op jit(solution)/shard_map/reshape;squeeze | solution.py:29
  6.9 1.3 copy-done.1
  8.2 3.2 %collective-permute-start.7 = (f32[16,14,8,128]{3,2,1,0:T(8,128)S(1)}, f32[16,14,8,128]{3,2,1,0:T(8,128)S(1)}, u32[]{:S(2)}, u32[]{:S(2)}) collective-permute-start(f32[16,14,8,128]{3,2,1,0:T(8,128)S(1)} %copy.32), channel_id=1, source_target_pairs={{0,8},{8,0},{1,9},{9,1},{2,10},{10,2},{3,11},{11,3},{4,12},{12,4},... | collective-permute-start | bytes 2752520 | tf_op jit(solution)/shard_map/ppermute | solution.py:19
  11.4 1.2 copy.38
  12.7 5.2 %collective-permute-start.2 = (f32[28,8,128]{2,1,0:T(8,128)S(1)}, f32[28,8,128]{2,1,0:T(8,128)S(1)}, u32[]{:S(2)}, u32[]{:S(2)}) collective-permute-start(f32[28,8,128]{2,1,0:T(8,128)S(1)} %bitcast.112), channel_id=1, source_target_pairs={{0,32},{16,48},{32,0},{48,16},{1,33},{17,49},{33,1},{49,17},{2,34}... | collective-permute-start | bytes 344072 | tf_op jit(solution)/shard_map/ppermute | solution.py:24
  17.8 2.4 %collective-permute-start = (f32[28,8,128]{2,1,0:T(8,128)S(1)}, f32[28,8,128]{2,1,0:T(8,128)}, u32[]{:S(2)}, u32[]{:S(2)}) collective-permute-start(f32[28,8,128]{2,1,0:T(8,128)S(1)} %bitcast.114), channel_id=1, source_target_pairs={{0,16},{16,32},{32,48},{48,0},{1,17},{17,33},{33,49},{49,1},{2,18}... | collective-permute-start | bytes 344072 | tf_op jit(solution)/shard_map/ppermute | solution.py:24
  20.4 5.1 %collective-permute-done = f32[28,8,128]{2,1,0:T(8,128)} collective-permute-done((f32[28,8,128]{2,1,0:T(8,128)S(1)}, f32[28,8,128]{2,1,0:T(8,128)}, u32[]{:S(2)}, u32[]{:S(2)}) %collective-permute-start) | collective-permute-done | bytes 114720 | tf_op jit(solution)/shard_map/ppermute | solution.py:24
  25.5 0.9 bitcast_dynamic-update-slice_fusion.7
  26.4 3.0 %collective-permute-done.1 = f32[28,8,128]{2,1,0:T(8,128)} collective-permute-done((f32[28,8,128]{2,1,0:T(8,128)S(1)}, f32[28,8,128]{2,1,0:T(8,128)}, u32[]{:S(2)}, u32[]{:S(2)}) %collective-permute-start.1) | collective-permute-done | bytes 114720 | tf_op jit(solution)/shard_map/ppermute | solution.py:24
  30.4 2.2 %copy_add_fusion = (f32[8,14,8,128]{3,1,2,0:T(8,128)S(1)}, f32[8,14,8,128]{3,1,2,0:T(8,128)S(1)}) fusion(f32[8,14,8,128]{3,2,1,0:T(8,128)S(1)} %constant_dynamic-slice_fusion.2, f32[16,8,56,128]{3,2,1,0:T(8,128)} %copy-done.1, s32[]{:T(128)S(6)} %select_n.368, s32[]{:T(128)S(6)} %select_n.366, f32[16,8,56,128]{3,2,1,0:T(8,128)} %copy-done, ...), kind=kLoop, calls=%fused_computation.21 | loop fusion | flops 458752 | bytes 3670032 | tf_op jit(solution)/shard_map/add | solution.py:74
  32.6 2.8 %collective-permute-start.13 = (f32[8,14,8,128]{3,1,2,0:T(8,128)S(1)}, f32[8,14,8,128]{3,1,2,0:T(8,128)S(1)}, u32[]{:S(2)}, u32[]{:S(2)}) collective-permute-start(f32[8,14,8,128]{3,1,2,0:T(8,128)S(1)} %get-tuple-element.12), channel_id=1, source_target_pairs={{0,192},{64,128},{128,64},{192,0},{1,193},{65,129},{129,65},{193,1... | collective-permute-start | bytes 1376264 | tf_op jit(solution)/shard_map/ppermute | solution.py:19
  35.5 1.5 collective-permute-start.3
  37.1 9.7 %collective-permute-done.13 = f32[8,14,8,128]{3,1,2,0:T(8,128)S(1)} collective-permute-done((f32[8,14,8,128]{3,1,2,0:T(8,128)S(1)}, f32[8,14,8,128]{3,1,2,0:T(8,128)S(1)}, u32[]{:S(2)}, u32[]{:S(2)}) %collective-permute-start.13) | collective-permute-done | bytes 458784 | tf_op jit(solution)/shard_map/ppermute | solution.py:19
  46.8 1.1 collective-permute-done.8
  47.9 1.5 fusion.3
  49.7 1.5 collective-permute-start.9
  51.2 10.1 %collective-permute-done.14 = f32[4,14,8,128]{3,1,2,0:T(8,128)S(1)} collective-permute-done((f32[4,14,8,128]{3,1,2,0:T(8,128)S(1)}, f32[4,14,8,128]{3,1,2,0:T(8,128)S(1)}, u32[]{:S(2)}, u32[]{:S(2)}) %collective-permute-start.14) | collective-permute-done | bytes 229408 | tf_op jit(solution)/shard_map/ppermute | solution.py:19
  61.3 1.0 collective-permute-done.9
  62.3 1.3 fusion.6
  63.6 2.0 %collective-permute-start.15 = (f32[2,14,8,128]{3,1,2,0:T(8,128)S(1)}, f32[2,14,8,128]{3,1,2,0:T(8,128)S(1)}, u32[]{:S(2)}, u32[]{:S(2)}) collective-permute-start(f32[2,14,8,128]{3,1,2,0:T(8,128)S(1)} %get-tuple-element.8), channel_id=1, source_target_pairs={{0,48},{16,32},{32,16},{48,0},{1,49},{17,33},{33,17},{49,1},{2,50}... | collective-permute-start | bytes 344072 | tf_op jit(solution)/shard_map/ppermute | solution.py:19
  66.3 3.4 %collective-permute-done.15 = f32[2,14,8,128]{3,1,2,0:T(8,128)S(1)} collective-permute-done((f32[2,14,8,128]{3,1,2,0:T(8,128)S(1)}, f32[2,14,8,128]{3,1,2,0:T(8,128)S(1)}, u32[]{:S(2)}, u32[]{:S(2)}) %collective-permute-start.15) | collective-permute-done | bytes 114720 | tf_op jit(solution)/shard_map/ppermute | solution.py:19
  69.7 0.9 fusion.12
  70.6 5.7 %collective-permute-start.16 = (f32[1,14,8,128]{3,1,2,0:T(8,128)S(1)}, f32[1,14,8,128]{3,1,2,0:T(8,128)S(1)}, u32[]{:S(2)}, u32[]{:S(2)}) collective-permute-start(f32[1,14,8,128]{3,1,2,0:T(8,128)S(1)} %fusion.12), channel_id=1, source_target_pairs={{0,16},{16,0},{32,48},{48,32},{1,17},{17,1},{33,49},{49,33},{2,18}... | collective-permute-start | bytes 172040 | tf_op jit(solution)/shard_map/ppermute | solution.py:19
  76.3 1.0 fusion.20
  77.9 0.9 multiply_reduce_fusion
  78.9 3.9 %collective-permute-done.11 = f32[1,14,8,128]{3,1,2,0:T(8,128)S(1)} collective-permute-done((f32[1,14,8,128]{3,1,2,0:T(8,128)S(1)}, f32[1,14,8,128]{3,1,2,0:T(8,128)S(1)}, u32[]{:S(2)}, u32[]{:S(2)}) %collective-permute-start.11) | collective-permute-done | bytes 57376 | tf_op jit(solution)/shard_map/ppermute | solution.py:19
  82.8 1.0 multiply_reduce_fusion.1
  83.8 1.0 collective-permute-start.17
  84.7 1.6 collective-permute-done.17
  86.3 2.4 %collective-permute-start.18 = (f32[8,128]{1,0:T(8,128)S(1)}, f32[8,128]{1,0:T(8,128)S(1)}, u32[]{:S(2)}, u32[]{:S(2)}) collective-permute-start(f32[8,128]{1,0:T(8,128)S(1)} %add.469), channel_id=1, source_target_pairs={{0,2},{1,3},{2,0},{3,1},{4,6},{5,7},{6,4},{7,5},{8,10},{9,11},{10,... | collective-permute-start | bytes 12296 | tf_op jit(solution)/shard_map/ppermute | solution.py:19
  88.7 1.6 collective-permute-done.18
  90.3 1.3 collective-permute-start.5
  91.5 2.1 %collective-permute-start.4 = (f32[4,28,8,128]{3,2,1,0:T(8,128)S(1)}, f32[4,28,8,128]{3,2,1,0:T(8,128)S(1)}, u32[]{:S(2)}, u32[]{:S(2)}) collective-permute-start(f32[4,28,8,128]{3,2,1,0:T(8,128)S(1)} %bitcast_dynamic-update-slice_fusion.5), channel_id=1, source_target_pairs={{0,192},{64,0},{128,64},{192,128},{1,193},{65,1},{129,65},{193,129... | collective-permute-start | bytes 1376264 | tf_op jit(solution)/shard_map/ppermute | solution.py:24
  93.6 7.6 %collective-permute-start.20 = (f32[8,128]{1,0:T(8,128)S(1)}, f32[8,128]{1,0:T(8,128)S(1)}, u32[]{:S(2)}, u32[]{:S(2)}) collective-permute-start(f32[8,128]{1,0:T(8,128)S(1)} %add.471), channel_id=1, source_target_pairs={{0,8},{8,0},{1,9},{9,1},{2,10},{10,2},{3,11},{11,3},{4,12},{12,4},... | collective-permute-start | bytes 12296 | tf_op jit(solution)/shard_map/ppermute | solution.py:19
  102.1 3.5 %collective-permute-done.21 = f32[8,128]{1,0:T(8,128)S(1)} collective-permute-done((f32[8,128]{1,0:T(8,128)S(1)}, f32[8,128]{1,0:T(8,128)S(1)}, u32[]{:S(2)}, u32[]{:S(2)}) %collective-permute-start.21) | collective-permute-done | bytes 4128 | tf_op jit(solution)/shard_map/ppermute | solution.py:19
  105.6 2.2 %collective-permute-start.22 = (f32[8,128]{1,0:T(8,128)S(1)}, f32[8,128]{1,0:T(8,128)S(1)}, u32[]{:S(2)}, u32[]{:S(2)}) collective-permute-start(f32[8,128]{1,0:T(8,128)S(1)} %add.473), channel_id=1, source_target_pairs={{0,16},{16,0},{32,48},{48,32},{1,17},{17,1},{33,49},{49,33},{2,18}... | collective-permute-start | bytes 12296 | tf_op jit(solution)/shard_map/ppermute | solution.py:19
  108.1 2.3 %collective-permute-start.25 = (f32[1,14,8,128]{3,1,2,0:T(8,128)S(1)}, f32[1,14,8,128]{3,1,2,0:T(8,128)S(1)}, u32[]{:S(2)}, u32[]{:S(2)}) collective-permute-start(f32[1,14,8,128]{3,1,2,0:T(8,128)S(1)} %get-tuple-element.7), channel_id=1, source_target_pairs={{0,48},{16,32},{32,16},{48,0},{1,49},{17,33},{33,17},{49,1},{2,50}... | collective-permute-start | bytes 172040 | tf_op jit(solution)/shard_map/ppermute | solution.py:19
  110.5 3.4 %collective-permute-start.23 = (f32[8,128]{1,0:T(8,128)S(1)}, f32[8,128]{1,0:T(8,128)S(1)}, u32[]{:S(2)}, u32[]{:S(2)}) collective-permute-start(f32[8,128]{1,0:T(8,128)S(1)} %add.474), channel_id=1, source_target_pairs={{0,192},{64,128},{128,64},{192,0},{1,193},{65,129},{129,65},{193,1... | collective-permute-start | bytes 12296 | tf_op jit(solution)/shard_map/ppermute | solution.py:19
  113.9 5.3 %collective-permute-start.6 = (f32[4,4,28,8,128]{4,3,2,1,0:T(8,128)S(1)}, f32[4,4,28,8,128]{4,3,2,1,0:T(8,128)}, u32[]{:S(2)}, u32[]{:S(2)}) collective-permute-start(f32[4,4,28,8,128]{4,3,2,1,0:T(8,128)S(1)} %bitcast_dynamic-update-slice_fusion), channel_id=1, source_target_pairs={{0,8},{8,0},{1,9},{9,1},{2,10},{10,2},{3,11},{11,3},{4,12},{12,4},... | collective-permute-start | bytes 5505032 | tf_op jit(solution)/shard_map/ppermute | solution.py:19
  119.3 1.0 collective-permute-start.30
  120.3 1.4 collective-permute-start.24
  121.8 2.1 %collective-permute-start.26 = (f32[2,14,8,128]{3,1,2,0:T(8,128)S(1)}, f32[2,14,8,128]{3,1,2,0:T(8,128)S(1)}, u32[]{:S(2)}, u32[]{:S(2)}) collective-permute-start(f32[2,14,8,128]{3,1,2,0:T(8,128)S(1)} %pad_maximum_fusion.7), channel_id=1, source_target_pairs={{0,16},{16,0},{32,48},{48,32},{1,17},{17,1},{33,49},{49,33},{2,18}... | collective-permute-start | bytes 344072 | tf_op jit(solution)/shard_map/ppermute | solution.py:19
  123.9 2.1 %collective-permute-start.31 = (f32[2,14,8,128]{3,1,2,0:T(8,128)S(1)}, f32[2,14,8,128]{3,1,2,0:T(8,128)S(1)}, u32[]{:S(2)}, u32[]{:S(2)}) collective-permute-start(f32[2,14,8,128]{3,1,2,0:T(8,128)S(1)} %pad_maximum_fusion.8), channel_id=1, source_target_pairs={{0,48},{16,32},{32,16},{48,0},{1,49},{17,33},{33,17},{49,1},{2,50}... | collective-permute-start | bytes 344072 | tf_op jit(solution)/shard_map/ppermute | solution.py:19
  126.0 2.2 %collective-permute-done.26 = f32[2,14,8,128]{3,1,2,0:T(8,128)S(1)} collective-permute-done((f32[2,14,8,128]{3,1,2,0:T(8,128)S(1)}, f32[2,14,8,128]{3,1,2,0:T(8,128)S(1)}, u32[]{:S(2)}, u32[]{:S(2)}) %collective-permute-start.26) | collective-permute-done | bytes 114720 | tf_op jit(solution)/shard_map/ppermute | solution.py:19
  128.3 3.4 %collective-permute-start.27 = (f32[4,14,8,128]{3,1,2,0:T(8,128)S(1)}, f32[4,14,8,128]{3,1,2,0:T(8,128)S(1)}, u32[]{:S(2)}, u32[]{:S(2)}) collective-permute-start(f32[4,14,8,128]{3,1,2,0:T(8,128)S(1)} %pad_maximum_fusion.5), channel_id=1, source_target_pairs={{0,192},{64,128},{128,64},{192,0},{1,193},{65,129},{129,65},{193,1... | collective-permute-start | bytes 688136 | tf_op jit(solution)/shard_map/ppermute | solution.py:19
  132.5 3.0 %collective-permute-done.27 = f32[4,14,8,128]{3,1,2,0:T(8,128)S(1)} collective-permute-done((f32[4,14,8,128]{3,1,2,0:T(8,128)S(1)}, f32[4,14,8,128]{3,1,2,0:T(8,128)S(1)}, u32[]{:S(2)}, u32[]{:S(2)}) %collective-permute-start.27) | collective-permute-done | bytes 229408 | tf_op jit(solution)/shard_map/ppermute | solution.py:19
  135.5 3.5 %collective-permute-start.28 = (f32[8,14,8,128]{3,1,2,0:T(8,128)S(1)}, f32[8,14,8,128]{3,1,2,0:T(8,128)}, u32[]{:S(2)}, u32[]{:S(2)}) collective-permute-start(f32[8,14,8,128]{3,1,2,0:T(8,128)S(1)} %pad_maximum_fusion.3), channel_id=1, source_target_pairs={{0,64},{64,0},{128,192},{192,128},{1,65},{65,1},{129,193},{193,129... | collective-permute-start | bytes 1376264 | tf_op jit(solution)/shard_map/ppermute | solution.py:19
  142.6 7.7 %collective-permute-done.28 = f32[8,14,8,128]{3,1,2,0:T(8,128)} collective-permute-done((f32[8,14,8,128]{3,1,2,0:T(8,128)S(1)}, f32[8,14,8,128]{3,1,2,0:T(8,128)}, u32[]{:S(2)}, u32[]{:S(2)}) %collective-permute-start.28) | collective-permute-done | bytes 458784 | tf_op jit(solution)/shard_map/ppermute | solution.py:19
  150.3 1.1 broadcast_select_fusion.3
  151.5 1.2 copy.44
  152.8 2.3 %collective-permute-start.29 = (f32[16,14,8,128]{3,2,1,0:T(8,128)}, f32[16,14,8,128]{3,2,1,0:T(8,128)}, u32[]{:S(2)}, u32[]{:S(2)}) collective-permute-start(f32[16,14,8,128]{3,2,1,0:T(8,128)} %copy.44), channel_id=1, source_target_pairs={{0,8},{8,0},{1,9},{9,1},{2,10},{10,2},{3,11},{11,3},{4,12},{12,4},... | collective-permute-start | bytes 2752520 | tf_op jit(solution)/shard_map/ppermute | solution.py:19
  155.0 1.1 broadcast_select_fusion.1
  156.3 1.2 copy.47
  157.5 1.4 collective-permute-start.34
  159.0 1.8 select_bitcast_fusion.1
  160.8 2.2 %maximum_multiply_fusion = f32[4,4,2,28,8,128]{5,4,3,2,1,0:T(8,128)} fusion(f32[4,4,1,28,8,128]{5,4,3,2,1,0:T(8,128)S(1)} %get-tuple-element.17, f32[4,4,1,28,8,128]{5,4,3,2,1,0:T(8,128)S(1)} %get-tuple-element.16), kind=kLoop, calls=%fused_computation.7 | loop fusion | flops 1835008 | bytes 7340032 | tf_op jit(solution)/shard_map/mul | solution.py:100
  163.0 5.3 %copy.31 = f32[128,7168]{1,0:T(8,128)} copy(f32[128,7168]{0,1:T(8,128)} %bitcast.106) | data formatting | bytes 7340032 | tf_op jit(solution)/shard_map/mul | solution.py:100
  168.3 1.6 copy_select_fusion.3
  169.9 2.2 %copy_select_fusion.1 = (f32[16,14,8,128]{3,1,2,0:T(8,128)S(1)}, f32[16,14,8,128]{3,1,2,0:T(8,128)S(1)}) fusion(f32[16,14,8,128]{3,2,1,0:T(8,128)} %collective-permute-done.34, pred[]{:T(512)S(6)} %eq.23, f32[8,14,8,128]{3,1,2,0:T(8,128)S(1)} %copy-done.5, f32[8,14,8,128]{3,1,2,0:T(8,128)S(1)} %get-tuple-element.24), kind=kLoop, calls=%fused_computation.12 | loop fusion | flops 688128 | bytes 3670017 | tf_op jit(solution)/shard_map/jit(_where)/select_n | solution.py:111
  172.2 1.8 fusion.2
  174.0 2.5 %copy.133 = f32[16,8,56,128]{3,1,2,0:T(8,128)} copy(f32[16,8,56,128]{3,2,1,0:T(8,128)S(1)} %get-tuple-element.2) | data formatting | bytes 7340032
  176.5 1.7 reshape.30
  178.2 1.7 constant_dynamic-slice_fusion.4
  179.9 2.5 %copy.62 = f32[28,8,128]{2,1,0:T(8,128)S(1)} copy(f32[28,8,128]{1,0,2:T(8,128)} %constant_dynamic-slice_fusion.4) | data formatting | bytes 229376
  (96 shorter events, 10.4 us)
Async XLA Ops:
  5.1 1.8 copy-start
  5.1 3.0 %copy-start.1 = (f32[16,8,56,128]{3,2,1,0:T(8,128)}, f32[16,8,56,128]{3,2,1,0:T(8,128)S(1)}, u32[]{:S(2)}) copy-start(f32[16,8,56,128]{3,2,1,0:T(8,128)S(1)} %get-tuple-element.42) | copy-start | bytes 11010052
  5.1 7.5 %copy-start.10 = (f32[128,1,224]{0,2,1:T(8,128)S(1)}, f32[128,1,224]{0,2,1:T(8,128)}, u32[]{:S(2)}) copy-start(f32[128,1,224]{0,2,1:T(8,128)} %param.5) | copy-start | bytes 344068
  8.2 22.2 %collective-permute-start.7 = (f32[16,14,8,128]{3,2,1,0:T(8,128)S(1)}, f32[16,14,8,128]{3,2,1,0:T(8,128)S(1)}, u32[]{:S(2)}, u32[]{:S(2)}) collective-permute-start(f32[16,14,8,128]{3,2,1,0:T(8,128)S(1)} %copy.32), channel_id=1, source_target_pairs={{0,8},{8,0},{1,9},{9,1},{2,10},{10,2},{3,11},{11,3},{4,12},{12,4},... | collective-permute-start | bytes 2752520 | tf_op jit(solution)/shard_map/ppermute | solution.py:19
  12.6 17.7 %collective-permute-start.12 = (f32[16,14,8,128]{3,2,1,0:T(8,128)}, f32[16,14,8,128]{3,2,1,0:T(8,128)S(1)}, u32[]{:S(2)}, u32[]{:S(2)}) collective-permute-start(f32[16,14,8,128]{3,2,1,0:T(8,128)} %copy.38), channel_id=1, source_target_pairs={{0,8},{8,0},{1,9},{9,1},{2,10},{10,2},{3,11},{11,3},{4,12},{12,4},... | collective-permute-start | bytes 2752520 | tf_op jit(solution)/shard_map/ppermute | solution.py:19
  12.7 22.8 %collective-permute-start.2 = (f32[28,8,128]{2,1,0:T(8,128)S(1)}, f32[28,8,128]{2,1,0:T(8,128)S(1)}, u32[]{:S(2)}, u32[]{:S(2)}) collective-permute-start(f32[28,8,128]{2,1,0:T(8,128)S(1)} %bitcast.112), channel_id=1, source_target_pairs={{0,32},{16,48},{32,0},{48,16},{1,33},{17,49},{33,1},{49,17},{2,34}... | collective-permute-start | bytes 344072 | tf_op jit(solution)/shard_map/ppermute | solution.py:24
  17.8 11.6 %collective-permute-start.1 = (f32[28,8,128]{2,1,0:T(8,128)S(1)}, f32[28,8,128]{2,1,0:T(8,128)}, u32[]{:S(2)}, u32[]{:S(2)}) collective-permute-start(f32[28,8,128]{2,1,0:T(8,128)S(1)} %bitcast.113), channel_id=1, source_target_pairs={{0,48},{16,0},{32,16},{48,32},{1,49},{17,1},{33,17},{49,33},{2,50}... | collective-permute-start | bytes 344072 | tf_op jit(solution)/shard_map/ppermute | solution.py:24
  17.8 7.7 %collective-permute-start = (f32[28,8,128]{2,1,0:T(8,128)S(1)}, f32[28,8,128]{2,1,0:T(8,128)}, u32[]{:S(2)}, u32[]{:S(2)}) collective-permute-start(f32[28,8,128]{2,1,0:T(8,128)S(1)} %bitcast.114), channel_id=1, source_target_pairs={{0,16},{16,32},{32,48},{48,0},{1,17},{17,33},{33,49},{49,1},{2,18}... | collective-permute-start | bytes 344072 | tf_op jit(solution)/shard_map/ppermute | solution.py:24
  32.6 14.2 %collective-permute-start.13 = (f32[8,14,8,128]{3,1,2,0:T(8,128)S(1)}, f32[8,14,8,128]{3,1,2,0:T(8,128)S(1)}, u32[]{:S(2)}, u32[]{:S(2)}) collective-permute-start(f32[8,14,8,128]{3,1,2,0:T(8,128)S(1)} %get-tuple-element.12), channel_id=1, source_target_pairs={{0,192},{64,128},{128,64},{192,0},{1,193},{65,129},{129,65},{193,1... | collective-permute-start | bytes 1376264 | tf_op jit(solution)/shard_map/ppermute | solution.py:19
  35.5 12.4 %collective-permute-start.8 = (f32[8,14,8,128]{3,1,2,0:T(8,128)S(1)}, f32[8,14,8,128]{3,1,2,0:T(8,128)S(1)}, u32[]{:S(2)}, u32[]{:S(2)}) collective-permute-start(f32[8,14,8,128]{3,1,2,0:T(8,128)S(1)} %get-tuple-element.13), channel_id=1, source_target_pairs={{0,64},{64,0},{128,192},{192,128},{1,65},{65,1},{129,193},{193,129... | collective-permute-start | bytes 1376264 | tf_op jit(solution)/shard_map/ppermute | solution.py:19
  35.5 66.5 %collective-permute-start.3 = (f32[4,28,8,128]{3,2,1,0:T(8,128)S(1)}, f32[4,28,8,128]{3,2,1,0:T(8,128)S(1)}, u32[]{:S(2)}, u32[]{:S(2)}) collective-permute-start(f32[4,28,8,128]{3,2,1,0:T(8,128)S(1)} %bitcast_dynamic-update-slice_fusion.5), channel_id=1, source_target_pairs={{0,64},{64,128},{128,192},{192,0},{1,65},{65,129},{129,193},{193,1... | collective-permute-start | bytes 1376264 | tf_op jit(solution)/shard_map/ppermute | solution.py:24
  49.4 11.9 %collective-permute-start.14 = (f32[4,14,8,128]{3,1,2,0:T(8,128)S(1)}, f32[4,14,8,128]{3,1,2,0:T(8,128)S(1)}, u32[]{:S(2)}, u32[]{:S(2)}) collective-permute-start(f32[4,14,8,128]{3,1,2,0:T(8,128)S(1)} %get-tuple-element.10), channel_id=1, source_target_pairs={{0,64},{64,0},{128,192},{192,128},{1,65},{65,1},{129,193},{193,129... | collective-permute-start | bytes 688136 | tf_op jit(solution)/shard_map/ppermute | solution.py:19
  49.7 12.6 %collective-permute-start.9 = (f32[4,14,8,128]{3,1,2,0:T(8,128)S(1)}, f32[4,14,8,128]{3,1,2,0:T(8,128)S(1)}, u32[]{:S(2)}, u32[]{:S(2)}) collective-permute-start(f32[4,14,8,128]{3,1,2,0:T(8,128)S(1)} %get-tuple-element.11), channel_id=1, source_target_pairs={{0,192},{64,128},{128,64},{192,0},{1,193},{65,129},{129,65},{193,1... | collective-permute-start | bytes 688136 | tf_op jit(solution)/shard_map/ppermute | solution.py:19
  63.6 6.1 %collective-permute-start.15 = (f32[2,14,8,128]{3,1,2,0:T(8,128)S(1)}, f32[2,14,8,128]{3,1,2,0:T(8,128)S(1)}, u32[]{:S(2)}, u32[]{:S(2)}) collective-permute-start(f32[2,14,8,128]{3,1,2,0:T(8,128)S(1)} %get-tuple-element.8), channel_id=1, source_target_pairs={{0,48},{16,32},{32,16},{48,0},{1,49},{17,33},{33,17},{49,1},{2,50}... | collective-permute-start | bytes 344072 | tf_op jit(solution)/shard_map/ppermute | solution.py:19
  65.6 10.7 %collective-permute-start.10 = (f32[2,14,8,128]{3,1,2,0:T(8,128)S(1)}, f32[2,14,8,128]{3,1,2,0:T(8,128)S(1)}, u32[]{:S(2)}, u32[]{:S(2)}) collective-permute-start(f32[2,14,8,128]{3,1,2,0:T(8,128)S(1)} %get-tuple-element.9), channel_id=1, source_target_pairs={{0,16},{16,0},{32,48},{48,32},{1,17},{17,1},{33,49},{49,33},{2,18}... | collective-permute-start | bytes 344072 | tf_op jit(solution)/shard_map/ppermute | solution.py:19
  70.6 7.4 %collective-permute-start.16 = (f32[1,14,8,128]{3,1,2,0:T(8,128)S(1)}, f32[1,14,8,128]{3,1,2,0:T(8,128)S(1)}, u32[]{:S(2)}, u32[]{:S(2)}) collective-permute-start(f32[1,14,8,128]{3,1,2,0:T(8,128)S(1)} %fusion.12), channel_id=1, source_target_pairs={{0,16},{16,0},{32,48},{48,32},{1,17},{17,1},{33,49},{49,33},{2,18}... | collective-permute-start | bytes 172040 | tf_op jit(solution)/shard_map/ppermute | solution.py:19
  77.3 5.5 %collective-permute-start.11 = (f32[1,14,8,128]{3,1,2,0:T(8,128)S(1)}, f32[1,14,8,128]{3,1,2,0:T(8,128)S(1)}, u32[]{:S(2)}, u32[]{:S(2)}) collective-permute-start(f32[1,14,8,128]{3,1,2,0:T(8,128)S(1)} %fusion.20), channel_id=1, source_target_pairs={{0,48},{16,32},{32,16},{48,0},{1,49},{17,33},{33,17},{49,1},{2,50}... | collective-permute-start | bytes 172040 | tf_op jit(solution)/shard_map/ppermute | solution.py:19
  83.8 2.5 %collective-permute-start.17 = (f32[8,128]{1,0:T(8,128)S(1)}, f32[8,128]{1,0:T(8,128)S(1)}, u32[]{:S(2)}, u32[]{:S(2)}) collective-permute-start(f32[8,128]{1,0:T(8,128)S(1)} %add.468), channel_id=1, source_target_pairs={{0,1},{1,0},{2,3},{3,2},{4,5},{5,4},{6,7},{7,6},{8,9},{9,8},{10,11... | collective-permute-start | bytes 12296 | tf_op jit(solution)/shard_map/ppermute | solution.py:19
  86.3 4.0 %collective-permute-start.18 = (f32[8,128]{1,0:T(8,128)S(1)}, f32[8,128]{1,0:T(8,128)S(1)}, u32[]{:S(2)}, u32[]{:S(2)}) collective-permute-start(f32[8,128]{1,0:T(8,128)S(1)} %add.469), channel_id=1, source_target_pairs={{0,2},{1,3},{2,0},{3,1},{4,6},{5,7},{6,4},{7,5},{8,10},{9,11},{10,... | collective-permute-start | bytes 12296 | tf_op jit(solution)/shard_map/ppermute | solution.py:19
  90.3 3.3 %collective-permute-start.19 = (f32[8,128]{1,0:T(8,128)S(1)}, f32[8,128]{1,0:T(8,128)S(1)}, u32[]{:S(2)}, u32[]{:S(2)}) collective-permute-start(f32[8,128]{1,0:T(8,128)S(1)} %add.470), channel_id=1, source_target_pairs={{0,4},{4,0},{1,5},{5,1},{2,6},{6,2},{3,7},{7,3},{8,12},{12,8},{9,1... | collective-permute-start | bytes 12296 | tf_op jit(solution)/shard_map/ppermute | solution.py:19
  90.3 23.6 %collective-permute-start.5 = (f32[4,28,8,128]{3,2,1,0:T(8,128)S(1)}, f32[4,28,8,128]{3,2,1,0:T(8,128)S(1)}, u32[]{:S(2)}, u32[]{:S(2)}) collective-permute-start(f32[4,28,8,128]{3,2,1,0:T(8,128)S(1)} %bitcast_dynamic-update-slice_fusion.5), channel_id=1, source_target_pairs={{0,128},{64,192},{128,0},{192,64},{1,129},{65,193},{129,1},{193,65... | collective-permute-start | bytes 1376264 | tf_op jit(solution)/shard_map/ppermute | solution.py:24
  91.5 16.5 %collective-permute-start.4 = (f32[4,28,8,128]{3,2,1,0:T(8,128)S(1)}, f32[4,28,8,128]{3,2,1,0:T(8,128)S(1)}, u32[]{:S(2)}, u32[]{:S(2)}) collective-permute-start(f32[4,28,8,128]{3,2,1,0:T(8,128)S(1)} %bitcast_dynamic-update-slice_fusion.5), channel_id=1, source_target_pairs={{0,192},{64,0},{128,64},{192,128},{1,193},{65,1},{129,65},{193,129... | collective-permute-start | bytes 1376264 | tf_op jit(solution)/shard_map/ppermute | solution.py:24
  93.6 8.4 %collective-permute-start.20 = (f32[8,128]{1,0:T(8,128)S(1)}, f32[8,128]{1,0:T(8,128)S(1)}, u32[]{:S(2)}, u32[]{:S(2)}) collective-permute-start(f32[8,128]{1,0:T(8,128)S(1)} %add.471), channel_id=1, source_target_pairs={{0,8},{8,0},{1,9},{9,1},{2,10},{10,2},{3,11},{11,3},{4,12},{12,4},... | collective-permute-start | bytes 12296 | tf_op jit(solution)/shard_map/ppermute | solution.py:19
  102.0 3.6 %collective-permute-start.21 = (f32[8,128]{1,0:T(8,128)S(1)}, f32[8,128]{1,0:T(8,128)S(1)}, u32[]{:S(2)}, u32[]{:S(2)}) collective-permute-start(f32[8,128]{1,0:T(8,128)S(1)} %add.472), channel_id=1, source_target_pairs={{0,64},{64,0},{128,192},{192,128},{1,65},{65,1},{129,193},{193,129... | collective-permute-start | bytes 12296 | tf_op jit(solution)/shard_map/ppermute | solution.py:19
  105.6 4.9 %collective-permute-start.22 = (f32[8,128]{1,0:T(8,128)S(1)}, f32[8,128]{1,0:T(8,128)S(1)}, u32[]{:S(2)}, u32[]{:S(2)}) collective-permute-start(f32[8,128]{1,0:T(8,128)S(1)} %add.473), channel_id=1, source_target_pairs={{0,16},{16,0},{32,48},{48,32},{1,17},{17,1},{33,49},{49,33},{2,18}... | collective-permute-start | bytes 12296 | tf_op jit(solution)/shard_map/ppermute | solution.py:19
  108.1 13.6 %collective-permute-start.25 = (f32[1,14,8,128]{3,1,2,0:T(8,128)S(1)}, f32[1,14,8,128]{3,1,2,0:T(8,128)S(1)}, u32[]{:S(2)}, u32[]{:S(2)}) collective-permute-start(f32[1,14,8,128]{3,1,2,0:T(8,128)S(1)} %get-tuple-element.7), channel_id=1, source_target_pairs={{0,48},{16,32},{32,16},{48,0},{1,49},{17,33},{33,17},{49,1},{2,50}... | collective-permute-start | bytes 172040 | tf_op jit(solution)/shard_map/ppermute | solution.py:19
  110.5 9.8 %collective-permute-start.23 = (f32[8,128]{1,0:T(8,128)S(1)}, f32[8,128]{1,0:T(8,128)S(1)}, u32[]{:S(2)}, u32[]{:S(2)}) collective-permute-start(f32[8,128]{1,0:T(8,128)S(1)} %add.474), channel_id=1, source_target_pairs={{0,192},{64,128},{128,64},{192,0},{1,193},{65,129},{129,65},{193,1... | collective-permute-start | bytes 12296 | tf_op jit(solution)/shard_map/ppermute | solution.py:19
  113.9 45.1 %collective-permute-start.6 = (f32[4,4,28,8,128]{4,3,2,1,0:T(8,128)S(1)}, f32[4,4,28,8,128]{4,3,2,1,0:T(8,128)}, u32[]{:S(2)}, u32[]{:S(2)}) collective-permute-start(f32[4,4,28,8,128]{4,3,2,1,0:T(8,128)S(1)} %bitcast_dynamic-update-slice_fusion), channel_id=1, source_target_pairs={{0,8},{8,0},{1,9},{9,1},{2,10},{10,2},{3,11},{11,3},{4,12},{12,4},... | collective-permute-start | bytes 5505032 | tf_op jit(solution)/shard_map/ppermute | solution.py:19
  119.3 4.6 %collective-permute-start.30 = (f32[1,14,8,128]{3,1,2,0:T(8,128)S(1)}, f32[1,14,8,128]{3,1,2,0:T(8,128)S(1)}, u32[]{:S(2)}, u32[]{:S(2)}) collective-permute-start(f32[1,14,8,128]{3,1,2,0:T(8,128)S(1)} %get-tuple-element.5), channel_id=1, source_target_pairs={{0,16},{16,0},{32,48},{48,32},{1,17},{17,1},{33,49},{49,33},{2,18}... | collective-permute-start | bytes 172040 | tf_op jit(solution)/shard_map/ppermute | solution.py:19
  120.3 21.0 %collective-permute-start.24 = (f32[8,128]{1,0:T(8,128)S(1)}, f32[8,128]{1,0:T(8,128)S(1)}, u32[]{:S(2)}, u32[]{:S(2)}) collective-permute-start(f32[8,128]{1,0:T(8,128)S(1)} %add.475), channel_id=1, source_target_pairs={{0,48},{16,32},{32,16},{48,0},{1,49},{17,33},{33,17},{49,1},{2,50}... | collective-permute-start | bytes 12296 | tf_op jit(solution)/shard_map/ppermute | solution.py:19
  121.8 6.5 %collective-permute-start.26 = (f32[2,14,8,128]{3,1,2,0:T(8,128)S(1)}, f32[2,14,8,128]{3,1,2,0:T(8,128)S(1)}, u32[]{:S(2)}, u32[]{:S(2)}) collective-permute-start(f32[2,14,8,128]{3,1,2,0:T(8,128)S(1)} %pad_maximum_fusion.7), channel_id=1, source_target_pairs={{0,16},{16,0},{32,48},{48,32},{1,17},{17,1},{33,49},{49,33},{2,18}... | collective-permute-start | bytes 344072 | tf_op jit(solution)/shard_map/ppermute | solution.py:19
  123.9 7.8 %collective-permute-start.31 = (f32[2,14,8,128]{3,1,2,0:T(8,128)S(1)}, f32[2,14,8,128]{3,1,2,0:T(8,128)S(1)}, u32[]{:S(2)}, u32[]{:S(2)}) collective-permute-start(f32[2,14,8,128]{3,1,2,0:T(8,128)S(1)} %pad_maximum_fusion.8), channel_id=1, source_target_pairs={{0,48},{16,32},{32,16},{48,0},{1,49},{17,33},{33,17},{49,1},{2,50}... | collective-permute-start | bytes 344072 | tf_op jit(solution)/shard_map/ppermute | solution.py:19
  128.3 7.1 %collective-permute-start.27 = (f32[4,14,8,128]{3,1,2,0:T(8,128)S(1)}, f32[4,14,8,128]{3,1,2,0:T(8,128)S(1)}, u32[]{:S(2)}, u32[]{:S(2)}) collective-permute-start(f32[4,14,8,128]{3,1,2,0:T(8,128)S(1)} %pad_maximum_fusion.5), channel_id=1, source_target_pairs={{0,192},{64,128},{128,64},{192,0},{1,193},{65,129},{129,65},{193,1... | collective-permute-start | bytes 688136 | tf_op jit(solution)/shard_map/ppermute | solution.py:19
  131.7 7.3 %collective-permute-start.32 = (f32[4,14,8,128]{3,1,2,0:T(8,128)S(1)}, f32[4,14,8,128]{3,1,2,0:T(8,128)S(1)}, u32[]{:S(2)}, u32[]{:S(2)}) collective-permute-start(f32[4,14,8,128]{3,1,2,0:T(8,128)S(1)} %pad_maximum_fusion.6), channel_id=1, source_target_pairs={{0,64},{64,0},{128,192},{192,128},{1,65},{65,1},{129,193},{193,129... | collective-permute-start | bytes 688136 | tf_op jit(solution)/shard_map/ppermute | solution.py:19
  135.5 14.8 %collective-permute-start.28 = (f32[8,14,8,128]{3,1,2,0:T(8,128)S(1)}, f32[8,14,8,128]{3,1,2,0:T(8,128)}, u32[]{:S(2)}, u32[]{:S(2)}) collective-permute-start(f32[8,14,8,128]{3,1,2,0:T(8,128)S(1)} %pad_maximum_fusion.3), channel_id=1, source_target_pairs={{0,64},{64,0},{128,192},{192,128},{1,65},{65,1},{129,193},{193,129... | collective-permute-start | bytes 1376264 | tf_op jit(solution)/shard_map/ppermute | solution.py:19
  139.1 0.7 copy-start.6
  139.1 1.5 copy-start.8
  140.6 14.4 %collective-permute-start.33 = (f32[8,14,8,128]{3,1,2,0:T(8,128)}, f32[8,14,8,128]{3,1,2,0:T(8,128)}, u32[]{:S(2)}, u32[]{:S(2)}) collective-permute-start(f32[8,14,8,128]{3,1,2,0:T(8,128)} %pad_maximum_fusion.4), channel_id=1, source_target_pairs={{0,192},{64,128},{128,64},{192,0},{1,193},{65,129},{129,65},{193,1... | collective-permute-start | bytes 1376264 | tf_op jit(solution)/shard_map/ppermute | solution.py:19
  142.6 12.4 %copy-start.7 = (f32[4,14,8,128]{3,1,2,0:T(8,128)S(1)}, f32[4,14,8,128]{3,1,2,0:T(8,128)}, u32[]{:S(2)}) copy-start(f32[4,14,8,128]{3,1,2,0:T(8,128)} %copy-done.6) | copy-start | bytes 688132
  142.6 12.4 %copy-start.9 = (f32[4,14,8,128]{3,1,2,0:T(8,128)S(1)}, f32[4,14,8,128]{3,1,2,0:T(8,128)}, u32[]{:S(2)}) copy-start(f32[4,14,8,128]{3,1,2,0:T(8,128)} %copy-done.8) | copy-start | bytes 688132
  152.8 15.5 %collective-permute-start.29 = (f32[16,14,8,128]{3,2,1,0:T(8,128)}, f32[16,14,8,128]{3,2,1,0:T(8,128)}, u32[]{:S(2)}, u32[]{:S(2)}) collective-permute-start(f32[16,14,8,128]{3,2,1,0:T(8,128)} %copy.44), channel_id=1, source_target_pairs={{0,8},{8,0},{1,9},{9,1},{2,10},{10,2},{3,11},{11,3},{4,12},{12,4},... | collective-permute-start | bytes 2752520 | tf_op jit(solution)/shard_map/ppermute | solution.py:19
  156.2 2.8 %copy-start.4 = (f32[8,14,8,128]{3,1,2,0:T(8,128)}, f32[8,14,8,128]{3,1,2,0:T(8,128)S(1)}, u32[]{:S(2)}) copy-start(f32[8,14,8,128]{3,1,2,0:T(8,128)S(1)} %get-tuple-element.25) | copy-start | bytes 1376260
  157.5 12.4 %collective-permute-start.34 = (f32[16,14,8,128]{3,2,1,0:T(8,128)}, f32[16,14,8,128]{3,2,1,0:T(8,128)}, u32[]{:S(2)}, u32[]{:S(2)}) collective-permute-start(f32[16,14,8,128]{3,2,1,0:T(8,128)} %copy.47), channel_id=1, source_target_pairs={{0,8},{8,0},{1,9},{9,1},{2,10},{10,2},{3,11},{11,3},{4,12},{12,4},... | collective-permute-start | bytes 2752520 | tf_op jit(solution)/shard_map/ppermute | solution.py:19
  163.0 6.9 %copy-start.5 = (f32[8,14,8,128]{3,1,2,0:T(8,128)S(1)}, f32[8,14,8,128]{3,1,2,0:T(8,128)}, u32[]{:S(2)}) copy-start(f32[8,14,8,128]{3,1,2,0:T(8,128)} %copy-done.4) | copy-start | bytes 1376260
  168.3 3.8 %copy-start.2 = (f32[128,7168]{1,0:T(8,128)S(1)}, f32[128,7168]{1,0:T(8,128)}, u32[]{:S(2)}) copy-start(f32[128,7168]{1,0:T(8,128)} %param.3) | copy-start | bytes 11010052
  168.3 3.9 %copy-start.3 = (f32[128,7168]{1,0:T(8,128)S(1)}, f32[128,7168]{1,0:T(8,128)}, u32[]{:S(2)}) copy-start(f32[128,7168]{1,0:T(8,128)} %copy.31) | copy-start | bytes 11010052

commit v2 on v0

v2 whole, which is shorter than its diff:
```python
import math

import jax
import jax.numpy as jnp
from jax import lax
from jax.experimental import pallas as pl
from jax.experimental.pallas import tpu as pltpu
from jax.sharding import Mesh, PartitionSpec as P

momentum_decay = 0.9
outer_rate = 0.7
clip_rms = 0.25

REPLICA = ("y", "zh", "core")
SUB = 8
LANE = 128


def swap(x, axis, mask):
    n = lax.axis_size(axis)
    return lax.ppermute(x, axis, [(i, i ^ mask) for i in range(n)])


def after(x, *others):
    return lax.optimization_barrier((x,) + others)[0]


def rows_at(x, start, count):
    return lax.dynamic_slice_in_dim(x, start, count, 0)


def half(x, bit):
    middle = x.shape[-1] // 2
    return jnp.where(bit == 0, x[..., :middle], x[..., middle:])


def join(mine, other, bit, dim):
    low, high = jnp.where(bit == 0, mine, other), jnp.where(bit == 0, other, mine)
    return jnp.concatenate([low, high], dim)


def rest_kernel(core_ref, anchor_ref, mine_ref, other_ref, rest_ref):
    groups, shard, lanes = mine_ref.shape
    swapped = core_ref[0] != 0
    parts = []
    for g in range(groups):
        mine, other = mine_ref[g], other_ref[g]
        parts += [jnp.where(swapped, other, mine), jnp.where(swapped, mine, other)]
    moment = jnp.concatenate(parts, 0).T
    rest_ref[...] = anchor_ref[...] - (outer_rate * momentum_decay * momentum_decay) * moment


def rest_of(core, anchor, mine, other):
    rows, cols = anchor.shape
    groups, shard, _ = mine.shape
    per = 2
    width = per * 2 * shard
    part = pl.BlockSpec((per, shard, rows), lambda i, c: (i, 0, 0))
    whole = pl.BlockSpec((rows, width), lambda i, c: (0, i))
    return pl.pallas_call(
        rest_kernel,
        out_shape=jax.ShapeDtypeStruct(anchor.shape, anchor.dtype),
        grid_spec=pltpu.PrefetchScalarGridSpec(
            num_scalar_prefetch=1, grid=(groups // per,), in_specs=[whole, part, part], out_specs=whole
        ),
        cost_estimate=pl.CostEstimate(flops=2 * rows * cols, bytes_accessed=12 * rows * cols, transcendentals=0),
        name="rest",
    )(core.reshape(1), anchor, mine, other)


def on_device(anchor, local_weights, momentum):
    y, zh, core = (lax.axis_index(a) for a in REPLICA)
    replicas = math.prod(lax.axis_size(a) for a in REPLICA)
    elements = anchor.shape[0] * anchor.shape[1] * lax.axis_size("zl") * lax.axis_size("x")
    ceiling = clip_rms * math.sqrt(elements)
    rows, cols = anchor.shape
    blocks = rows // SUB
    a_rows = anchor.reshape(blocks, SUB, cols)
    l_rows = local_weights.reshape(blocks, SUB, cols)

    gray_y, gray_z = (y ^ (y >> 1)) & 1, (zh ^ (zh >> 1)) & 1
    over_y = ((("y", 1, gray_y), ("y", 3, y >> 1)), (("y", 3, y >> 1), ("y", 1, y & 1)))
    over_z = ((("zh", 1, gray_z), ("zh", 3, zh >> 1)), (("zh", 3, zh >> 1), ("zh", 1, zh & 1)))
    each = blocks // 2
    streams = (0, 1)
    count = each // 2
    got = [[], []]
    first = [s * each + core * count for s in streams]

    def total(s, start, n, locals_=l_rows):
        value = rows_at(a_rows, start, n) - rows_at(locals_, start, n)
        for origin, part in got[s]:
            value = value + rows_at(part, start - origin, n)
        return value

    def hold(s, *others):
        origin, part = got[s][-1]
        got[s][-1] = (origin, after(part, *others))

    own_moment = momentum[:, 0, :].T
    shard = own_moment.shape[0]

    sent = [total(0, (1 - core) * count, count)]
    sent.append(total(1, each + (1 - core) * count, count, after(l_rows, sent[0])))
    for s in streams:
        got[s].append((first[s], swap(sent[s], "core", 1)))
    moment_z = after(own_moment, sent[1])
    beside = [swap(moment_z, "zh", 1), swap(moment_z, "zh", 3)]

    for step in (0, 1):
        count //= 2
        sent = []
        for s in streams:
            axis, mask, bit = over_y[s][step]
            if s == 1:
                hold(1, sent[0])
            elif step == 1:
                hold(0, *beside)
            sent.append(total(s, first[s] + (1 - bit) * count, count))
            first[s] = first[s] + bit * count
        for s in streams:
            axis, mask, bit = over_y[s][step]
            got[s].append((first[s], swap(sent[s], axis, mask)))
        if step == 1:
            third = swap(after(moment_z, sent[1]), "zh", 2)
    whole = jnp.zeros((4, shard, LANE), own_moment.dtype)
    for mask, part in ((0, own_moment), (1, beside[0]), (3, beside[1]), (2, third)):
        whole = lax.dynamic_update_index_in_dim(whole, part, zh ^ mask, 0)

    hold(0, whole)
    own = [total(0, first[0], count)]
    hold(1, own[0])
    own.append(total(1, first[1], count))
    for step in (0, 1):
        sent = []
        for s in streams:
            axis, mask, bit = over_z[s][step]
            if s == 1:
                own[1] = after(own[1], sent[0])
            sent.append(half(own[s], 1 - bit))
        if step == 0:
            moment_y = after(whole, sent[1])
            beside = [swap(moment_y, "y", 1), swap(moment_y, "y", 3)]
        for s in streams:
            axis, mask, bit = over_z[s][step]
            own[s] = half(own[s], bit) + swap(sent[s], axis, mask)
    own = [p * (1.0 / replicas) for p in own]
    own[0] = after(own[0], *beside)
    own[1] = after(own[1], own[0])

    squares = sum(jnp.sum(p.reshape(SUB, -1, LANE) ** 2, axis=1) for p in own)

    def add_squares(squares, *steps):
        for axis, mask in steps:
            squares = squares + swap(squares, axis, mask)
        return squares

    squares = add_squares(after(squares, own[1]), ("x", 1))
    third = swap(after(moment_y, own[1]), "y", 2)
    for step in (1, 0):
        if step == 0:
            own[0] = after(own[0], squares)
            own[1] = after(own[1], own[0])
            squares = add_squares(after(squares, own[1]), ("x", 2))
        for s in streams:
            axis, mask, bit = over_z[s][step]
            own[s] = join(own[s], swap(own[s], axis, mask), bit, 2)
    whole = jnp.zeros((4, 4, shard, LANE), own_moment.dtype)
    for mask, part in ((0, moment_y), (1, beside[0]), (3, beside[1]), (2, third)):
        whole = lax.dynamic_update_index_in_dim(whole, part, y ^ mask, 0)
    whole = whole.reshape(16, shard, LANE)

    own[0] = after(own[0], squares, whole)
    own[1] = after(own[1], own[0])
    squares = add_squares(after(squares, own[1]), ("zl", 1), ("core", 1))
    whole = after(whole, own[1])
    other = swap(whole, "core", 1)
    for s in streams:
        axis, mask, bit = over_y[s][1]
        own[s] = join(own[s], swap(own[s], axis, mask), bit, 0)
    own[0] = after(own[0], squares, other)
    own[1] = after(own[1], own[0])
    squares = add_squares(after(squares, own[1]), ("zh", 1), ("zh", 3), ("y", 1))
    rest = rest_of(core, anchor, after(whole, own[1]), other)
    for s in streams:
        axis, mask, bit = over_y[s][0]
        own[s] = join(own[s], swap(own[s], axis, mask), bit, 0)

    own[0] = after(own[0], squares, rest)
    own[1] = after(own[1], own[0])
    squares = add_squares(after(squares, own[1]), ("y", 3))
    others = [swap(own[s], "core", 1) for s in streams]
    norm = jnp.sqrt(jnp.sum(squares))
    scaling = ceiling / jnp.maximum(norm, ceiling)

    factor = (outer_rate * (1.0 + momentum_decay)) * scaling
    at = (y * 8 + zh * 2 + core) * shard
    count = each // 2
    result = rest.reshape(blocks, SUB, cols)
    for pieces, of_core in ((own, core), (others, 1 - core)):
        for s in streams:
            start = s * each + of_core * count
            value = rows_at(result, start, count) - factor * pieces[s]
            result = lax.dynamic_update_slice_in_dim(result, value, start, 0)

    columns = []
    for s in streams:
        mine, other = (lax.dynamic_slice_in_dim(p[s].reshape(count * SUB, cols), at, shard, 1) for p in (own, others))
        columns.append(join(mine, other, core, 0))
    columns = jnp.concatenate(columns, 0)
    new_moment = momentum_decay * momentum[:, 0, :] + scaling * columns
    return result.reshape(rows, cols), new_moment[:, None, :]


def solution(mesh):
    fine = Mesh(mesh.devices.reshape(4, 4, 2, 2, 4), ("y", "zh", "core", "zl", "x"))
    in_specs = (P("zl", "x"), P(REPLICA, "zl", "x"), P("zl", "x", REPLICA))
    out_specs = (P("zl", "x"), P("zl", "x", REPLICA))
    return jax.shard_map(on_device, mesh=fine, in_specs=in_specs, out_specs=out_specs, check_vma=False)
```

time: 410 us -> 143 us (0.35)
  waiting for transfers between devices: 341 us -> 47 us
  starting transfers between devices: 0.08 us -> 59.5 us
  blocking collectives: 16.1 us -> 0 us
  local copies, waits for them, and re-layouts: 17.3 us -> 2.16 us
  between operations: 14.8 us -> 1.87 us
  Pallas kernels: 0 us -> 7.71 us
    psum x1 -> x0, waiting for transfers between devices: 299 us -> none  [on_device(): summed = lax.psum(drift_term, 'replica')]
    ppermute x0 -> x35, starting transfers between devices: none -> 59.5 us  [swap(): return lax.ppermute(x, axis, [(i, i ^ mask) for i in range(n)])]
    ppermute x0 -> x35, waiting for transfers between devices: none -> 47 us  [swap(): return lax.ppermute(x, axis, [(i, i ^ mask) for i in range(n)])]
    all_gather x1 -> x0, waiting for transfers between devices: 41.1 us -> none  [on_device(): gathered = lax.all_gather(momentum, 'replica', axis=2, tiled=True)]
    psum x1 -> x0, blocking collectives: 16.1 us -> none  [on_device(): squares = lax.psum(jnp.sum(pseudo_grad * pseudo_grad), ('fsdp', 'tensor'))]
    unnamed x7 -> x8, local copies, waits for them, and re-layouts: 15.8 us -> 1.77 us
    dynamic_update_slice x0 -> x4, other arithmetic: none -> 9.06 us  [on_device(): result = lax.dynamic_update_slice_in_dim(result, value, start, 0)]
    pallas_call x0 -> x1, Pallas kernels: none -> 7.71 us  [rest_of(): pl.pallas_call(rest_kernel, out_shape=jax.ShapeDtypeStruct(anchor.shape,...]
  transfers between devices with their start and end apart: 2 -> 35, of which waited for: 2 -> 18; matrix products, arithmetic and copies ran while one was open for 1% -> 9% of each run, Pallas kernels for 0% -> 5%
where the time goes in v2:
time: 143 us; the launch traced here: 142 us
  starting transfers between devices  59.5 us (42%)
  waiting for transfers between devices  47 us (33%)
  other arithmetic  23.3 us (16%)
  Pallas kernels  7.71 us (5%)
  local copies, waits for them, and re-layouts  2.16 us (2%)
  between operations  1.87 us (1%)
    ppermute x35, starting transfers between devices, swap(): return lax.ppermute(x, axis, [(i, i ^ mask) for i in range(n)])  59.5 us
    ppermute x35, waiting for transfers between devices, swap(): return lax.ppermute(x, axis, [(i, i ^ mask) for i in range(n)])  47 us
    dynamic_update_slice x4, other arithmetic, on_device(): result = lax.dynamic_update_slice_in_dim(result, value, start, 0)  9.06 us
    pallas_call x1, Pallas kernels, rest_of(): pl.pallas_call(rest_kernel, out_shape=jax.ShapeDtypeStruct(anchor.shape,...  7.71 us
    add x6, other arithmetic, total(): value = value + rows_at(part, start - origin, n)  6.9 us
    sub x2, other arithmetic, total(): value = rows_at(a_rows, start, n) - rows_at(locals_, start, n)  4.05 us
  transfers between devices with their start and end apart: 35, of which 18 were waited for; matrix products, arithmetic and copies ran while one was open for 9% of the time, Pallas kernels for 5%

profile of v2, /device:TPU:1, one launch (start us, length us, event | category | flops | bytes accessed | tf_op | source)
XLA Modules:
  0.0 141.6 jit_solution(293642574429773226)
XLA Ops:
  0.6 1.6 %dynamic-slice_subtract_fusion.1 = f32[4,8,7168]{2,1,0:T(8,128)S(1)} fusion(f32[16,8,7168]{2,1,0:T(8,128)} %bitcast.56, s32[]{:T(128)S(6)} %select_n.256, f32[16,8,7168]{2,1,0:T(8,128)} %bitcast.44), kind=kLoop, calls=%fused_computation.7 | loop fusion | flops 229376 | bytes 2752516 | tf_op jit(solution)/shard_map/sub | solution.py:91
  2.2 3.3 %collective-permute-start.3 = (f32[4,8,7168]{2,1,0:T(8,128)S(1)}, f32[4,8,7168]{2,1,0:T(8,128)S(1)}, u32[]{:S(2)}, u32[]{:S(2)}) collective-permute-start(f32[4,8,7168]{2,1,0:T(8,128)S(1)} %dynamic-slice_subtract_fusion.1), channel_id=1, source_target_pairs={{0,8},{8,0},{1,9},{9,1},{2,10},{10,2},{3,11},{11,3},{4,12},{12,4},... | collective-permute-start | bytes 2752520 | tf_op jit(solution)/shard_map/ppermute | solution.py:21
  5.6 2.5 %dynamic-slice_subtract_fusion = f32[4,8,7168]{2,1,0:T(8,128)} fusion(f32[16,8,7168]{2,1,0:T(8,128)} %bitcast.57, s32[]{:T(128)S(6)} %select_n.255, f32[16,8,7168]{2,1,0:T(8,128)} %bitcast.45), kind=kLoop, calls=%fused_computation.6 | loop fusion | flops 229376 | bytes 2752516 | tf_op jit(solution)/shard_map/sub | solution.py:91
  8.0 4.3 %collective-permute-start.1 = (f32[224,128]{1,0:T(8,128)S(1)}, f32[224,128]{1,0:T(8,128)S(1)}, u32[]{:S(2)}, u32[]{:S(2)}) collective-permute-start(f32[224,128]{1,0:T(8,128)S(1)} %bitcast.65), channel_id=1, source_target_pairs={{0,48},{16,32},{32,16},{48,0},{1,49},{17,33},{33,17},{49,1},{2,50}... | collective-permute-start | bytes 344072 | tf_op jit(solution)/shard_map/ppermute | solution.py:21
  12.3 1.2 collective-permute-start
  13.5 0.6 collective-permute-start.2
  14.2 5.1 %collective-permute-done = f32[224,128]{1,0:T(8,128)S(1)} collective-permute-done((f32[224,128]{1,0:T(8,128)S(1)}, f32[224,128]{1,0:T(8,128)S(1)}, u32[]{:S(2)}, u32[]{:S(2)}) %collective-permute-start) | collective-permute-done | bytes 114720 | tf_op jit(solution)/shard_map/ppermute | solution.py:21
  19.4 1.2 dynamic-slice_add_fusion.1
  20.6 1.4 collective-permute-start.5
  22.0 1.2 dynamic-slice_add_fusion
  23.2 2.0 %collective-permute-start.4 = (f32[2,8,7168]{2,1,0:T(8,128)S(1)}, f32[2,8,7168]{2,1,0:T(8,128)S(1)}, u32[]{:S(2)}, u32[]{:S(2)}) collective-permute-start(f32[2,8,7168]{2,1,0:T(8,128)S(1)} %dynamic-slice_add_fusion), channel_id=1, source_target_pairs={{0,192},{64,128},{128,64},{192,0},{1,193},{65,129},{129,65},{193,1... | collective-permute-start | bytes 1376264 | tf_op jit(solution)/shard_map/ppermute | solution.py:21
  25.2 5.6 %collective-permute-done.5 = f32[2,8,7168]{2,1,0:T(8,128)S(1)} collective-permute-done((f32[2,8,7168]{2,1,0:T(8,128)S(1)}, f32[2,8,7168]{2,1,0:T(8,128)S(1)}, u32[]{:S(2)}, u32[]{:S(2)}) %collective-permute-start.5) | collective-permute-done | bytes 458784 | tf_op jit(solution)/shard_map/ppermute | solution.py:21
  30.8 1.1 dynamic-slice_add_fusion.3
  31.9 2.4 %collective-permute-done.4 = f32[2,8,7168]{2,1,0:T(8,128)S(1)} collective-permute-done((f32[2,8,7168]{2,1,0:T(8,128)S(1)}, f32[2,8,7168]{2,1,0:T(8,128)S(1)}, u32[]{:S(2)}, u32[]{:S(2)}) %collective-permute-start.4) | collective-permute-done | bytes 458784 | tf_op jit(solution)/shard_map/ppermute | solution.py:21
  34.3 1.1 dynamic-slice_add_fusion.2
  35.4 3.2 %collective-permute-start.6 = (f32[224,128]{1,0:T(8,128)S(1)}, f32[224,128]{1,0:T(8,128)S(1)}, u32[]{:S(2)}, u32[]{:S(2)}) collective-permute-start(f32[224,128]{1,0:T(8,128)S(1)} %bitcast.67), channel_id=1, source_target_pairs={{0,32},{16,48},{32,0},{48,16},{1,33},{17,49},{33,1},{49,17},{2,34}... | collective-permute-start | bytes 344072 | tf_op jit(solution)/shard_map/ppermute | solution.py:21
  38.7 2.0 %collective-permute-start.8 = (f32[1,8,7168]{2,1,0:T(8,128)S(1)}, f32[1,8,7168]{2,1,0:T(8,128)S(1)}, u32[]{:S(2)}, u32[]{:S(2)}) collective-permute-start(f32[1,8,7168]{2,1,0:T(8,128)S(1)} %dynamic-slice_add_fusion.3), channel_id=1, source_target_pairs={{0,192},{64,128},{128,64},{192,0},{1,193},{65,129},{129,65},{193,1... | collective-permute-start | bytes 688136 | tf_op jit(solution)/shard_map/ppermute | solution.py:21
  40.7 3.7 %collective-permute-done.6 = f32[224,128]{1,0:T(8,128)S(1)} collective-permute-done((f32[224,128]{1,0:T(8,128)S(1)}, f32[224,128]{1,0:T(8,128)S(1)}, u32[]{:S(2)}, u32[]{:S(2)}) %collective-permute-start.6) | collective-permute-done | bytes 114720 | tf_op jit(solution)/shard_map/ppermute | solution.py:21
  44.4 0.5 collective-permute-done.8
  44.9 1.1 add_add_fusion
  46.1 1.1 add_add_fusion.1
  47.2 3.0 %collective-permute-start.11 = (f32[1,8,3584]{2,1,0:T(8,128)S(1)}, f32[1,8,3584]{2,1,0:T(8,128)S(1)}, u32[]{:S(2)}, u32[]{:S(2)}) collective-permute-start(f32[1,8,3584]{2,1,0:T(8,128)S(1)} %slice_select_fusion.1), channel_id=1, source_target_pairs={{0,48},{16,32},{32,16},{48,0},{1,49},{17,33},{33,17},{49,1},{2,50}... | collective-permute-start | bytes 344072 | tf_op jit(solution)/shard_map/ppermute | solution.py:21
  50.2 1.9 %collective-permute-start.10 = (f32[4,224,128]{2,1,0:T(8,128)S(1)}, f32[4,224,128]{2,1,0:T(8,128)S(1)}, u32[]{:S(2)}, u32[]{:S(2)}) collective-permute-start(f32[4,224,128]{2,1,0:T(8,128)S(1)} %bitcast_dynamic-update-slice_fusion.5), channel_id=1, source_target_pairs={{0,192},{64,128},{128,64},{192,0},{1,193},{65,129},{129,65},{193,1... | collective-permute-start | bytes 1376264 | tf_op jit(solution)/shard_map/ppermute | solution.py:21
  52.4 3.8 %collective-permute-done.12 = f32[1,8,3584]{2,1,0:T(8,128)S(1)} collective-permute-done((f32[1,8,3584]{2,1,0:T(8,128)S(1)}, f32[1,8,3584]{2,1,0:T(8,128)S(1)}, u32[]{:S(2)}, u32[]{:S(2)}) %collective-permute-start.12) | collective-permute-done | bytes 114720 | tf_op jit(solution)/shard_map/ppermute | solution.py:21
  56.2 0.5 collective-permute-start.14
  56.8 1.9 %collective-permute-start.13 = (f32[1,8,1792]{2,1,0:T(8,128)S(1)}, f32[1,8,1792]{2,1,0:T(8,128)S(1)}, u32[]{:S(2)}, u32[]{:S(2)}) collective-permute-start(f32[1,8,1792]{2,1,0:T(8,128)S(1)} %slice_select_fusion.3), channel_id=1, source_target_pairs={{0,16},{16,0},{32,48},{48,32},{1,17},{17,1},{33,49},{49,33},{2,18}... | collective-permute-start | bytes 172040 | tf_op jit(solution)/shard_map/ppermute | solution.py:21
  58.8 2.7 %collective-permute-done.14 = f32[1,8,1792]{2,1,0:T(8,128)S(1)} collective-permute-done((f32[1,8,1792]{2,1,0:T(8,128)S(1)}, f32[1,8,1792]{2,1,0:T(8,128)S(1)}, u32[]{:S(2)}, u32[]{:S(2)}) %collective-permute-start.14) | collective-permute-done | bytes 57376 | tf_op jit(solution)/shard_map/ppermute | solution.py:21
  61.6 1.9 %collective-permute-start.16 = (f32[1,8,1792]{2,1,0:T(8,128)S(1)}, f32[1,8,1792]{2,1,0:T(8,128)S(1)}, u32[]{:S(2)}, u32[]{:S(2)}) collective-permute-start(f32[1,8,1792]{2,1,0:T(8,128)S(1)} %add_multiply_fusion.1), channel_id=1, source_target_pairs={{0,16},{16,0},{32,48},{48,32},{1,17},{17,1},{33,49},{49,33},{2,18}... | collective-permute-start | bytes 172040 | tf_op jit(solution)/shard_map/ppermute | solution.py:21
  63.5 2.0 %collective-permute-start.17 = (f32[1,8,1792]{2,1,0:T(8,128)S(1)}, f32[1,8,1792]{2,1,0:T(8,128)S(1)}, u32[]{:S(2)}, u32[]{:S(2)}) collective-permute-start(f32[1,8,1792]{2,1,0:T(8,128)S(1)} %add_multiply_fusion), channel_id=1, source_target_pairs={{0,48},{16,32},{32,16},{48,0},{1,49},{17,33},{33,17},{49,1},{2,50}... | collective-permute-start | bytes 172040 | tf_op jit(solution)/shard_map/ppermute | solution.py:21
  65.5 1.2 collective-permute-start.18
  66.7 0.7 collective-permute-start.15
  67.4 0.5 collective-permute-done.18
  68.0 1.2 collective-permute-done.17
  69.2 2.0 %collective-permute-start.19 = (f32[1,8,3584]{2,1,0:T(8,128)S(1)}, f32[1,8,3584]{2,1,0:T(8,128)S(1)}, u32[]{:S(2)}, u32[]{:S(2)}) collective-permute-start(f32[1,8,3584]{2,1,0:T(8,128)S(1)} %pad_maximum_fusion.6), channel_id=1, source_target_pairs={{0,48},{16,32},{32,16},{48,0},{1,49},{17,33},{33,17},{49,1},{2,50}... | collective-permute-start | bytes 344072 | tf_op jit(solution)/shard_map/ppermute | solution.py:21
  71.2 2.7 %collective-permute-start.21 = (f32[8,128]{1,0:T(8,128)S(1)}, f32[8,128]{1,0:T(8,128)S(1)}, u32[]{:S(2)}, u32[]{:S(2)}) collective-permute-start(f32[8,128]{1,0:T(8,128)S(1)} %add.282), channel_id=1, source_target_pairs={{0,2},{1,3},{2,0},{3,1},{4,6},{5,7},{6,4},{7,5},{8,10},{9,11},{10,... | collective-permute-start | bytes 12296 | tf_op jit(solution)/shard_map/ppermute | solution.py:21
  74.0 1.1 collective-permute-start.20
  75.1 0.4 collective-permute-done.21
  75.5 0.5 collective-permute-done.19
  76.0 3.7 %collective-permute-done.20 = f32[1,8,3584]{2,1,0:T(8,128)S(1)} collective-permute-done((f32[1,8,3584]{2,1,0:T(8,128)S(1)}, f32[1,8,3584]{2,1,0:T(8,128)S(1)}, u32[]{:S(2)}, u32[]{:S(2)}) %collective-permute-start.20) | collective-permute-done | bytes 114720 | tf_op jit(solution)/shard_map/ppermute | solution.py:21
  79.8 2.0 %collective-permute-start.23 = (f32[1,8,7168]{2,1,0:T(8,128)S(1)}, f32[1,8,7168]{2,1,0:T(8,128)S(1)}, u32[]{:S(2)}, u32[]{:S(2)}) collective-permute-start(f32[1,8,7168]{2,1,0:T(8,128)S(1)} %pad_maximum_fusion.5), channel_id=1, source_target_pairs={{0,192},{64,128},{128,64},{192,0},{1,193},{65,129},{129,65},{193,1... | collective-permute-start | bytes 688136 | tf_op jit(solution)/shard_map/ppermute | solution.py:21
  81.9 2.7 %collective-permute-done.24 = f32[8,128]{1,0:T(8,128)S(1)} collective-permute-done((f32[8,128]{1,0:T(8,128)S(1)}, f32[8,128]{1,0:T(8,128)S(1)}, u32[]{:S(2)}, u32[]{:S(2)}) %collective-permute-start.24) | collective-permute-done | bytes 4128 | tf_op jit(solution)/shard_map/ppermute | solution.py:21
  84.7 11.0 %collective-permute-start.25 = (f32[8,128]{1,0:T(8,128)S(1)}, f32[8,128]{1,0:T(8,128)S(1)}, u32[]{:S(2)}, u32[]{:S(2)}) collective-permute-start(f32[8,128]{1,0:T(8,128)S(1)} %add.284), channel_id=1, source_target_pairs={{0,8},{8,0},{1,9},{9,1},{2,10},{10,2},{3,11},{11,3},{4,12},{12,4},... | collective-permute-start | bytes 12296 | tf_op jit(solution)/shard_map/ppermute | solution.py:21
  95.7 0.7 collective-permute-done.25
  96.5 6.3 %collective-permute-done.22 = f32[1,8,7168]{2,1,0:T(8,128)S(1)} collective-permute-done((f32[1,8,7168]{2,1,0:T(8,128)S(1)}, f32[1,8,7168]{2,1,0:T(8,128)S(1)}, u32[]{:S(2)}, u32[]{:S(2)}) %collective-permute-start.22) | collective-permute-done | bytes 229408 | tf_op jit(solution)/shard_map/ppermute | solution.py:21
  102.9 0.3 collective-permute-start.31
  103.2 0.9 copy-done.1
  104.2 1.0 collective-permute-start.27
  105.2 2.4 %collective-permute-done.27 = f32[8,128]{1,0:T(8,128)S(1)} collective-permute-done((f32[8,128]{1,0:T(8,128)S(1)}, f32[8,128]{1,0:T(8,128)S(1)}, u32[]{:S(2)}, u32[]{:S(2)}) %collective-permute-start.27) | collective-permute-done | bytes 4128 | tf_op jit(solution)/shard_map/ppermute | solution.py:21
  107.6 0.9 collective-permute-start.28
  108.5 3.7 %collective-permute-done.28 = f32[8,128]{1,0:T(8,128)S(1)} collective-permute-done((f32[8,128]{1,0:T(8,128)S(1)}, f32[8,128]{1,0:T(8,128)S(1)}, u32[]{:S(2)}, u32[]{:S(2)}) %collective-permute-start.28) | collective-permute-done | bytes 4128 | tf_op jit(solution)/shard_map/ppermute | solution.py:21
  112.2 0.3 collective-permute-start.29
  112.5 0.8 collective-permute-start.30
  113.3 7.7 %rest.1 = f32[128,7168]{1,0:T(8,128)} custom-call(s32[1]{0:T(128)} %bitcast.core_ref, f32[128,7168]{1,0:T(8,128)} %anchor_ref.1, f32[16,224,128]{2,1,0:T(8,128)} %bitcast.53, f32[16,224,128]{2,1,0:T(8,128)} %copy-done.1), custom_call_target="tpu_custom_call" | custom-call | flops 1835008 | bytes 11010048 | tf_op jit(solution)/shard_map/rest/pallas_call | solution.py:60
  121.2 1.0 collective-permute-done.30
  122.2 1.1 broadcast_select_fusion.3
  123.4 1.0 collective-permute-start.32
  124.5 4.8 %collective-permute-start.34 = (f32[4,8,7168]{2,1,0:T(8,128)S(1)}, f32[4,8,7168]{2,1,0:T(8,128)S(1)}, u32[]{:S(2)}, u32[]{:S(2)}) collective-permute-start(f32[4,8,7168]{2,1,0:T(8,128)S(1)} %pad_maximum_fusion), channel_id=1, source_target_pairs={{0,8},{8,0},{1,9},{9,1},{2,10},{10,2},{3,11},{11,3},{4,12},{12,4},... | collective-permute-start | bytes 2752520 | tf_op jit(solution)/shard_map/ppermute | solution.py:21
  129.4 0.6 add_reduce_fusion
  130.7 2.2 %subtract_dynamic-update-slice_fusion.3 = f32[16,8,7168]{2,1,0:T(8,128)} fusion(f32[16,8,7168]{2,1,0:T(8,128)} %bitcast.42, s32[]{:T(128)S(6)} %select_n.310, f32[4,8,7168]{2,1,0:T(8,128)S(1)} %pad_maximum_fusion.1, f32[]{:T(128)S(6)} %mul_shard_map.3), kind=kLoop, calls=%fused_computation.5 | loop fusion | flops 458752 | bytes 2752520 | tf_op jit(solution)/shard_map/dynamic_update_slice | solution.py:204
  132.9 2.2 %subtract_dynamic-update-slice_fusion.2 = f32[16,8,7168]{2,1,0:T(8,128)} fusion(f32[16,8,7168]{2,1,0:T(8,128)} %subtract_dynamic-update-slice_fusion.3, s32[]{:T(128)S(6)} %select_n.317, f32[4,8,7168]{2,1,0:T(8,128)S(1)} %pad_maximum_fusion, f32[]{:T(128)S(6)} %mul_shard_map.3), kind=kLoop, calls=%fused_computation.4 | loop fusion | flops 458752 | bytes 2752520 | tf_op jit(solution)/shard_map/dynamic_update_slice | solution.py:204
  135.2 0.9 select_bitcast_fusion.3
  136.2 0.7 copy.12
  136.9 2.5 %subtract_dynamic-update-slice_fusion.1 = f32[16,8,7168]{2,1,0:T(8,128)} fusion(f32[16,8,7168]{2,1,0:T(8,128)} %subtract_dynamic-update-slice_fusion.2, s32[]{:T(128)S(6)} %select_n.256, f32[4,8,7168]{2,1,0:T(8,128)} %collective-permute-done.33, f32[]{:T(128)S(6)} %mul_shard_map.3), kind=kLoop, calls=%fused_computation.3 | loop fusion | flops 458752 | bytes 2752520 | tf_op jit(solution)/shard_map/dynamic_update_slice | solution.py:204
  139.4 2.2 %subtract_dynamic-update-slice_fusion = f32[16,8,7168]{2,1,0:T(8,128)} fusion(f32[16,8,7168]{2,1,0:T(8,128)} %subtract_dynamic-update-slice_fusion.1, s32[]{:T(128)S(6)} %select_n.255, f32[4,8,7168]{2,1,0:T(8,128)S(1)} %collective-permute-done.34, f32[]{:T(128)S(6)} %mul_shard_map.3), kind=kLoop, calls=%fused_computation.2 | loop fusion | flops 458752 | bytes 2752520 | tf_op jit(solution)/shard_map/dynamic_update_slice | solution.py:204
  (75 shorter events, 1.7 us)
Async XLA Ops:
  0.6 7.4 %copy-start.2 = (f32[128,1,224]{0,2,1:T(8,128)S(1)}, f32[128,1,224]{0,2,1:T(8,128)}, u32[]{:S(2)}) copy-start(f32[128,1,224]{0,2,1:T(8,128)} %param.5) | copy-start | bytes 344068
  2.2 17.1 %collective-permute-start.3 = (f32[4,8,7168]{2,1,0:T(8,128)S(1)}, f32[4,8,7168]{2,1,0:T(8,128)S(1)}, u32[]{:S(2)}, u32[]{:S(2)}) collective-permute-start(f32[4,8,7168]{2,1,0:T(8,128)S(1)} %dynamic-slice_subtract_fusion.1), channel_id=1, source_target_pairs={{0,8},{8,0},{1,9},{9,1},{2,10},{10,2},{3,11},{11,3},{4,12},{12,4},... | collective-permute-start | bytes 2752520 | tf_op jit(solution)/shard_map/ppermute | solution.py:21
  8.0 17.1 %collective-permute-start.1 = (f32[224,128]{1,0:T(8,128)S(1)}, f32[224,128]{1,0:T(8,128)S(1)}, u32[]{:S(2)}, u32[]{:S(2)}) collective-permute-start(f32[224,128]{1,0:T(8,128)S(1)} %bitcast.65), channel_id=1, source_target_pairs={{0,48},{16,32},{32,16},{48,0},{1,49},{17,33},{33,17},{49,1},{2,50}... | collective-permute-start | bytes 344072 | tf_op jit(solution)/shard_map/ppermute | solution.py:21
  12.3 7.0 %collective-permute-start = (f32[224,128]{1,0:T(8,128)S(1)}, f32[224,128]{1,0:T(8,128)S(1)}, u32[]{:S(2)}, u32[]{:S(2)}) collective-permute-start(f32[224,128]{1,0:T(8,128)S(1)} %bitcast.66), channel_id=1, source_target_pairs={{0,16},{16,0},{32,48},{48,32},{1,17},{17,1},{33,49},{49,33},{2,18}... | collective-permute-start | bytes 344072 | tf_op jit(solution)/shard_map/ppermute | solution.py:21
  13.5 8.5 %collective-permute-start.2 = (f32[4,8,7168]{2,1,0:T(8,128)}, f32[4,8,7168]{2,1,0:T(8,128)S(1)}, u32[]{:S(2)}, u32[]{:S(2)}) collective-permute-start(f32[4,8,7168]{2,1,0:T(8,128)} %dynamic-slice_subtract_fusion), channel_id=1, source_target_pairs={{0,8},{8,0},{1,9},{9,1},{2,10},{10,2},{3,11},{11,3},{4,12},{12,4},... | collective-permute-start | bytes 2752520 | tf_op jit(solution)/shard_map/ppermute | solution.py:21
  20.6 10.2 %collective-permute-start.5 = (f32[2,8,7168]{2,1,0:T(8,128)S(1)}, f32[2,8,7168]{2,1,0:T(8,128)S(1)}, u32[]{:S(2)}, u32[]{:S(2)}) collective-permute-start(f32[2,8,7168]{2,1,0:T(8,128)S(1)} %dynamic-slice_add_fusion.1), channel_id=1, source_target_pairs={{0,64},{64,0},{128,192},{192,128},{1,65},{65,1},{129,193},{193,129... | collective-permute-start | bytes 1376264 | tf_op jit(solution)/shard_map/ppermute | solution.py:21
  23.2 11.1 %collective-permute-start.4 = (f32[2,8,7168]{2,1,0:T(8,128)S(1)}, f32[2,8,7168]{2,1,0:T(8,128)S(1)}, u32[]{:S(2)}, u32[]{:S(2)}) collective-permute-start(f32[2,8,7168]{2,1,0:T(8,128)S(1)} %dynamic-slice_add_fusion), channel_id=1, source_target_pairs={{0,192},{64,128},{128,64},{192,0},{1,193},{65,129},{129,65},{193,1... | collective-permute-start | bytes 1376264 | tf_op jit(solution)/shard_map/ppermute | solution.py:21
  35.4 9.0 %collective-permute-start.6 = (f32[224,128]{1,0:T(8,128)S(1)}, f32[224,128]{1,0:T(8,128)S(1)}, u32[]{:S(2)}, u32[]{:S(2)}) collective-permute-start(f32[224,128]{1,0:T(8,128)S(1)} %bitcast.67), channel_id=1, source_target_pairs={{0,32},{16,48},{32,0},{48,16},{1,33},{17,49},{33,1},{49,17},{2,34}... | collective-permute-start | bytes 344072 | tf_op jit(solution)/shard_map/ppermute | solution.py:21
  38.6 7.4 %collective-permute-start.7 = (f32[1,8,7168]{2,1,0:T(8,128)S(1)}, f32[1,8,7168]{2,1,0:T(8,128)S(1)}, u32[]{:S(2)}, u32[]{:S(2)}) collective-permute-start(f32[1,8,7168]{2,1,0:T(8,128)S(1)} %dynamic-slice_add_fusion.2), channel_id=1, source_target_pairs={{0,64},{64,0},{128,192},{192,128},{1,65},{65,1},{129,193},{193,129... | collective-permute-start | bytes 688136 | tf_op jit(solution)/shard_map/ppermute | solution.py:21
  38.7 6.2 %collective-permute-start.8 = (f32[1,8,7168]{2,1,0:T(8,128)S(1)}, f32[1,8,7168]{2,1,0:T(8,128)S(1)}, u32[]{:S(2)}, u32[]{:S(2)}) collective-permute-start(f32[1,8,7168]{2,1,0:T(8,128)S(1)} %dynamic-slice_add_fusion.3), channel_id=1, source_target_pairs={{0,192},{64,128},{128,64},{192,0},{1,193},{65,129},{129,65},{193,1... | collective-permute-start | bytes 688136 | tf_op jit(solution)/shard_map/ppermute | solution.py:21
  47.2 9.6 %collective-permute-start.11 = (f32[1,8,3584]{2,1,0:T(8,128)S(1)}, f32[1,8,3584]{2,1,0:T(8,128)S(1)}, u32[]{:S(2)}, u32[]{:S(2)}) collective-permute-start(f32[1,8,3584]{2,1,0:T(8,128)S(1)} %slice_select_fusion.1), channel_id=1, source_target_pairs={{0,48},{16,32},{32,16},{48,0},{1,49},{17,33},{33,17},{49,1},{2,50}... | collective-permute-start | bytes 344072 | tf_op jit(solution)/shard_map/ppermute | solution.py:21
  50.2 6.0 %collective-permute-start.12 = (f32[1,8,3584]{2,1,0:T(8,128)S(1)}, f32[1,8,3584]{2,1,0:T(8,128)S(1)}, u32[]{:S(2)}, u32[]{:S(2)}) collective-permute-start(f32[1,8,3584]{2,1,0:T(8,128)S(1)} %slice_select_fusion), channel_id=1, source_target_pairs={{0,16},{16,0},{32,48},{48,32},{1,17},{17,1},{33,49},{49,33},{2,18}... | collective-permute-start | bytes 344072 | tf_op jit(solution)/shard_map/ppermute | solution.py:21
  50.2 11.3 %collective-permute-start.10 = (f32[4,224,128]{2,1,0:T(8,128)S(1)}, f32[4,224,128]{2,1,0:T(8,128)S(1)}, u32[]{:S(2)}, u32[]{:S(2)}) collective-permute-start(f32[4,224,128]{2,1,0:T(8,128)S(1)} %bitcast_dynamic-update-slice_fusion.5), channel_id=1, source_target_pairs={{0,192},{64,128},{128,64},{192,0},{1,193},{65,129},{129,65},{193,1... | collective-permute-start | bytes 1376264 | tf_op jit(solution)/shard_map/ppermute | solution.py:21
  52.1 9.4 %collective-permute-start.9 = (f32[4,224,128]{2,1,0:T(8,128)S(1)}, f32[4,224,128]{2,1,0:T(8,128)S(1)}, u32[]{:S(2)}, u32[]{:S(2)}) collective-permute-start(f32[4,224,128]{2,1,0:T(8,128)S(1)} %bitcast_dynamic-update-slice_fusion.5), channel_id=1, source_target_pairs={{0,64},{64,0},{128,192},{192,128},{1,65},{65,1},{129,193},{193,129... | collective-permute-start | bytes 1376264 | tf_op jit(solution)/shard_map/ppermute | solution.py:21
  56.2 5.2 %collective-permute-start.14 = (f32[1,8,1792]{2,1,0:T(8,128)S(1)}, f32[1,8,1792]{2,1,0:T(8,128)S(1)}, u32[]{:S(2)}, u32[]{:S(2)}) collective-permute-start(f32[1,8,1792]{2,1,0:T(8,128)S(1)} %slice_select_fusion.2), channel_id=1, source_target_pairs={{0,48},{16,32},{32,16},{48,0},{1,49},{17,33},{33,17},{49,1},{2,50}... | collective-permute-start | bytes 172040 | tf_op jit(solution)/shard_map/ppermute | solution.py:21
  56.8 4.7 %collective-permute-start.13 = (f32[1,8,1792]{2,1,0:T(8,128)S(1)}, f32[1,8,1792]{2,1,0:T(8,128)S(1)}, u32[]{:S(2)}, u32[]{:S(2)}) collective-permute-start(f32[1,8,1792]{2,1,0:T(8,128)S(1)} %slice_select_fusion.3), channel_id=1, source_target_pairs={{0,16},{16,0},{32,48},{48,32},{1,17},{17,1},{33,49},{49,33},{2,18}... | collective-permute-start | bytes 172040 | tf_op jit(solution)/shard_map/ppermute | solution.py:21
  61.6 7.6 %collective-permute-start.16 = (f32[1,8,1792]{2,1,0:T(8,128)S(1)}, f32[1,8,1792]{2,1,0:T(8,128)S(1)}, u32[]{:S(2)}, u32[]{:S(2)}) collective-permute-start(f32[1,8,1792]{2,1,0:T(8,128)S(1)} %add_multiply_fusion.1), channel_id=1, source_target_pairs={{0,16},{16,0},{32,48},{48,32},{1,17},{17,1},{33,49},{49,33},{2,18}... | collective-permute-start | bytes 172040 | tf_op jit(solution)/shard_map/ppermute | solution.py:21
  63.5 5.7 %collective-permute-start.17 = (f32[1,8,1792]{2,1,0:T(8,128)S(1)}, f32[1,8,1792]{2,1,0:T(8,128)S(1)}, u32[]{:S(2)}, u32[]{:S(2)}) collective-permute-start(f32[1,8,1792]{2,1,0:T(8,128)S(1)} %add_multiply_fusion), channel_id=1, source_target_pairs={{0,48},{16,32},{32,16},{48,0},{1,49},{17,33},{33,17},{49,1},{2,50}... | collective-permute-start | bytes 172040 | tf_op jit(solution)/shard_map/ppermute | solution.py:21
  65.5 2.5 %collective-permute-start.18 = (f32[8,128]{1,0:T(8,128)S(1)}, f32[8,128]{1,0:T(8,128)S(1)}, u32[]{:S(2)}, u32[]{:S(2)}) collective-permute-start(f32[8,128]{1,0:T(8,128)S(1)} %add.281), channel_id=1, source_target_pairs={{0,1},{1,0},{2,3},{3,2},{4,5},{5,4},{6,7},{7,6},{8,9},{9,8},{10,11... | collective-permute-start | bytes 12296 | tf_op jit(solution)/shard_map/ppermute | solution.py:21
  66.7 13.0 %collective-permute-start.15 = (f32[4,224,128]{2,1,0:T(8,128)S(1)}, f32[4,224,128]{2,1,0:T(8,128)S(1)}, u32[]{:S(2)}, u32[]{:S(2)}) collective-permute-start(f32[4,224,128]{2,1,0:T(8,128)S(1)} %bitcast_dynamic-update-slice_fusion.5), channel_id=1, source_target_pairs={{0,128},{64,192},{128,0},{192,64},{1,129},{65,193},{129,1},{193,65... | collective-permute-start | bytes 1376264 | tf_op jit(solution)/shard_map/ppermute | solution.py:21
  69.2 6.8 %collective-permute-start.19 = (f32[1,8,3584]{2,1,0:T(8,128)S(1)}, f32[1,8,3584]{2,1,0:T(8,128)S(1)}, u32[]{:S(2)}, u32[]{:S(2)}) collective-permute-start(f32[1,8,3584]{2,1,0:T(8,128)S(1)} %pad_maximum_fusion.6), channel_id=1, source_target_pairs={{0,48},{16,32},{32,16},{48,0},{1,49},{17,33},{33,17},{49,1},{2,50}... | collective-permute-start | bytes 344072 | tf_op jit(solution)/shard_map/ppermute | solution.py:21
  71.2 4.3 %collective-permute-start.21 = (f32[8,128]{1,0:T(8,128)S(1)}, f32[8,128]{1,0:T(8,128)S(1)}, u32[]{:S(2)}, u32[]{:S(2)}) collective-permute-start(f32[8,128]{1,0:T(8,128)S(1)} %add.282), channel_id=1, source_target_pairs={{0,2},{1,3},{2,0},{3,1},{4,6},{5,7},{6,4},{7,5},{8,10},{9,11},{10,... | collective-permute-start | bytes 12296 | tf_op jit(solution)/shard_map/ppermute | solution.py:21
  74.0 5.7 %collective-permute-start.20 = (f32[1,8,3584]{2,1,0:T(8,128)S(1)}, f32[1,8,3584]{2,1,0:T(8,128)S(1)}, u32[]{:S(2)}, u32[]{:S(2)}) collective-permute-start(f32[1,8,3584]{2,1,0:T(8,128)S(1)} %pad_maximum_fusion.7), channel_id=1, source_target_pairs={{0,16},{16,0},{32,48},{48,32},{1,17},{17,1},{33,49},{49,33},{2,18}... | collective-permute-start | bytes 344072 | tf_op jit(solution)/shard_map/ppermute | solution.py:21
  79.8 33.5 %copy-start = (f32[4,4,224,128]{3,2,1,0:T(8,128)}, f32[4,4,224,128]{3,2,1,0:T(8,128)S(1)}, u32[]{:S(2)}) copy-start(f32[4,4,224,128]{3,2,1,0:T(8,128)S(1)} %bitcast_dynamic-update-slice_fusion) | copy-start | bytes 5505028
  79.8 16.7 %collective-permute-start.23 = (f32[1,8,7168]{2,1,0:T(8,128)S(1)}, f32[1,8,7168]{2,1,0:T(8,128)S(1)}, u32[]{:S(2)}, u32[]{:S(2)}) collective-permute-start(f32[1,8,7168]{2,1,0:T(8,128)S(1)} %pad_maximum_fusion.5), channel_id=1, source_target_pairs={{0,192},{64,128},{128,64},{192,0},{1,193},{65,129},{129,65},{193,1... | collective-permute-start | bytes 688136 | tf_op jit(solution)/shard_map/ppermute | solution.py:21
  81.8 2.8 %collective-permute-start.24 = (f32[8,128]{1,0:T(8,128)S(1)}, f32[8,128]{1,0:T(8,128)S(1)}, u32[]{:S(2)}, u32[]{:S(2)}) collective-permute-start(f32[8,128]{1,0:T(8,128)S(1)} %add.283), channel_id=1, source_target_pairs={{0,4},{4,0},{1,5},{5,1},{2,6},{6,2},{3,7},{7,3},{8,12},{12,8},{9,1... | collective-permute-start | bytes 12296 | tf_op jit(solution)/shard_map/ppermute | solution.py:21
  84.7 11.8 %collective-permute-start.25 = (f32[8,128]{1,0:T(8,128)S(1)}, f32[8,128]{1,0:T(8,128)S(1)}, u32[]{:S(2)}, u32[]{:S(2)}) collective-permute-start(f32[8,128]{1,0:T(8,128)S(1)} %add.284), channel_id=1, source_target_pairs={{0,8},{8,0},{1,9},{9,1},{2,10},{10,2},{3,11},{11,3},{4,12},{12,4},... | collective-permute-start | bytes 12296 | tf_op jit(solution)/shard_map/ppermute | solution.py:21
  95.6 7.2 %collective-permute-start.22 = (f32[1,8,7168]{2,1,0:T(8,128)S(1)}, f32[1,8,7168]{2,1,0:T(8,128)S(1)}, u32[]{:S(2)}, u32[]{:S(2)}) collective-permute-start(f32[1,8,7168]{2,1,0:T(8,128)S(1)} %pad_maximum_fusion.4), channel_id=1, source_target_pairs={{0,64},{64,0},{128,192},{192,128},{1,65},{65,1},{129,193},{193,129... | collective-permute-start | bytes 688136 | tf_op jit(solution)/shard_map/ppermute | solution.py:21
  95.6 7.3 %collective-permute-start.26 = (f32[16,224,128]{2,1,0:T(8,128)S(1)}, f32[16,224,128]{2,1,0:T(8,128)S(1)}, u32[]{:S(2)}, u32[]{:S(2)}) collective-permute-start(f32[16,224,128]{2,1,0:T(8,128)S(1)} %bitcast.52), channel_id=1, source_target_pairs={{0,8},{8,0},{1,9},{9,1},{2,10},{10,2},{3,11},{11,3},{4,12},{12,4},... | collective-permute-start | bytes 5505032 | tf_op jit(solution)/shard_map/ppermute | solution.py:21
  102.9 1.2 copy-start.1
  102.9 18.1 %collective-permute-start.31 = (f32[2,8,7168]{2,1,0:T(8,128)S(1)}, f32[2,8,7168]{2,1,0:T(8,128)S(1)}, u32[]{:S(2)}, u32[]{:S(2)}) collective-permute-start(f32[2,8,7168]{2,1,0:T(8,128)S(1)} %pad_maximum_fusion.3), channel_id=1, source_target_pairs={{0,64},{64,0},{128,192},{192,128},{1,65},{65,1},{129,193},{193,129... | collective-permute-start | bytes 1376264 | tf_op jit(solution)/shard_map/ppermute | solution.py:21
  104.2 3.4 %collective-permute-start.27 = (f32[8,128]{1,0:T(8,128)S(1)}, f32[8,128]{1,0:T(8,128)S(1)}, u32[]{:S(2)}, u32[]{:S(2)}) collective-permute-start(f32[8,128]{1,0:T(8,128)S(1)} %add.285), channel_id=1, source_target_pairs={{0,16},{16,0},{32,48},{48,32},{1,17},{17,1},{33,49},{49,33},{2,18}... | collective-permute-start | bytes 12296 | tf_op jit(solution)/shard_map/ppermute | solution.py:21
  107.6 4.6 %collective-permute-start.28 = (f32[8,128]{1,0:T(8,128)S(1)}, f32[8,128]{1,0:T(8,128)S(1)}, u32[]{:S(2)}, u32[]{:S(2)}) collective-permute-start(f32[8,128]{1,0:T(8,128)S(1)} %add.287), channel_id=1, source_target_pairs={{0,48},{16,32},{32,16},{48,0},{1,49},{17,33},{33,17},{49,1},{2,50}... | collective-permute-start | bytes 12296 | tf_op jit(solution)/shard_map/ppermute | solution.py:21
  112.2 8.8 %collective-permute-start.29 = (f32[8,128]{1,0:T(8,128)S(1)}, f32[8,128]{1,0:T(8,128)S(1)}, u32[]{:S(2)}, u32[]{:S(2)}) collective-permute-start(f32[8,128]{1,0:T(8,128)S(1)} %add.288), channel_id=1, source_target_pairs={{0,64},{64,0},{128,192},{192,128},{1,65},{65,1},{129,193},{193,129... | collective-permute-start | bytes 12296 | tf_op jit(solution)/shard_map/ppermute | solution.py:21
  112.5 9.7 %collective-permute-start.30 = (f32[2,8,7168]{2,1,0:T(8,128)S(1)}, f32[2,8,7168]{2,1,0:T(8,128)}, u32[]{:S(2)}, u32[]{:S(2)}) collective-permute-start(f32[2,8,7168]{2,1,0:T(8,128)S(1)} %pad_maximum_fusion.2), channel_id=1, source_target_pairs={{0,192},{64,128},{128,64},{192,0},{1,193},{65,129},{129,65},{193,1... | collective-permute-start | bytes 1376264 | tf_op jit(solution)/shard_map/ppermute | solution.py:21
  123.4 6.0 %collective-permute-start.32 = (f32[8,128]{1,0:T(8,128)S(1)}, f32[8,128]{1,0:T(8,128)S(1)}, u32[]{:S(2)}, u32[]{:S(2)}) collective-permute-start(f32[8,128]{1,0:T(8,128)S(1)} %add.289), channel_id=1, source_target_pairs={{0,192},{64,128},{128,64},{192,0},{1,193},{65,129},{129,65},{193,1... | collective-permute-start | bytes 12296 | tf_op jit(solution)/shard_map/ppermute | solution.py:21
  124.5 10.7 %collective-permute-start.34 = (f32[4,8,7168]{2,1,0:T(8,128)S(1)}, f32[4,8,7168]{2,1,0:T(8,128)S(1)}, u32[]{:S(2)}, u32[]{:S(2)}) collective-permute-start(f32[4,8,7168]{2,1,0:T(8,128)S(1)} %pad_maximum_fusion), channel_id=1, source_target_pairs={{0,8},{8,0},{1,9},{9,1},{2,10},{10,2},{3,11},{11,3},{4,12},{12,4},... | collective-permute-start | bytes 2752520 | tf_op jit(solution)/shard_map/ppermute | solution.py:21
  129.3 5.9 %collective-permute-start.33 = (f32[4,8,7168]{2,1,0:T(8,128)S(1)}, f32[4,8,7168]{2,1,0:T(8,128)}, u32[]{:S(2)}, u32[]{:S(2)}) collective-permute-start(f32[4,8,7168]{2,1,0:T(8,128)S(1)} %pad_maximum_fusion.1), channel_id=1, source_target_pairs={{0,8},{8,0},{1,9},{9,1},{2,10},{10,2},{3,11},{11,3},{4,12},{12,4},... | collective-permute-start | bytes 2752520 | tf_op jit(solution)/shard_map/ppermute | solution.py:21

commit v3 on v2

--- a/solution.py
+++ b/solution.py
@@ -19,6 +19,15 @@
 def swap(x, axis, mask):
     n = lax.axis_size(axis)
     return lax.ppermute(x, axis, [(i, i ^ mask) for i in range(n)])
+
+
+def swap_all(x, masks):
+    axes = tuple(masks)
+    sizes = [lax.axis_size(a) for a in axes]
+    mask = 0
+    for a, n in zip(axes, sizes):
+        mask = mask * n + masks[a]
+    return lax.ppermute(x, axes, [(i, i ^ mask) for i in range(math.prod(sizes))])
 
 
 def after(x, *others):
@@ -104,8 +113,6 @@
     sent.append(total(1, each + (1 - core) * count, count, after(l_rows, sent[0])))
     for s in streams:
         got[s].append((first[s], swap(sent[s], "core", 1)))
-    moment_z = after(own_moment, sent[1])
-    beside = [swap(moment_z, "zh", 1), swap(moment_z, "zh", 3)]
 
     for step in (0, 1):
         count //= 2
@@ -121,8 +128,11 @@
         for s in streams:
             axis, mask, bit = over_y[s][step]
             got[s].append((first[s], swap(sent[s], axis, mask)))
-        if step == 1:
-            third = swap(after(moment_z, sent[1]), "zh", 2)
+        moment_z = after(own_moment, sent[1])
+        if step == 0:
+            beside = [swap(moment_z, "zh", 1), swap(moment_z, "zh", 3)]
+        else:
+            third = swap(moment_z, "zh", 2)
     whole = jnp.zeros((4, shard, LANE), own_moment.dtype)
     for mask, part in ((0, own_moment), (1, beside[0]), (3, beside[1]), (2, third)):
         whole = lax.dynamic_update_index_in_dim(whole, part, zh ^ mask, 0)
@@ -151,17 +161,15 @@
     squares = sum(jnp.sum(p.reshape(SUB, -1, LANE) ** 2, axis=1) for p in own)
 
     def add_squares(squares, *steps):
-        for axis, mask in steps:
-            squares = squares + swap(squares, axis, mask)
-        return squares
-
-    squares = add_squares(after(squares, own[1]), ("x", 1))
+        return squares + sum(swap_all(squares, masks) for masks in steps)
+
+    squares = add_squares(after(squares, own[1]), {"x": 1}, {"x": 2}, {"x": 3})
     third = swap(after(moment_y, own[1]), "y", 2)
     for step in (1, 0):
         if step == 0:
             own[0] = after(own[0], squares)
             own[1] = after(own[1], own[0])
-            squares = add_squares(after(squares, own[1]), ("x", 2))
+            squares = add_squares(after(squares, own[1]), {"core": 1}, {"zl": 1}, {"core": 1, "zl": 1})
         for s in streams:
             axis, mask, bit = over_z[s][step]
             own[s] = join(own[s], swap(own[s], axis, mask), bit, 2)
@@ -172,7 +180,7 @@
 
     own[0] = after(own[0], squares, whole)
     own[1] = after(own[1], own[0])
-    squares = add_squares(after(squares, own[1]), ("zl", 1), ("core", 1))
+    squares = add_squares(after(squares, own[1]), {"y": 1}, {"y": 2}, {"y": 3})
     whole = after(whole, own[1])
     other = swap(whole, "core", 1)
     for s in streams:
@@ -180,7 +188,7 @@
         own[s] = join(own[s], swap(own[s], axis, mask), bit, 0)
     own[0] = after(own[0], squares, other)
     own[1] = after(own[1], own[0])
-    squares = add_squares(after(squares, own[1]), ("zh", 1), ("zh", 3), ("y", 1))
+    squares = add_squares(after(squares, own[1]), {"zh": 1}, {"zh": 2}, {"zh": 3})
     rest = rest_of(core, anchor, after(whole, own[1]), other)
     for s in streams:
         axis, mask, bit = over_y[s][0]
@@ -188,7 +196,6 @@
 
     own[0] = after(own[0], squares, rest)
     own[1] = after(own[1], own[0])
-    squares = add_squares(after(squares, own[1]), ("y", 3))
     others = [swap(own[s], "core", 1) for s in streams]
     norm = jnp.sqrt(jnp.sum(squares))
     scaling = ceiling / jnp.maximum(norm, ceiling)

time: 143 us -> 133 us (0.930)
  waiting for transfers between devices: 47 us -> 29.8 us
  starting transfers between devices: 59.5 us -> 67 us
    ppermute x0 -> x12, starting transfers between devices: none -> 20.9 us  [swap_all(): lax.ppermute(x, axes, [(i, i ^ mask) for i in range(math.prod(sizes))])]
    ppermute x35 -> x27, waiting for transfers between devices: 47 us -> 29 us  [swap(): return lax.ppermute(x, axis, [(i, i ^ mask) for i in range(n)])]
    ppermute x35 -> x27, starting transfers between devices: 59.5 us -> 46.1 us  [swap(): return lax.ppermute(x, axis, [(i, i ^ mask) for i in range(n)])]
  transfers between devices with their start and end apart: 35 -> 39, of which waited for: 18 -> 14; matrix products, arithmetic and copies ran while one was open for 9% -> 12% of each run, Pallas kernels for 5% -> 6%
where the time goes in v3:
time: 133 us; the launch traced here: 132 us
  starting transfers between devices  67 us (50%)
  waiting for transfers between devices  29.8 us (22%)
  other arithmetic  24.1 us (18%)
  Pallas kernels  7.71 us (6%)
  between operations  1.85 us (1%)
  local copies, waits for them, and re-layouts  1.45 us (1%)
    ppermute x27, starting transfers between devices, swap(): return lax.ppermute(x, axis, [(i, i ^ mask) for i in range(n)])  46.1 us
    ppermute x27, waiting for transfers between devices, swap(): return lax.ppermute(x, axis, [(i, i ^ mask) for i in range(n)])  29 us
    ppermute x12, starting transfers between devices, swap_all(): lax.ppermute(x, axes, [(i, i ^ mask) for i in range(math.prod(sizes))])  20.9 us
    dynamic_update_slice x4, other arithmetic, on_device(): result = lax.dynamic_update_slice_in_dim(result, value, start, 0)  8.77 us
    pallas_call x1, Pallas kernels, rest_of(): pl.pallas_call(rest_kernel, out_shape=jax.ShapeDtypeStruct(anchor.shape,...  7.71 us
    add x6, other arithmetic, total(): value = value + rows_at(part, start - origin, n)  7.71 us
    sub x2, other arithmetic, total(): value = rows_at(a_rows, start, n) - rows_at(locals_, start, n)  4.02 us
  transfers between devices with their start and end apart: 39, of which 14 were waited for; matrix products, arithmetic and copies ran while one was open for 12% of the time, Pallas kernels for 6%

profile of v3, /device:TPU:1, one launch (start us, length us, event | category | flops | bytes accessed | tf_op | source)
XLA Modules:
  0.0 131.9 jit_solution(14477289543827131157)
XLA Ops:
  0.6 1.6 %dynamic-slice_subtract_fusion.1 = f32[4,8,7168]{2,1,0:T(8,128)S(1)} fusion(f32[16,8,7168]{2,1,0:T(8,128)} %bitcast.54, s32[]{:T(128)S(6)} %select_n.257, f32[16,8,7168]{2,1,0:T(8,128)} %bitcast.42), kind=kLoop, calls=%fused_computation.7 | loop fusion | flops 229376 | bytes 2752516 | tf_op jit(solution)/shard_map/sub | solution.py:100
  2.2 3.3 %collective-permute-start.1 = (f32[4,8,7168]{2,1,0:T(8,128)S(1)}, f32[4,8,7168]{2,1,0:T(8,128)S(1)}, u32[]{:S(2)}, u32[]{:S(2)}) collective-permute-start(f32[4,8,7168]{2,1,0:T(8,128)S(1)} %dynamic-slice_subtract_fusion.1), channel_id=1, source_target_pairs={{0,8},{8,0},{1,9},{9,1},{2,10},{10,2},{3,11},{11,3},{4,12},{12,4},... | collective-permute-start | bytes 2752520 | tf_op jit(solution)/shard_map/ppermute | solution.py:21
  5.5 2.5 %dynamic-slice_subtract_fusion = f32[4,8,7168]{2,1,0:T(8,128)} fusion(f32[16,8,7168]{2,1,0:T(8,128)} %bitcast.55, s32[]{:T(128)S(6)} %select_n.256, f32[16,8,7168]{2,1,0:T(8,128)} %bitcast.43), kind=kLoop, calls=%fused_computation.6 | loop fusion | flops 229376 | bytes 2752516 | tf_op jit(solution)/shard_map/sub | solution.py:100
  8.0 1.2 dynamic-slice_add_fusion.1
  9.3 1.3 %collective-permute-done = f32[4,8,7168]{2,1,0:T(8,128)S(1)} collective-permute-done((f32[4,8,7168]{2,1,0:T(8,128)}, f32[4,8,7168]{2,1,0:T(8,128)S(1)}, u32[]{:S(2)}, u32[]{:S(2)}) %collective-permute-start) | collective-permute-done | bytes 917536 | tf_op jit(solution)/shard_map/ppermute | solution.py:21
  10.7 2.0 %dynamic-slice_add_fusion = f32[2,8,7168]{2,1,0:T(8,128)} fusion(f32[4,8,7168]{2,1,0:T(8,128)S(1)} %collective-permute-done, s32[]{:T(128)S(6)} %select_n.260, f32[16,8,7168]{2,1,0:T(8,128)} %bitcast.57, s32[]{:T(128)S(6)} %select_n.255, f32[16,8,7168]{2,1,0:T(8,128)} %bitcast.45), kind=kLoop, calls=%fused_computation.14 | loop fusion | flops 229376 | bytes 1835016 | tf_op jit(solution)/shard_map/add | solution.py:102
  12.7 1.3 collective-permute-start.2
  14.1 4.3 %collective-permute-start.3 = (f32[224,128]{1,0:T(8,128)S(1)}, f32[224,128]{1,0:T(8,128)S(1)}, u32[]{:S(2)}, u32[]{:S(2)}) collective-permute-start(f32[224,128]{1,0:T(8,128)S(1)} %bitcast.65), channel_id=1, source_target_pairs={{0,48},{16,32},{32,16},{48,0},{1,49},{17,33},{33,17},{49,1},{2,50}... | collective-permute-start | bytes 344072 | tf_op jit(solution)/shard_map/ppermute | solution.py:21
  18.4 2.7 %collective-permute-start.4 = (f32[2,8,7168]{2,1,0:T(8,128)}, f32[2,8,7168]{2,1,0:T(8,128)S(1)}, u32[]{:S(2)}, u32[]{:S(2)}) collective-permute-start(f32[2,8,7168]{2,1,0:T(8,128)} %dynamic-slice_add_fusion), channel_id=1, source_target_pairs={{0,192},{64,128},{128,64},{192,0},{1,193},{65,129},{129,65},{193,1... | collective-permute-start | bytes 1376264 | tf_op jit(solution)/shard_map/ppermute | solution.py:21
  21.1 0.8 collective-permute-done.3
  22.0 1.1 dynamic-slice_add_fusion.3
  23.1 7.6 %collective-permute-done.4 = f32[2,8,7168]{2,1,0:T(8,128)S(1)} collective-permute-done((f32[2,8,7168]{2,1,0:T(8,128)}, f32[2,8,7168]{2,1,0:T(8,128)S(1)}, u32[]{:S(2)}, u32[]{:S(2)}) %collective-permute-start.4) | collective-permute-done | bytes 458784 | tf_op jit(solution)/shard_map/ppermute | solution.py:21
  30.6 1.1 dynamic-slice_add_fusion.2
  31.8 1.4 %collective-permute-start.6 = (f32[224,128]{1,0:T(8,128)S(1)}, f32[224,128]{1,0:T(8,128)S(1)}, u32[]{:S(2)}, u32[]{:S(2)}) collective-permute-start(f32[224,128]{1,0:T(8,128)S(1)} %bitcast.66), channel_id=1, source_target_pairs={{0,32},{16,48},{32,0},{48,16},{1,33},{17,49},{33,1},{49,17},{2,34}... | collective-permute-start | bytes 344072 | tf_op jit(solution)/shard_map/ppermute | solution.py:21
  33.2 0.7 collective-permute-start.7
  33.9 2.7 %collective-permute-start.8 = (f32[1,8,7168]{2,1,0:T(8,128)S(1)}, f32[1,8,7168]{2,1,0:T(8,128)S(1)}, u32[]{:S(2)}, u32[]{:S(2)}) collective-permute-start(f32[1,8,7168]{2,1,0:T(8,128)S(1)} %dynamic-slice_add_fusion.3), channel_id=1, source_target_pairs={{0,192},{64,128},{128,64},{192,0},{1,193},{65,129},{129,65},{193,1... | collective-permute-start | bytes 688136 | tf_op jit(solution)/shard_map/ppermute | solution.py:21
  36.6 3.9 %collective-permute-done.6 = f32[224,128]{1,0:T(8,128)S(1)} collective-permute-done((f32[224,128]{1,0:T(8,128)S(1)}, f32[224,128]{1,0:T(8,128)S(1)}, u32[]{:S(2)}, u32[]{:S(2)}) %collective-permute-start.6) | collective-permute-done | bytes 114720 | tf_op jit(solution)/shard_map/ppermute | solution.py:21
  40.5 1.1 add_add_fusion
  41.7 1.1 add_add_fusion.1
  42.8 2.8 %collective-permute-start.11 = (f32[1,8,3584]{2,1,0:T(8,128)S(1)}, f32[1,8,3584]{2,1,0:T(8,128)S(1)}, u32[]{:S(2)}, u32[]{:S(2)}) collective-permute-start(f32[1,8,3584]{2,1,0:T(8,128)S(1)} %slice_select_fusion.1), channel_id=1, source_target_pairs={{0,48},{16,32},{32,16},{48,0},{1,49},{17,33},{33,17},{49,1},{2,50}... | collective-permute-start | bytes 344072 | tf_op jit(solution)/shard_map/ppermute | solution.py:21
  45.7 1.4 %collective-permute-start.12 = (f32[1,8,3584]{2,1,0:T(8,128)S(1)}, f32[1,8,3584]{2,1,0:T(8,128)S(1)}, u32[]{:S(2)}, u32[]{:S(2)}) collective-permute-start(f32[1,8,3584]{2,1,0:T(8,128)S(1)} %slice_select_fusion), channel_id=1, source_target_pairs={{0,16},{16,0},{32,48},{48,32},{1,17},{17,1},{33,49},{49,33},{2,18}... | collective-permute-start | bytes 344072 | tf_op jit(solution)/shard_map/ppermute | solution.py:21
  47.1 2.7 %collective-permute-start.10 = (f32[4,224,128]{2,1,0:T(8,128)S(1)}, f32[4,224,128]{2,1,0:T(8,128)S(1)}, u32[]{:S(2)}, u32[]{:S(2)}) collective-permute-start(f32[4,224,128]{2,1,0:T(8,128)S(1)} %bitcast_dynamic-update-slice_fusion.5), channel_id=1, source_target_pairs={{0,192},{64,128},{128,64},{192,0},{1,193},{65,129},{129,65},{193,1... | collective-permute-start | bytes 1376264 | tf_op jit(solution)/shard_map/ppermute | solution.py:21
  50.0 0.6 collective-permute-done.12
  50.7 1.4 %collective-permute-start.14 = (f32[1,8,1792]{2,1,0:T(8,128)S(1)}, f32[1,8,1792]{2,1,0:T(8,128)S(1)}, u32[]{:S(2)}, u32[]{:S(2)}) collective-permute-start(f32[1,8,1792]{2,1,0:T(8,128)S(1)} %slice_select_fusion.2), channel_id=1, source_target_pairs={{0,48},{16,32},{32,16},{48,0},{1,49},{17,33},{33,17},{49,1},{2,50}... | collective-permute-start | bytes 172040 | tf_op jit(solution)/shard_map/ppermute | solution.py:21
  52.1 1.6 %collective-permute-start.13 = (f32[1,8,1792]{2,1,0:T(8,128)S(1)}, f32[1,8,1792]{2,1,0:T(8,128)S(1)}, u32[]{:S(2)}, u32[]{:S(2)}) collective-permute-start(f32[1,8,1792]{2,1,0:T(8,128)S(1)} %slice_select_fusion.3), channel_id=1, source_target_pairs={{0,16},{16,0},{32,48},{48,32},{1,17},{17,1},{33,49},{49,33},{2,18}... | collective-permute-start | bytes 172040 | tf_op jit(solution)/shard_map/ppermute | solution.py:21
  53.7 2.2 %collective-permute-done.14 = f32[1,8,1792]{2,1,0:T(8,128)S(1)} collective-permute-done((f32[1,8,1792]{2,1,0:T(8,128)S(1)}, f32[1,8,1792]{2,1,0:T(8,128)S(1)}, u32[]{:S(2)}, u32[]{:S(2)}) %collective-permute-start.14) | collective-permute-done | bytes 57376 | tf_op jit(solution)/shard_map/ppermute | solution.py:21
  55.9 1.1 collective-permute-done.13
  57.0 1.2 collective-permute-done.9
  58.2 2.6 %collective-permute-start.20 = (f32[8,128]{1,0:T(8,128)S(1)}, f32[8,128]{1,0:T(8,128)S(1)}, u32[]{:S(2)}, u32[]{:S(2)}) collective-permute-start(f32[8,128]{1,0:T(8,128)S(1)} %add.293), channel_id=1, source_target_pairs={{0,3},{1,2},{2,1},{3,0},{4,7},{5,6},{6,5},{7,4},{8,11},{9,10},{10,... | collective-permute-start | bytes 12296 | tf_op jit(solution)/shard_map/ppermute | solution.py:30
  60.8 0.5 collective-permute-start.19
  61.6 1.2 collective-permute-start.16
  62.8 2.2 %collective-permute-start.17 = (f32[1,8,1792]{2,1,0:T(8,128)S(1)}, f32[1,8,1792]{2,1,0:T(8,128)S(1)}, u32[]{:S(2)}, u32[]{:S(2)}) collective-permute-start(f32[1,8,1792]{2,1,0:T(8,128)S(1)} %add_multiply_fusion), channel_id=1, source_target_pairs={{0,48},{16,32},{32,16},{48,0},{1,49},{17,33},{33,17},{49,1},{2,50}... | collective-permute-start | bytes 172040 | tf_op jit(solution)/shard_map/ppermute | solution.py:21
  65.0 2.1 %collective-permute-start.15 = (f32[4,224,128]{2,1,0:T(8,128)S(1)}, f32[4,224,128]{2,1,0:T(8,128)S(1)}, u32[]{:S(2)}, u32[]{:S(2)}) collective-permute-start(f32[4,224,128]{2,1,0:T(8,128)S(1)} %bitcast_dynamic-update-slice_fusion.5), channel_id=1, source_target_pairs={{0,128},{64,192},{128,0},{192,64},{1,129},{65,193},{129,1},{193,65... | collective-permute-start | bytes 1376264 | tf_op jit(solution)/shard_map/ppermute | solution.py:21
  67.1 0.9 collective-permute-done.17
  68.1 7.5 %collective-permute-start.25 = (f32[8,128]{1,0:T(8,128)S(1)}, f32[8,128]{1,0:T(8,128)S(1)}, u32[]{:S(2)}, u32[]{:S(2)}) collective-permute-start(f32[8,128]{1,0:T(8,128)S(1)} %add_add_fusion.5), channel_id=1, source_target_pairs={{0,12},{4,8},{8,4},{12,0},{1,13},{5,9},{9,5},{13,1},{2,14},{6,10},... | collective-permute-start | bytes 12296 | tf_op jit(solution)/shard_map/ppermute | solution.py:30
  75.6 1.0 collective-permute-start.24
  76.6 2.0 %collective-permute-start.21 = (f32[1,8,3584]{2,1,0:T(8,128)S(1)}, f32[1,8,3584]{2,1,0:T(8,128)S(1)}, u32[]{:S(2)}, u32[]{:S(2)}) collective-permute-start(f32[1,8,3584]{2,1,0:T(8,128)S(1)} %pad_maximum_fusion.6), channel_id=1, source_target_pairs={{0,48},{16,32},{32,16},{48,0},{1,49},{17,33},{33,17},{49,1},{2,50}... | collective-permute-start | bytes 344072 | tf_op jit(solution)/shard_map/ppermute | solution.py:21
  78.7 1.1 collective-permute-start.22
  79.8 4.5 %collective-permute-done.21 = f32[1,8,3584]{2,1,0:T(8,128)S(1)} collective-permute-done((f32[1,8,3584]{2,1,0:T(8,128)S(1)}, f32[1,8,3584]{2,1,0:T(8,128)S(1)}, u32[]{:S(2)}, u32[]{:S(2)}) %collective-permute-start.21) | collective-permute-done | bytes 114720 | tf_op jit(solution)/shard_map/ppermute | solution.py:21
  84.3 1.7 %collective-permute-done.22 = f32[1,8,3584]{2,1,0:T(8,128)S(1)} collective-permute-done((f32[1,8,3584]{2,1,0:T(8,128)S(1)}, f32[1,8,3584]{2,1,0:T(8,128)S(1)}, u32[]{:S(2)}, u32[]{:S(2)}) %collective-permute-start.22) | collective-permute-done | bytes 114720 | tf_op jit(solution)/shard_map/ppermute | solution.py:21
  86.1 2.2 %collective-permute-start.27 = (f32[1,8,7168]{2,1,0:T(8,128)S(1)}, f32[1,8,7168]{2,1,0:T(8,128)S(1)}, u32[]{:S(2)}, u32[]{:S(2)}) collective-permute-start(f32[1,8,7168]{2,1,0:T(8,128)S(1)} %pad_maximum_fusion.5), channel_id=1, source_target_pairs={{0,192},{64,128},{128,64},{192,0},{1,193},{65,129},{129,65},{193,1... | collective-permute-start | bytes 688136 | tf_op jit(solution)/shard_map/ppermute | solution.py:21
  88.4 0.6 collective-permute-start.30
  89.0 1.8 %collective-permute-start.29 = (f32[8,128]{1,0:T(8,128)S(1)}, f32[8,128]{1,0:T(8,128)S(1)}, u32[]{:S(2)}, u32[]{:S(2)}) collective-permute-start(f32[8,128]{1,0:T(8,128)S(1)} %add_add_fusion.4), channel_id=1, source_target_pairs={{0,128},{64,192},{128,0},{192,64},{1,129},{65,193},{129,1},{193,65... | collective-permute-start | bytes 12296 | tf_op jit(solution)/shard_map/ppermute | solution.py:30
  90.8 1.0 collective-permute-start.28
  91.7 0.5 collective-permute-start.26
  92.2 0.7 collective-permute-done.30
  93.0 3.0 %collective-permute-start.31 = (f32[16,224,128]{2,1,0:T(8,128)S(1)}, f32[16,224,128]{2,1,0:T(8,128)S(1)}, u32[]{:S(2)}, u32[]{:S(2)}) collective-permute-start(f32[16,224,128]{2,1,0:T(8,128)S(1)} %bitcast.50), channel_id=1, source_target_pairs={{0,8},{8,0},{1,9},{9,1},{2,10},{10,2},{3,11},{11,3},{4,12},{12,4},... | collective-permute-start | bytes 5505032 | tf_op jit(solution)/shard_map/ppermute | solution.py:21
  96.1 0.6 collective-permute-done.26
  96.7 2.6 %collective-permute-done.31.other_ref = f32[16,224,128]{2,1,0:T(8,128)S(1)} collective-permute-done((f32[16,224,128]{2,1,0:T(8,128)S(1)}, f32[16,224,128]{2,1,0:T(8,128)S(1)}, u32[]{:S(2)}, u32[]{:S(2)}) %collective-permute-start.31) | collective-permute-done | bytes 1835040 | tf_op jit(solution)/shard_map/ppermute | solution.py:21
  99.4 1.0 collective-permute-start.35
  100.7 2.2 %collective-permute-start.34 = (f32[8,128]{1,0:T(8,128)S(1)}, f32[8,128]{1,0:T(8,128)S(1)}, u32[]{:S(2)}, u32[]{:S(2)}) collective-permute-start(f32[8,128]{1,0:T(8,128)S(1)} %add_add_fusion.3), channel_id=1, source_target_pairs={{0,48},{16,32},{32,16},{48,0},{1,49},{17,33},{33,17},{49,1},{2,50}... | collective-permute-start | bytes 12296 | tf_op jit(solution)/shard_map/ppermute | solution.py:30
  102.8 2.7 %collective-permute-start.33 = (f32[8,128]{1,0:T(8,128)S(1)}, f32[8,128]{1,0:T(8,128)S(1)}, u32[]{:S(2)}, u32[]{:S(2)}) collective-permute-start(f32[8,128]{1,0:T(8,128)S(1)} %add_add_fusion.3), channel_id=1, source_target_pairs={{0,32},{16,48},{32,0},{48,16},{1,33},{17,49},{33,1},{49,17},{2,34}... | collective-permute-start | bytes 12296 | tf_op jit(solution)/shard_map/ppermute | solution.py:30
  105.5 0.9 collective-permute-start.32
  106.5 2.2 %collective-permute-start.36 = (f32[2,8,7168]{2,1,0:T(8,128)S(1)}, f32[2,8,7168]{2,1,0:T(8,128)}, u32[]{:S(2)}, u32[]{:S(2)}) collective-permute-start(f32[2,8,7168]{2,1,0:T(8,128)S(1)} %pad_maximum_fusion.2), channel_id=1, source_target_pairs={{0,192},{64,128},{128,64},{192,0},{1,193},{65,129},{129,65},{193,1... | collective-permute-start | bytes 1376264 | tf_op jit(solution)/shard_map/ppermute | solution.py:21
  108.7 7.7 %rest.1 = f32[128,7168]{1,0:T(8,128)} custom-call(s32[1]{0:T(128)} %bitcast.core_ref, f32[128,7168]{1,0:T(8,128)} %anchor_ref.1, f32[16,224,128]{2,1,0:T(8,128)} %bitcast.51, f32[16,224,128]{2,1,0:T(8,128)} %copy-done.1), custom_call_target="tpu_custom_call" | custom-call | flops 1835008 | bytes 11010048 | tf_op jit(solution)/shard_map/rest/pallas_call | solution.py:69
  116.5 0.6 fusion.1
  117.8 1.1 broadcast_select_fusion.3
  119.0 1.6 %collective-permute-start.37 = (f32[4,8,7168]{2,1,0:T(8,128)S(1)}, f32[4,8,7168]{2,1,0:T(8,128)S(1)}, u32[]{:S(2)}, u32[]{:S(2)}) collective-permute-start(f32[4,8,7168]{2,1,0:T(8,128)S(1)} %pad_maximum_fusion), channel_id=1, source_target_pairs={{0,8},{8,0},{1,9},{9,1},{2,10},{10,2},{3,11},{11,3},{4,12},{12,4},... | collective-permute-start | bytes 2752520 | tf_op jit(solution)/shard_map/ppermute | solution.py:21
  120.6 1.1 broadcast_select_fusion.1
  122.1 2.2 %subtract_dynamic-update-slice_fusion.3 = f32[16,8,7168]{2,1,0:T(8,128)} fusion(f32[16,8,7168]{2,1,0:T(8,128)} %bitcast.17, s32[]{:T(128)S(6)} %select_n.310, f32[4,8,7168]{2,1,0:T(8,128)S(1)} %pad_maximum_fusion, f32[]{:T(128)S(6)} %mul_shard_map.3), kind=kLoop, calls=%fused_computation.5 | loop fusion | flops 458752 | bytes 2752520 | tf_op jit(solution)/shard_map/dynamic_update_slice | solution.py:211
  124.3 2.2 %subtract_dynamic-update-slice_fusion.2 = f32[16,8,7168]{2,1,0:T(8,128)} fusion(f32[16,8,7168]{2,1,0:T(8,128)} %subtract_dynamic-update-slice_fusion.3, s32[]{:T(128)S(6)} %select_n.314, f32[4,8,7168]{2,1,0:T(8,128)S(1)} %pad_maximum_fusion.1, f32[]{:T(128)S(6)} %mul_shard_map.3), kind=kLoop, calls=%fused_computation.4 | loop fusion | flops 458752 | bytes 2752520 | tf_op jit(solution)/shard_map/dynamic_update_slice | solution.py:211
  126.7 0.7 copy.12
  127.5 2.2 %subtract_dynamic-update-slice_fusion.1 = f32[16,8,7168]{2,1,0:T(8,128)} fusion(f32[16,8,7168]{2,1,0:T(8,128)} %subtract_dynamic-update-slice_fusion.2, s32[]{:T(128)S(6)} %select_n.257, f32[4,8,7168]{2,1,0:T(8,128)S(1)} %collective-permute-done.37, f32[]{:T(128)S(6)} %mul_shard_map.3), kind=kLoop, calls=%fused_computation.3 | loop fusion | flops 458752 | bytes 2752520 | tf_op jit(solution)/shard_map/dynamic_update_slice | solution.py:211
  129.7 2.2 %subtract_dynamic-update-slice_fusion = f32[16,8,7168]{2,1,0:T(8,128)} fusion(f32[16,8,7168]{2,1,0:T(8,128)} %subtract_dynamic-update-slice_fusion.1, s32[]{:T(128)S(6)} %select_n.256, f32[4,8,7168]{2,1,0:T(8,128)S(1)} %collective-permute-done.38, f32[]{:T(128)S(6)} %mul_shard_map.3), kind=kLoop, calls=%fused_computation.2 | loop fusion | flops 458752 | bytes 2752520 | tf_op jit(solution)/shard_map/dynamic_update_slice | solution.py:211
  (79 shorter events, 2.4 us)
Async XLA Ops:
  2.2 10.5 %copy-start.2 = (f32[128,1,224]{0,2,1:T(8,128)S(1)}, f32[128,1,224]{0,2,1:T(8,128)}, u32[]{:S(2)}) copy-start(f32[128,1,224]{0,2,1:T(8,128)} %param.5) | copy-start | bytes 344068
  2.2 5.8 %collective-permute-start.1 = (f32[4,8,7168]{2,1,0:T(8,128)S(1)}, f32[4,8,7168]{2,1,0:T(8,128)S(1)}, u32[]{:S(2)}, u32[]{:S(2)}) collective-permute-start(f32[4,8,7168]{2,1,0:T(8,128)S(1)} %dynamic-slice_subtract_fusion.1), channel_id=1, source_target_pairs={{0,8},{8,0},{1,9},{9,1},{2,10},{10,2},{3,11},{11,3},{4,12},{12,4},... | collective-permute-start | bytes 2752520 | tf_op jit(solution)/shard_map/ppermute | solution.py:21
  8.0 2.7 %collective-permute-start = (f32[4,8,7168]{2,1,0:T(8,128)}, f32[4,8,7168]{2,1,0:T(8,128)S(1)}, u32[]{:S(2)}, u32[]{:S(2)}) collective-permute-start(f32[4,8,7168]{2,1,0:T(8,128)} %dynamic-slice_subtract_fusion), channel_id=1, source_target_pairs={{0,8},{8,0},{1,9},{9,1},{2,10},{10,2},{3,11},{11,3},{4,12},{12,4},... | collective-permute-start | bytes 2752520 | tf_op jit(solution)/shard_map/ppermute | solution.py:21
  9.2 12.7 %collective-permute-start.5 = (f32[2,8,7168]{2,1,0:T(8,128)S(1)}, f32[2,8,7168]{2,1,0:T(8,128)S(1)}, u32[]{:S(2)}, u32[]{:S(2)}) collective-permute-start(f32[2,8,7168]{2,1,0:T(8,128)S(1)} %dynamic-slice_add_fusion.1), channel_id=1, source_target_pairs={{0,64},{64,0},{128,192},{192,128},{1,65},{65,1},{129,193},{193,129... | collective-permute-start | bytes 1376264 | tf_op jit(solution)/shard_map/ppermute | solution.py:21
  12.7 8.4 %collective-permute-start.2 = (f32[224,128]{1,0:T(8,128)S(1)}, f32[224,128]{1,0:T(8,128)S(1)}, u32[]{:S(2)}, u32[]{:S(2)}) collective-permute-start(f32[224,128]{1,0:T(8,128)S(1)} %bitcast.64), channel_id=1, source_target_pairs={{0,16},{16,0},{32,48},{48,32},{1,17},{17,1},{33,49},{49,33},{2,18}... | collective-permute-start | bytes 344072 | tf_op jit(solution)/shard_map/ppermute | solution.py:21
  14.1 7.9 %collective-permute-start.3 = (f32[224,128]{1,0:T(8,128)S(1)}, f32[224,128]{1,0:T(8,128)S(1)}, u32[]{:S(2)}, u32[]{:S(2)}) collective-permute-start(f32[224,128]{1,0:T(8,128)S(1)} %bitcast.65), channel_id=1, source_target_pairs={{0,48},{16,32},{32,16},{48,0},{1,49},{17,33},{33,17},{49,1},{2,50}... | collective-permute-start | bytes 344072 | tf_op jit(solution)/shard_map/ppermute | solution.py:21
  18.4 12.3 %collective-permute-start.4 = (f32[2,8,7168]{2,1,0:T(8,128)}, f32[2,8,7168]{2,1,0:T(8,128)S(1)}, u32[]{:S(2)}, u32[]{:S(2)}) collective-permute-start(f32[2,8,7168]{2,1,0:T(8,128)} %dynamic-slice_add_fusion), channel_id=1, source_target_pairs={{0,192},{64,128},{128,64},{192,0},{1,193},{65,129},{129,65},{193,1... | collective-permute-start | bytes 1376264 | tf_op jit(solution)/shard_map/ppermute | solution.py:21
  31.8 8.7 %collective-permute-start.6 = (f32[224,128]{1,0:T(8,128)S(1)}, f32[224,128]{1,0:T(8,128)S(1)}, u32[]{:S(2)}, u32[]{:S(2)}) collective-permute-start(f32[224,128]{1,0:T(8,128)S(1)} %bitcast.66), channel_id=1, source_target_pairs={{0,32},{16,48},{32,0},{48,16},{1,33},{17,49},{33,1},{49,17},{2,34}... | collective-permute-start | bytes 344072 | tf_op jit(solution)/shard_map/ppermute | solution.py:21
  33.2 8.5 %collective-permute-start.7 = (f32[1,8,7168]{2,1,0:T(8,128)S(1)}, f32[1,8,7168]{2,1,0:T(8,128)S(1)}, u32[]{:S(2)}, u32[]{:S(2)}) collective-permute-start(f32[1,8,7168]{2,1,0:T(8,128)S(1)} %dynamic-slice_add_fusion.2), channel_id=1, source_target_pairs={{0,64},{64,0},{128,192},{192,128},{1,65},{65,1},{129,193},{193,129... | collective-permute-start | bytes 688136 | tf_op jit(solution)/shard_map/ppermute | solution.py:21
  33.9 6.6 %collective-permute-start.8 = (f32[1,8,7168]{2,1,0:T(8,128)S(1)}, f32[1,8,7168]{2,1,0:T(8,128)S(1)}, u32[]{:S(2)}, u32[]{:S(2)}) collective-permute-start(f32[1,8,7168]{2,1,0:T(8,128)S(1)} %dynamic-slice_add_fusion.3), channel_id=1, source_target_pairs={{0,192},{64,128},{128,64},{192,0},{1,193},{65,129},{129,65},{193,1... | collective-permute-start | bytes 688136 | tf_op jit(solution)/shard_map/ppermute | solution.py:21
  42.8 9.2 %collective-permute-start.11 = (f32[1,8,3584]{2,1,0:T(8,128)S(1)}, f32[1,8,3584]{2,1,0:T(8,128)S(1)}, u32[]{:S(2)}, u32[]{:S(2)}) collective-permute-start(f32[1,8,3584]{2,1,0:T(8,128)S(1)} %slice_select_fusion.1), channel_id=1, source_target_pairs={{0,48},{16,32},{32,16},{48,0},{1,49},{17,33},{33,17},{49,1},{2,50}... | collective-permute-start | bytes 344072 | tf_op jit(solution)/shard_map/ppermute | solution.py:21
  45.7 5.0 %collective-permute-start.12 = (f32[1,8,3584]{2,1,0:T(8,128)S(1)}, f32[1,8,3584]{2,1,0:T(8,128)S(1)}, u32[]{:S(2)}, u32[]{:S(2)}) collective-permute-start(f32[1,8,3584]{2,1,0:T(8,128)S(1)} %slice_select_fusion), channel_id=1, source_target_pairs={{0,16},{16,0},{32,48},{48,32},{1,17},{17,1},{33,49},{49,33},{2,18}... | collective-permute-start | bytes 344072 | tf_op jit(solution)/shard_map/ppermute | solution.py:21
  47.1 9.9 %collective-permute-start.10 = (f32[4,224,128]{2,1,0:T(8,128)S(1)}, f32[4,224,128]{2,1,0:T(8,128)S(1)}, u32[]{:S(2)}, u32[]{:S(2)}) collective-permute-start(f32[4,224,128]{2,1,0:T(8,128)S(1)} %bitcast_dynamic-update-slice_fusion.5), channel_id=1, source_target_pairs={{0,192},{64,128},{128,64},{192,0},{1,193},{65,129},{129,65},{193,1... | collective-permute-start | bytes 1376264 | tf_op jit(solution)/shard_map/ppermute | solution.py:21
  49.8 8.4 %collective-permute-start.9 = (f32[4,224,128]{2,1,0:T(8,128)S(1)}, f32[4,224,128]{2,1,0:T(8,128)S(1)}, u32[]{:S(2)}, u32[]{:S(2)}) collective-permute-start(f32[4,224,128]{2,1,0:T(8,128)S(1)} %bitcast_dynamic-update-slice_fusion.5), channel_id=1, source_target_pairs={{0,64},{64,0},{128,192},{192,128},{1,65},{65,1},{129,193},{193,129... | collective-permute-start | bytes 1376264 | tf_op jit(solution)/shard_map/ppermute | solution.py:21
  50.7 5.2 %collective-permute-start.14 = (f32[1,8,1792]{2,1,0:T(8,128)S(1)}, f32[1,8,1792]{2,1,0:T(8,128)S(1)}, u32[]{:S(2)}, u32[]{:S(2)}) collective-permute-start(f32[1,8,1792]{2,1,0:T(8,128)S(1)} %slice_select_fusion.2), channel_id=1, source_target_pairs={{0,48},{16,32},{32,16},{48,0},{1,49},{17,33},{33,17},{49,1},{2,50}... | collective-permute-start | bytes 172040 | tf_op jit(solution)/shard_map/ppermute | solution.py:21
  52.1 4.9 %collective-permute-start.13 = (f32[1,8,1792]{2,1,0:T(8,128)S(1)}, f32[1,8,1792]{2,1,0:T(8,128)S(1)}, u32[]{:S(2)}, u32[]{:S(2)}) collective-permute-start(f32[1,8,1792]{2,1,0:T(8,128)S(1)} %slice_select_fusion.3), channel_id=1, source_target_pairs={{0,16},{16,0},{32,48},{48,32},{1,17},{17,1},{33,49},{49,33},{2,18}... | collective-permute-start | bytes 172040 | tf_op jit(solution)/shard_map/ppermute | solution.py:21
  58.2 6.8 %collective-permute-start.20 = (f32[8,128]{1,0:T(8,128)S(1)}, f32[8,128]{1,0:T(8,128)S(1)}, u32[]{:S(2)}, u32[]{:S(2)}) collective-permute-start(f32[8,128]{1,0:T(8,128)S(1)} %add.293), channel_id=1, source_target_pairs={{0,3},{1,2},{2,1},{3,0},{4,7},{5,6},{6,5},{7,4},{8,11},{9,10},{10,... | collective-permute-start | bytes 12296 | tf_op jit(solution)/shard_map/ppermute | solution.py:30
  60.8 6.3 %collective-permute-start.19 = (f32[8,128]{1,0:T(8,128)S(1)}, f32[8,128]{1,0:T(8,128)S(1)}, u32[]{:S(2)}, u32[]{:S(2)}) collective-permute-start(f32[8,128]{1,0:T(8,128)S(1)} %add.293), channel_id=1, source_target_pairs={{0,2},{1,3},{2,0},{3,1},{4,6},{5,7},{6,4},{7,5},{8,10},{9,11},{10,... | collective-permute-start | bytes 12296 | tf_op jit(solution)/shard_map/ppermute | solution.py:30
  61.3 5.8 %collective-permute-start.18 = (f32[8,128]{1,0:T(8,128)S(1)}, f32[8,128]{1,0:T(8,128)S(1)}, u32[]{:S(2)}, u32[]{:S(2)}) collective-permute-start(f32[8,128]{1,0:T(8,128)S(1)} %add.293), channel_id=1, source_target_pairs={{0,1},{1,0},{2,3},{3,2},{4,5},{5,4},{6,7},{7,6},{8,9},{9,8},{10,11... | collective-permute-start | bytes 12296 | tf_op jit(solution)/shard_map/ppermute | solution.py:30
  61.6 6.5 %collective-permute-start.16 = (f32[1,8,1792]{2,1,0:T(8,128)S(1)}, f32[1,8,1792]{2,1,0:T(8,128)S(1)}, u32[]{:S(2)}, u32[]{:S(2)}) collective-permute-start(f32[1,8,1792]{2,1,0:T(8,128)S(1)} %add_multiply_fusion.1), channel_id=1, source_target_pairs={{0,16},{16,0},{32,48},{48,32},{1,17},{17,1},{33,49},{49,33},{2,18}... | collective-permute-start | bytes 172040 | tf_op jit(solution)/shard_map/ppermute | solution.py:21
  62.8 5.2 %collective-permute-start.17 = (f32[1,8,1792]{2,1,0:T(8,128)S(1)}, f32[1,8,1792]{2,1,0:T(8,128)S(1)}, u32[]{:S(2)}, u32[]{:S(2)}) collective-permute-start(f32[1,8,1792]{2,1,0:T(8,128)S(1)} %add_multiply_fusion), channel_id=1, source_target_pairs={{0,48},{16,32},{32,16},{48,0},{1,49},{17,33},{33,17},{49,1},{2,50}... | collective-permute-start | bytes 172040 | tf_op jit(solution)/shard_map/ppermute | solution.py:21
  65.0 21.0 %collective-permute-start.15 = (f32[4,224,128]{2,1,0:T(8,128)S(1)}, f32[4,224,128]{2,1,0:T(8,128)S(1)}, u32[]{:S(2)}, u32[]{:S(2)}) collective-permute-start(f32[4,224,128]{2,1,0:T(8,128)S(1)} %bitcast_dynamic-update-slice_fusion.5), channel_id=1, source_target_pairs={{0,128},{64,192},{128,0},{192,64},{1,129},{65,193},{129,1},{193,65... | collective-permute-start | bytes 1376264 | tf_op jit(solution)/shard_map/ppermute | solution.py:21
  68.1 10.6 %collective-permute-start.25 = (f32[8,128]{1,0:T(8,128)S(1)}, f32[8,128]{1,0:T(8,128)S(1)}, u32[]{:S(2)}, u32[]{:S(2)}) collective-permute-start(f32[8,128]{1,0:T(8,128)S(1)} %add_add_fusion.5), channel_id=1, source_target_pairs={{0,12},{4,8},{8,4},{12,0},{1,13},{5,9},{9,5},{13,1},{2,14},{6,10},... | collective-permute-start | bytes 12296 | tf_op jit(solution)/shard_map/ppermute | solution.py:30
  75.6 4.2 %collective-permute-start.24 = (f32[8,128]{1,0:T(8,128)S(1)}, f32[8,128]{1,0:T(8,128)S(1)}, u32[]{:S(2)}, u32[]{:S(2)}) collective-permute-start(f32[8,128]{1,0:T(8,128)S(1)} %add_add_fusion.5), channel_id=1, source_target_pairs={{0,4},{4,0},{1,5},{5,1},{2,6},{6,2},{3,7},{7,3},{8,12},{12,8},{9,1... | collective-permute-start | bytes 12296 | tf_op jit(solution)/shard_map/ppermute | solution.py:30
  76.6 3.2 %collective-permute-start.23 = (f32[8,128]{1,0:T(8,128)S(1)}, f32[8,128]{1,0:T(8,128)S(1)}, u32[]{:S(2)}, u32[]{:S(2)}) collective-permute-start(f32[8,128]{1,0:T(8,128)S(1)} %add_add_fusion.5), channel_id=1, source_target_pairs={{0,8},{8,0},{1,9},{9,1},{2,10},{10,2},{3,11},{11,3},{4,12},{12,4},... | collective-permute-start | bytes 12296 | tf_op jit(solution)/shard_map/ppermute | solution.py:30
  76.6 7.6 %collective-permute-start.21 = (f32[1,8,3584]{2,1,0:T(8,128)S(1)}, f32[1,8,3584]{2,1,0:T(8,128)S(1)}, u32[]{:S(2)}, u32[]{:S(2)}) collective-permute-start(f32[1,8,3584]{2,1,0:T(8,128)S(1)} %pad_maximum_fusion.6), channel_id=1, source_target_pairs={{0,48},{16,32},{32,16},{48,0},{1,49},{17,33},{33,17},{49,1},{2,50}... | collective-permute-start | bytes 344072 | tf_op jit(solution)/shard_map/ppermute | solution.py:21
  78.7 7.3 %collective-permute-start.22 = (f32[1,8,3584]{2,1,0:T(8,128)S(1)}, f32[1,8,3584]{2,1,0:T(8,128)S(1)}, u32[]{:S(2)}, u32[]{:S(2)}) collective-permute-start(f32[1,8,3584]{2,1,0:T(8,128)S(1)} %pad_maximum_fusion.7), channel_id=1, source_target_pairs={{0,16},{16,0},{32,48},{48,32},{1,17},{17,1},{33,49},{49,33},{2,18}... | collective-permute-start | bytes 344072 | tf_op jit(solution)/shard_map/ppermute | solution.py:21
  86.1 22.6 %copy-start = (f32[4,4,224,128]{3,2,1,0:T(8,128)}, f32[4,4,224,128]{3,2,1,0:T(8,128)S(1)}, u32[]{:S(2)}) copy-start(f32[4,4,224,128]{3,2,1,0:T(8,128)S(1)} %bitcast_dynamic-update-slice_fusion) | copy-start | bytes 5505028
  86.1 9.9 %collective-permute-start.27 = (f32[1,8,7168]{2,1,0:T(8,128)S(1)}, f32[1,8,7168]{2,1,0:T(8,128)S(1)}, u32[]{:S(2)}, u32[]{:S(2)}) collective-permute-start(f32[1,8,7168]{2,1,0:T(8,128)S(1)} %pad_maximum_fusion.5), channel_id=1, source_target_pairs={{0,192},{64,128},{128,64},{192,0},{1,193},{65,129},{129,65},{193,1... | collective-permute-start | bytes 688136 | tf_op jit(solution)/shard_map/ppermute | solution.py:21
  88.4 4.6 %collective-permute-start.30 = (f32[8,128]{1,0:T(8,128)S(1)}, f32[8,128]{1,0:T(8,128)S(1)}, u32[]{:S(2)}, u32[]{:S(2)}) collective-permute-start(f32[8,128]{1,0:T(8,128)S(1)} %add_add_fusion.4), channel_id=1, source_target_pairs={{0,192},{64,128},{128,64},{192,0},{1,193},{65,129},{129,65},{193,1... | collective-permute-start | bytes 12296 | tf_op jit(solution)/shard_map/ppermute | solution.py:30
  89.0 7.0 %collective-permute-start.29 = (f32[8,128]{1,0:T(8,128)S(1)}, f32[8,128]{1,0:T(8,128)S(1)}, u32[]{:S(2)}, u32[]{:S(2)}) collective-permute-start(f32[8,128]{1,0:T(8,128)S(1)} %add_add_fusion.4), channel_id=1, source_target_pairs={{0,128},{64,192},{128,0},{192,64},{1,129},{65,193},{129,1},{193,65... | collective-permute-start | bytes 12296 | tf_op jit(solution)/shard_map/ppermute | solution.py:30
  90.8 5.2 %collective-permute-start.28 = (f32[8,128]{1,0:T(8,128)S(1)}, f32[8,128]{1,0:T(8,128)S(1)}, u32[]{:S(2)}, u32[]{:S(2)}) collective-permute-start(f32[8,128]{1,0:T(8,128)S(1)} %add_add_fusion.4), channel_id=1, source_target_pairs={{0,64},{64,0},{128,192},{192,128},{1,65},{65,1},{129,193},{193,129... | collective-permute-start | bytes 12296 | tf_op jit(solution)/shard_map/ppermute | solution.py:30
  91.7 5.0 %collective-permute-start.26 = (f32[1,8,7168]{2,1,0:T(8,128)S(1)}, f32[1,8,7168]{2,1,0:T(8,128)S(1)}, u32[]{:S(2)}, u32[]{:S(2)}) collective-permute-start(f32[1,8,7168]{2,1,0:T(8,128)S(1)} %pad_maximum_fusion.4), channel_id=1, source_target_pairs={{0,64},{64,0},{128,192},{192,128},{1,65},{65,1},{129,193},{193,129... | collective-permute-start | bytes 688136 | tf_op jit(solution)/shard_map/ppermute | solution.py:21
  93.0 6.4 %collective-permute-start.31 = (f32[16,224,128]{2,1,0:T(8,128)S(1)}, f32[16,224,128]{2,1,0:T(8,128)S(1)}, u32[]{:S(2)}, u32[]{:S(2)}) collective-permute-start(f32[16,224,128]{2,1,0:T(8,128)S(1)} %bitcast.50), channel_id=1, source_target_pairs={{0,8},{8,0},{1,9},{9,1},{2,10},{10,2},{3,11},{11,3},{4,12},{12,4},... | collective-permute-start | bytes 5505032 | tf_op jit(solution)/shard_map/ppermute | solution.py:21
  99.4 1.2 copy-start.1
  99.4 18.4 %collective-permute-start.35 = (f32[2,8,7168]{2,1,0:T(8,128)S(1)}, f32[2,8,7168]{2,1,0:T(8,128)}, u32[]{:S(2)}, u32[]{:S(2)}) collective-permute-start(f32[2,8,7168]{2,1,0:T(8,128)S(1)} %pad_maximum_fusion.3), channel_id=1, source_target_pairs={{0,64},{64,0},{128,192},{192,128},{1,65},{65,1},{129,193},{193,129... | collective-permute-start | bytes 1376264 | tf_op jit(solution)/shard_map/ppermute | solution.py:21
  100.7 15.8 %collective-permute-start.34 = (f32[8,128]{1,0:T(8,128)S(1)}, f32[8,128]{1,0:T(8,128)S(1)}, u32[]{:S(2)}, u32[]{:S(2)}) collective-permute-start(f32[8,128]{1,0:T(8,128)S(1)} %add_add_fusion.3), channel_id=1, source_target_pairs={{0,48},{16,32},{32,16},{48,0},{1,49},{17,33},{33,17},{49,1},{2,50}... | collective-permute-start | bytes 12296 | tf_op jit(solution)/shard_map/ppermute | solution.py:30
  102.8 13.6 %collective-permute-start.33 = (f32[8,128]{1,0:T(8,128)S(1)}, f32[8,128]{1,0:T(8,128)S(1)}, u32[]{:S(2)}, u32[]{:S(2)}) collective-permute-start(f32[8,128]{1,0:T(8,128)S(1)} %add_add_fusion.3), channel_id=1, source_target_pairs={{0,32},{16,48},{32,0},{48,16},{1,33},{17,49},{33,1},{49,17},{2,34}... | collective-permute-start | bytes 12296 | tf_op jit(solution)/shard_map/ppermute | solution.py:30
  105.5 10.9 %collective-permute-start.32 = (f32[8,128]{1,0:T(8,128)S(1)}, f32[8,128]{1,0:T(8,128)S(1)}, u32[]{:S(2)}, u32[]{:S(2)}) collective-permute-start(f32[8,128]{1,0:T(8,128)S(1)} %add_add_fusion.3), channel_id=1, source_target_pairs={{0,16},{16,0},{32,48},{48,32},{1,17},{17,1},{33,49},{49,33},{2,18}... | collective-permute-start | bytes 12296 | tf_op jit(solution)/shard_map/ppermute | solution.py:30
  106.5 14.0 %collective-permute-start.36 = (f32[2,8,7168]{2,1,0:T(8,128)S(1)}, f32[2,8,7168]{2,1,0:T(8,128)}, u32[]{:S(2)}, u32[]{:S(2)}) collective-permute-start(f32[2,8,7168]{2,1,0:T(8,128)S(1)} %pad_maximum_fusion.2), channel_id=1, source_target_pairs={{0,192},{64,128},{128,64},{192,0},{1,193},{65,129},{129,65},{193,1... | collective-permute-start | bytes 1376264 | tf_op jit(solution)/shard_map/ppermute | solution.py:21
  119.0 7.6 %collective-permute-start.37 = (f32[4,8,7168]{2,1,0:T(8,128)S(1)}, f32[4,8,7168]{2,1,0:T(8,128)S(1)}, u32[]{:S(2)}, u32[]{:S(2)}) collective-permute-start(f32[4,8,7168]{2,1,0:T(8,128)S(1)} %pad_maximum_fusion), channel_id=1, source_target_pairs={{0,8},{8,0},{1,9},{9,1},{2,10},{10,2},{3,11},{11,3},{4,12},{12,4},... | collective-permute-start | bytes 2752520 | tf_op jit(solution)/shard_map/ppermute | solution.py:21
  121.7 4.8 %collective-permute-start.38 = (f32[4,8,7168]{2,1,0:T(8,128)S(1)}, f32[4,8,7168]{2,1,0:T(8,128)S(1)}, u32[]{:S(2)}, u32[]{:S(2)}) collective-permute-start(f32[4,8,7168]{2,1,0:T(8,128)S(1)} %pad_maximum_fusion.1), channel_id=1, source_target_pairs={{0,8},{8,0},{1,9},{9,1},{2,10},{10,2},{3,11},{11,3},{4,12},{12,4},... | collective-permute-start | bytes 2752520 | tf_op jit(solution)/shard_map/ppermute | solution.py:21

commit v4 on v0

v4 whole, which is shorter than its diff:
```python
import math

import jax
import jax.numpy as jnp
from jax import lax
from jax.experimental import pallas as pl
from jax.experimental.pallas import tpu as pltpu
from jax.sharding import Mesh, PartitionSpec as P

momentum_decay = 0.9
outer_rate = 0.7
clip_rms = 0.25

REPLICA = ("y", "zh", "core")
SUB = 8
LANE = 128
MASKS = (1, 3, 2)
HOLD_BYTES = 2 << 20
IN_VMEM = pl.BlockSpec(memory_space=pltpu.VMEM)


def swap(x, /, **masks):
    axes = tuple(masks)
    sizes = [lax.axis_size(a) for a in axes]
    mask = 0
    for a, n in zip(axes, sizes):
        mask = mask * n + masks[a]
    return lax.ppermute(x, axes, [(i, i ^ mask) for i in range(math.prod(sizes))])


def after(x, other):
    tile = other.reshape(-1, SUB, other.shape[-1])[0, :, :LANE]
    return x + 0.0 * jnp.clip(tile, -1.0, 1.0)


def hold_kernel(tile_ref, x_ref, out_ref):
    del tile_ref
    out_ref[...] = x_ref[...]


def hold(x, other):
    tile = other.reshape(-1, SUB, other.shape[-1])[0, :, :LANE]
    flat = x.reshape(-1, LANE)
    return pl.pallas_call(
        hold_kernel,
        out_shape=jax.ShapeDtypeStruct(flat.shape, flat.dtype),
        in_specs=[IN_VMEM, IN_VMEM],
        out_specs=IN_VMEM,
        cost_estimate=pl.CostEstimate(flops=0, bytes_accessed=HOLD_BYTES, transcendentals=0),
        compiler_params=pltpu.CompilerParams(vmem_limit_bytes=16 << 20),
        name="hold",
    )(tile, flat).reshape(x.shape)


def rows_at(x, start, count):
    return lax.dynamic_slice_in_dim(x, start, count, 0)


def half(x, bit):
    middle = x.shape[-1] // 2
    return jnp.where(bit == 0, x[..., :middle], x[..., middle:])


def join(mine, other, bit, dim):
    low, high = jnp.where(bit == 0, mine, other), jnp.where(bit == 0, other, mine)
    return jnp.concatenate([low, high], dim)


def final_kernel(ceiling, place_ref, anchor_ref, own_ref, mine_ref, other_ref, *refs):
    pieces, sums, (out_ref, moment_ref, grad) = refs[:8], refs[8:16], refs[16:]
    step = pl.program_id(0)
    high = pieces[0].shape[0]
    row = sums[0][0:1, :]
    for part in sums[1:]:
        row = row + part[0:1, :]
    scaling = ceiling / jnp.maximum(jnp.sqrt(jnp.sum(row, axis=1, keepdims=True)), ceiling)
    factor = (outer_rate * (1.0 + momentum_decay)) * scaling
    swapped = place_ref[8] != 0
    parts = []
    for g in range(mine_ref.shape[0]):
        mine, other = mine_ref[g], other_ref[g]
        parts += [jnp.where(swapped, other, mine), jnp.where(swapped, mine, other)]
    moment = jnp.concatenate(parts, 0).T
    for i, piece in enumerate(pieces):
        at = pl.multiple_of(place_ref[i] * high, high)
        grad[pl.ds(at, high), :] = piece[...]
    rest = anchor_ref[...] - (outer_rate * momentum_decay * momentum_decay) * moment
    out_ref[...] = rest - factor * grad[...]

    @pl.when(step == place_ref[9])
    def _():
        shard = own_ref.shape[0]
        turned = grad[...].T
        own = turned[0:shard]
        for k in range(1, turned.shape[0] // shard):
            own = jnp.where(place_ref[10] == k, turned[k * shard : (k + 1) * shard], own)
        moment_ref[...] = momentum_decay * own_ref[...] + scaling * own


def final(ceiling, place, anchor, own_moment, mine, other, pieces):
    rows, cols = anchor.shape
    groups, shard, _ = mine.shape
    high = pieces[0].shape[0]
    per = 4
    width = per * 2 * shard
    block = pl.BlockSpec((rows, width), lambda i, p: (0, i))
    part = pl.BlockSpec((per, shard, rows), lambda i, p: (i, 0, 0))
    piece = pl.BlockSpec((high, width), lambda i, p: (0, i))
    squares = pl.BlockSpec((SUB, LANE), lambda i, p: (0, cols // LANE))
    whole = pl.BlockSpec(own_moment.shape, lambda i, p: (0, 0))
    count = len(pieces)
    return pl.pallas_call(
        lambda *refs: final_kernel(ceiling, *refs),
        out_shape=(
            jax.ShapeDtypeStruct(anchor.shape, anchor.dtype),
            jax.ShapeDtypeStruct(own_moment.shape, own_moment.dtype),
        ),
        grid_spec=pltpu.PrefetchScalarGridSpec(
            num_scalar_prefetch=1,
            grid=(groups // per,),
            in_specs=[block, whole, part, part] + [piece] * count + [squares] * count,
            out_specs=(block, whole),
            scratch_shapes=[pltpu.VMEM((rows, width), jnp.float32)],
        ),
        cost_estimate=pl.CostEstimate(flops=5 * rows * cols, bytes_accessed=16 * rows * cols, transcendentals=0),
        compiler_params=pltpu.CompilerParams(vmem_limit_bytes=56 << 20),
        name="final",
    )(place, anchor, own_moment, mine, other, *pieces, *pieces)


def on_device(anchor, local_weights, momentum):
    y, zh, core = (lax.axis_index(a) for a in REPLICA)
    replicas = math.prod(lax.axis_size(a) for a in REPLICA)
    elements = anchor.shape[0] * anchor.shape[1] * lax.axis_size("zl") * lax.axis_size("x")
    ceiling = clip_rms * math.sqrt(elements)
    rows, cols = anchor.shape
    blocks = rows // SUB
    a_rows = anchor.reshape(blocks, SUB, cols)
    l_rows = local_weights.reshape(blocks, SUB, cols)
    own_moment = momentum[:, 0, :].T
    shard = own_moment.shape[0]

    high = blocks // 8

    def drift(start, count):
        return rows_at(a_rows, start, count) - rows_at(l_rows, start, count)

    over_core = {}
    for pair in ((y >> 1) ^ 1, y >> 1):
        start = ((1 - core) * 4 + pair * 2) * high
        over_core[len(over_core)] = swap(drift(start, 2 * high), core=1)

    def summed(mask):
        at = rows_at(over_core[1 - (mask >> 1)], ((y ^ mask) & 1) * high, high)
        return drift((core * 4 + (y ^ mask)) * high, high) + at

    over_y = {}
    for mask in (3, 2, 1):
        over_y[mask] = swap(summed(mask), y=mask)
    moments = {0: own_moment}
    for mask in MASKS:
        moments[mask] = swap(own_moment, zh=mask)
    total = summed(0)
    for mask in (3, 2, 1):
        total = total + over_y[mask]

    def part_of(x, index):
        return half(rows_at(x, index >> 1, 1), index & 1)

    sends = {mask: part_of(total, zh ^ mask) for mask in MASKS}
    own = part_of(total, zh)

    moment = jnp.zeros((4, shard // SUB, SUB, LANE), own_moment.dtype)
    for mask, part in moments.items():
        part = after(part.reshape(shard // SUB, SUB, LANE), total)
        moment = lax.dynamic_update_index_in_dim(moment, part, zh ^ mask, 0)
    moment_y = hold(moment, sends[2])
    moments = {mask: swap(moment_y, y=mask) for mask in (1, 3)}
    for mask in MASKS:
        own = own + swap(sends[mask], zh=mask)
    own = own * (1.0 / replicas)
    moments[2] = swap(hold(moment, own), y=2)

    place = [(core ^ c) * 4 + (y ^ mask) for c in (0, 1) for mask in (0, 1, 3, 2)]
    place = jnp.stack(place + [core, (y * 8 + zh * 2 + core) // 8, zh * 2 + core]).astype(jnp.int32)

    def add_squares(squares, axes):
        n = math.prod(lax.axis_size(a) for a in axes)
        row = jnp.sum(squares, axis=0, keepdims=True)
        return jnp.sum(lax.all_to_all(jnp.broadcast_to(row, (n,) + row.shape), axes, 0, 0), axis=0)

    squares = jnp.sum(own.reshape(SUB, -1, LANE) ** 2, axis=1)
    back = {mask: swap(own, zh=mask) for mask in MASKS}
    squares = add_squares(squares, ("zh", "zl", "x"))
    own = join(join(own, back[1], zh & 1, 2), join(back[2], back[3], zh & 1, 2), zh >> 1, 0)

    squares = jnp.broadcast_to(squares, own.shape[:2] + (LANE,))
    squares = after(after(squares, moments[1]), moments[3])
    whole = jnp.zeros((4,) + moment.shape, own_moment.dtype)
    for mask, part in ((0, moment),) + tuple(moments.items()):
        whole = lax.dynamic_update_index_in_dim(whole, after(part, own), y ^ mask, 0)
    whole = whole.reshape(16, shard, LANE)
    own = jnp.concatenate([own, squares], 2)
    pieces = [own] + [swap(own, y=mask) for mask in (1, 3, 2)]
    pieces += [swap(piece, core=1) for piece in pieces]
    pieces = [piece.reshape(high * SUB, cols + LANE) for piece in pieces]
    new_anchor, new_moment = final(ceiling, place, anchor, own_moment, whole, swap(whole, core=1), pieces)
    return new_anchor, new_moment.T[:, None, :]


def solution(mesh):
    fine = Mesh(mesh.devices.reshape(4, 4, 2, 2, 4), ("y", "zh", "core", "zl", "x"))
    in_specs = (P("zl", "x"), P(REPLICA, "zl", "x"), P("zl", "x", REPLICA))
    out_specs = (P("zl", "x"), P("zl", "x", REPLICA))
    return jax.shard_map(on_device, mesh=fine, in_specs=in_specs, out_specs=out_specs, check_vma=False)
```

time: 410 us -> 121 us (0.30)
  waiting for transfers between devices: 341 us -> 34.7 us
  starting transfers between devices: 0.08 us -> 66.1 us
  blocking collectives: 16.1 us -> 0 us
  local copies, waits for them, and re-layouts: 17.3 us -> 2.86 us
  between operations: 14.8 us -> 1.12 us
  other arithmetic: 19.9 us -> 7.81 us
  Pallas kernels: 0 us -> 7.84 us
    psum x1 -> x0, waiting for transfers between devices: 299 us -> none  [on_device(): summed = lax.psum(drift_term, 'replica')]
    ppermute x0 -> x25, starting transfers between devices: none -> 55.3 us  [swap(): lax.ppermute(x, axes, [(i, i ^ mask) for i in range(math.prod(sizes))])]
    all_gather x1 -> x0, waiting for transfers between devices: 41.1 us -> none  [on_device(): gathered = lax.all_gather(momentum, 'replica', axis=2, tiled=True)]
    ppermute x0 -> x25, waiting for transfers between devices: none -> 31.8 us  [swap(): lax.ppermute(x, axes, [(i, i ^ mask) for i in range(math.prod(sizes))])]
    psum x1 -> x0, blocking collectives: 16.1 us -> none  [on_device(): squares = lax.psum(jnp.sum(pseudo_grad * pseudo_grad), ('fsdp', 'tensor'))]
    unnamed x7 -> x20, local copies, waits for them, and re-layouts: 15.8 us -> 1.35 us
    all_to_all x0 -> x1, starting transfers between devices: none -> 10.8 us  [add_squares(): lax.all_to_all(jnp.broadcast_to(row, (n,) + row.shape), axes, 0, 0)]
    pallas_call x0 -> x3, Pallas kernels: none -> 7.84 us  [the longest x1 7.77 us: final(): pl.pallas_call(lambda *refs: final_kernel(ceiling, *refs), out_shape=(jax...]
  transfers between devices with their start and end apart: 2 -> 26, of which waited for: 2 -> 9; matrix products, arithmetic and copies ran while one was open for 1% -> 4% of each run, Pallas kernels for 0% -> 0%
where the time goes in v4:
time: 121 us; the launch traced here: 120 us
  starting transfers between devices  66.1 us (55%)
  waiting for transfers between devices  34.7 us (29%)
  Pallas kernels  7.84 us (6%)
  other arithmetic  7.81 us (6%)
  local copies, waits for them, and re-layouts  2.86 us (2%)
    ppermute x25, starting transfers between devices, swap(): lax.ppermute(x, axes, [(i, i ^ mask) for i in range(math.prod(sizes))])  55.3 us
    ppermute x25, waiting for transfers between devices, swap(): lax.ppermute(x, axes, [(i, i ^ mask) for i in range(math.prod(sizes))])  31.8 us
    all_to_all x1, starting transfers between devices, add_squares(): lax.all_to_all(jnp.broadcast_to(row, (n,) + row.shape), axes, 0, 0)  10.8 us
    pallas_call x1, Pallas kernels, final(): pl.pallas_call(lambda *refs: final_kernel(ceiling, *refs), out_shape=(jax...  7.77 us
    sub x1, other arithmetic, drift(): return rows_at(a_rows, start, count) - rows_at(l_rows, start, count)  3.12 us
    all_to_all x1, waiting for transfers between devices, add_squares(): lax.all_to_all(jnp.broadcast_to(row, (n,) + row.shape), axes, 0, 0)  2.83 us
  transfers between devices with their start and end apart: 26, of which 9 were waited for; matrix products, arithmetic and copies ran while one was open for 4% of the time, Pallas kernels for 0%

profile of v4, /device:TPU:1, one launch (start us, length us, event | category | flops | bytes accessed | tf_op | source)
XLA Modules:
  0.0 120.4 jit_solution(14836551153509883658)
XLA Ops:
  0.6 3.1 %dynamic-slice_subtract_fusion = (f32[4,8,7168]{2,1,0:T(8,128)}, f32[4,8,7168]{2,1,0:T(8,128)S(1)}) fusion(f32[16,8,7168]{2,1,0:T(8,128)} %bitcast.90, s32[]{:T(128)S(6)} %select_n.154, f32[16,8,7168]{2,1,0:T(8,128)} %bitcast.85, s32[]{:T(128)S(6)} %select_n.151), kind=kLoop, calls=%fused_computation | loop fusion | flops 458752 | bytes 5505032 | tf_op jit(solution)/shard_map/sub | solution.py:146
  3.8 3.2 %collective-permute-start.1 = (f32[4,8,7168]{2,1,0:T(8,128)}, f32[4,8,7168]{2,1,0:T(8,128)S(1)}, u32[]{:S(2)}, u32[]{:S(2)}) collective-permute-start(f32[4,8,7168]{2,1,0:T(8,128)} %get-tuple-element.11), channel_id=1, source_target_pairs={{0,8},{8,0},{1,9},{9,1},{2,10},{10,2},{3,11},{11,3},{4,12},{12,4},... | collective-permute-start | bytes 2752520 | tf_op jit(solution)/shard_map/ppermute | solution.py:28
  7.0 0.0 collective-permute-start
  7.0 3.6 %collective-permute-done.1 = f32[4,8,7168]{2,1,0:T(8,128)S(1)} collective-permute-done((f32[4,8,7168]{2,1,0:T(8,128)}, f32[4,8,7168]{2,1,0:T(8,128)S(1)}, u32[]{:S(2)}, u32[]{:S(2)}) %collective-permute-start.1) | collective-permute-done | bytes 917536 | tf_op jit(solution)/shard_map/ppermute | solution.py:28
  10.6 0.0 collective-permute-done
  10.6 1.9 %dynamic-slice_add_fusion.2 = (f32[2,8,7168]{2,1,0:T(8,128)S(1)}, f32[2,8,7168]{2,1,0:T(8,128)S(1)}, f32[2,8,7168]{2,1,0:T(8,128)S(1)}) fusion(f32[4,8,7168]{2,1,0:T(8,128)S(1)} %collective-permute-done.1, s32[]{:T(128)S(6)} %select_n.155, f32[16,8,7168]{2,1,0:T(8,128)} %bitcast.91, s32[]{:T(128)S(6)} %select_n.153, f32[16,8,7168]{2,1,0:T(8,128)} %bitcast.86, ...), kind=kLoop, calls=%fused_computation.12 | loop fusion | flops 688128 | bytes 5505048 | tf_op jit(solution)/shard_map/add | solution.py:155
  12.5 1.1 collective-permute-start.2
  13.6 0.3 collective-permute-start.3
  13.9 1.9 %collective-permute-start.4 = (f32[2,8,7168]{2,1,0:T(8,128)S(1)}, f32[2,8,7168]{2,1,0:T(8,128)}, u32[]{:S(2)}, u32[]{:S(2)}) collective-permute-start(f32[2,8,7168]{2,1,0:T(8,128)S(1)} %get-tuple-element.10), channel_id=1, source_target_pairs={{0,64},{64,0},{128,192},{192,128},{1,65},{65,1},{129,193},{193,129... | collective-permute-start | bytes 1376264 | tf_op jit(solution)/shard_map/ppermute | solution.py:28
  15.9 5.3 %collective-permute-start.7 = (f32[224,128]{1,0:T(8,128)S(1)}, f32[224,128]{1,0:T(8,128)S(1)}, u32[]{:S(2)}, u32[]{:S(2)}) collective-permute-start(f32[224,128]{1,0:T(8,128)S(1)} %bitcast.110), channel_id=1, source_target_pairs={{0,32},{16,48},{32,0},{48,16},{1,33},{17,49},{33,1},{49,17},{2,34}... | collective-permute-start | bytes 344072 | tf_op jit(solution)/shard_map/ppermute | solution.py:28
  21.2 0.0 collective-permute-start.6
  21.2 0.7 stack.47.refs_0_
  21.9 13.5 %collective-permute-done.2 = f32[2,8,7168]{2,1,0:T(8,128)S(1)} collective-permute-done((f32[2,8,7168]{2,1,0:T(8,128)S(1)}, f32[2,8,7168]{2,1,0:T(8,128)S(1)}, u32[]{:S(2)}, u32[]{:S(2)}) %collective-permute-start.2) | collective-permute-done | bytes 458784 | tf_op jit(solution)/shard_map/ppermute | solution.py:28
  35.4 1.4 %collective-permute-start.5 = (f32[224,128]{1,0:T(8,128)S(1)}, f32[224,128]{1,0:T(8,128)S(1)}, u32[]{:S(2)}, u32[]{:S(2)}) collective-permute-start(f32[224,128]{1,0:T(8,128)S(1)} %bitcast.112), channel_id=1, source_target_pairs={{0,16},{16,0},{32,48},{48,32},{1,17},{17,1},{33,49},{49,33},{2,18}... | collective-permute-start | bytes 344072 | tf_op jit(solution)/shard_map/ppermute | solution.py:28
  36.8 0.0 collective-permute-done.3
  36.8 0.0 collective-permute-done.4
  36.8 1.4 %add_add_fusion = f32[2,8,7168]{2,1,0:T(8,128)S(1)} fusion(f32[2,8,7168]{2,1,0:T(8,128)} %collective-permute-done.4, f32[2,8,7168]{2,1,0:T(8,128)S(1)} %collective-permute-done.3, f32[2,8,7168]{2,1,0:T(8,128)S(1)} %collective-permute-done.2, f32[4,8,7168]{2,1,0:T(8,128)S(1)} %collective-permute-done, s32[]{:T(128)S(6)} %select_n.152, ...), kind=kLoop, calls=%fused_computation.10 | loop fusion | flops 573440 | bytes 3211272 | tf_op jit(solution)/shard_map/add | solution.py:165
  38.2 0.1 dynamic-slice_select_fusion.2
  38.3 1.1 collective-permute-start.8
  39.3 4.4 %collective-permute-start.9 = (f32[1,8,3584]{2,1,0:T(8,128)S(1)}, f32[1,8,3584]{2,1,0:T(8,128)S(1)}, u32[]{:S(2)}, u32[]{:S(2)}) collective-permute-start(f32[1,8,3584]{2,1,0:T(8,128)S(1)} %get-tuple-element.17), channel_id=1, source_target_pairs={{0,48},{16,32},{32,16},{48,0},{1,49},{17,33},{33,17},{49,1},{2,50}... | collective-permute-start | bytes 344072 | tf_op jit(solution)/shard_map/ppermute | solution.py:28
  43.8 0.0 collective-permute-done.5
  43.8 7.1 %collective-permute-start.10 = (f32[1,8,3584]{2,1,0:T(8,128)S(1)}, f32[1,8,3584]{2,1,0:T(8,128)S(1)}, u32[]{:S(2)}, u32[]{:S(2)}) collective-permute-start(f32[1,8,3584]{2,1,0:T(8,128)S(1)} %get-tuple-element.16), channel_id=1, source_target_pairs={{0,32},{16,48},{32,0},{48,16},{1,33},{17,49},{33,1},{49,17},{2,34}... | collective-permute-start | bytes 344072 | tf_op jit(solution)/shard_map/ppermute | solution.py:28
  50.9 0.0 collective-permute-done.6
  50.9 0.0 collective-permute-done.7
  51.0 3.2 %collective-permute-start.15 = (f32[4,28,8,128]{3,2,1,0:T(8,128)S(1)}, f32[4,28,8,128]{3,2,1,0:T(8,128)S(1)}, u32[]{:S(2)}, u32[]{:S(2)}) collective-permute-start(f32[4,28,8,128]{3,2,1,0:T(8,128)S(1)} %bitcast.82), channel_id=1, source_target_pairs={{0,192},{64,128},{128,64},{192,0},{1,193},{65,129},{129,65},{193,1... | collective-permute-start | bytes 1376264 | tf_op jit(solution)/shard_map/ppermute | solution.py:28
  54.2 0.0 collective-permute-start.14
  54.2 0.0 collective-permute-done.8
  54.2 0.0 collective-permute-done.9
  54.2 0.0 collective-permute-done.10
  54.2 0.1 multiply_reduce_fusion
  54.4 0.6 broadcast_in_dim.54
  55.0 10.8 %all-to-all-start = ((f32[32,1,128]{2,1,0:T(1,128)}), f32[32,1,128]{2,1,0:T(1,128)S(1)}, u32[]{:S(2)}, u32[]{:S(2)}) async-start(f32[32,1,128]{2,1,0:T(1,128)} %broadcast_in_dim.54), calls=%async_computation | async-start | bytes 32768 | tf_op jit(solution)/shard_map/all_to_all | solution.py:190
  65.8 2.2 %collective-permute-start.11 = (f32[1,8,3584]{2,1,0:T(8,128)S(1)}, f32[1,8,3584]{2,1,0:T(8,128)S(1)}, u32[]{:S(2)}, u32[]{:S(2)}) collective-permute-start(f32[1,8,3584]{2,1,0:T(8,128)S(1)} %get-tuple-element.7), channel_id=1, source_target_pairs={{0,16},{16,0},{32,48},{48,32},{1,17},{17,1},{33,49},{49,33},{2,18}... | collective-permute-start | bytes 344072 | tf_op jit(solution)/shard_map/ppermute | solution.py:28
  68.0 3.3 %collective-permute-start.13 = (f32[1,8,3584]{2,1,0:T(8,128)S(1)}, f32[1,8,3584]{2,1,0:T(8,128)S(1)}, u32[]{:S(2)}, u32[]{:S(2)}) collective-permute-start(f32[1,8,3584]{2,1,0:T(8,128)S(1)} %get-tuple-element.7), channel_id=1, source_target_pairs={{0,48},{16,32},{32,16},{48,0},{1,49},{17,33},{33,17},{49,1},{2,50}... | collective-permute-start | bytes 344072 | tf_op jit(solution)/shard_map/ppermute | solution.py:28
  71.3 0.2 collective-permute-start.12
  71.5 2.8 %all-to-all-done = f32[32,1,128]{2,1,0:T(1,128)S(1)} async-done(((f32[32,1,128]{2,1,0:T(1,128)}), f32[32,1,128]{2,1,0:T(1,128)S(1)}, u32[]{:S(2)}, u32[]{:S(2)}) %all-to-all-start) | async-done | bytes 16416 | tf_op jit(solution)/shard_map/all_to_all | solution.py:190
  74.4 0.0 collective-permute-done.11
  74.4 1.4 %collective-permute-start.16 = (f32[4,28,8,128]{3,2,1,0:T(8,128)S(1)}, f32[4,28,8,128]{3,2,1,0:T(8,128)S(1)}, u32[]{:S(2)}, u32[]{:S(2)}) collective-permute-start(f32[4,28,8,128]{3,2,1,0:T(8,128)S(1)} %bitcast.84), channel_id=1, source_target_pairs={{0,128},{64,192},{128,0},{192,64},{1,129},{65,193},{129,1},{193,65... | collective-permute-start | bytes 1376264 | tf_op jit(solution)/shard_map/ppermute | solution.py:28
  75.9 0.0 collective-permute-done.13
  75.9 4.5 %collective-permute-done.12 = f32[1,8,3584]{2,1,0:T(8,128)S(1)} collective-permute-done((f32[1,8,3584]{2,1,0:T(8,128)S(1)}, f32[1,8,3584]{2,1,0:T(8,128)S(1)}, u32[]{:S(2)}, u32[]{:S(2)}) %collective-permute-start.12) | collective-permute-done | bytes 114720 | tf_op jit(solution)/shard_map/ppermute | solution.py:28
  80.4 0.2 broadcast_in_dim.48
  80.6 0.0 collective-permute-done.15
  80.7 0.0 collective-permute-done.14
  80.7 1.4 %collective-permute-start.20 = (f32[2,8,7296]{2,1,0:T(8,128)S(1)}, f32[2,8,7296]{2,1,0:T(8,128)S(1)}, u32[]{:S(2)}, u32[]{:S(2)}) collective-permute-start(f32[2,8,7296]{2,1,0:T(8,128)S(1)} %pad_maximum_fusion.1), channel_id=1, source_target_pairs={{0,128},{64,192},{128,0},{192,64},{1,129},{65,193},{129,1},{193,65... | collective-permute-start | bytes 1400840 | tf_op jit(solution)/shard_map/ppermute | solution.py:28
  82.1 0.8 collective-permute-start.19
  82.9 0.6 collective-permute-start.18
  83.6 0.6 collective-permute-done.16
  84.2 8.4 %collective-permute-start.17 = (f32[16,224,128]{2,1,0:T(8,128)S(1)}, f32[16,224,128]{2,1,0:T(8,128)S(1)}, u32[]{:S(2)}, u32[]{:S(2)}) collective-permute-start(f32[16,224,128]{2,1,0:T(8,128)S(1)} %bitcast.88), channel_id=1, source_target_pairs={{0,8},{8,0},{1,9},{9,1},{2,10},{10,2},{3,11},{11,3},{4,12},{12,4},... | collective-permute-start | bytes 5505032 | tf_op jit(solution)/shard_map/ppermute | solution.py:28
  92.6 0.1 collective-permute-start.21
  92.7 2.4 %collective-permute-done.20 = f32[2,8,7296]{2,1,0:T(8,128)S(1)} collective-permute-done((f32[2,8,7296]{2,1,0:T(8,128)S(1)}, f32[2,8,7296]{2,1,0:T(8,128)S(1)}, u32[]{:S(2)}, u32[]{:S(2)}) %collective-permute-start.20) | collective-permute-done | bytes 466976 | tf_op jit(solution)/shard_map/ppermute | solution.py:28
  95.1 7.3 %collective-permute-start.24 = (f32[2,8,7296]{2,1,0:T(8,128)S(1)}, f32[2,8,7296]{2,1,0:T(8,128)S(1)}, u32[]{:S(2)}, u32[]{:S(2)}) collective-permute-start(f32[2,8,7296]{2,1,0:T(8,128)S(1)} %collective-permute-done.20), channel_id=1, source_target_pairs={{0,8},{8,0},{1,9},{9,1},{2,10},{10,2},{3,11},{11,3},{4,12},{12,4},... | collective-permute-start | bytes 1400840 | tf_op jit(solution)/shard_map/ppermute | solution.py:28
  102.4 6.0 %collective-permute-done.19 = f32[2,8,7296]{2,1,0:T(8,128)S(1)} collective-permute-done((f32[2,8,7296]{2,1,0:T(8,128)S(1)}, f32[2,8,7296]{2,1,0:T(8,128)S(1)}, u32[]{:S(2)}, u32[]{:S(2)}) %collective-permute-start.19) | collective-permute-done | bytes 466976 | tf_op jit(solution)/shard_map/ppermute | solution.py:28
  108.4 0.5 collective-permute-start.23
  108.9 0.1 collective-permute-start.22
  109.0 0.8 pad_maximum_fusion.refs_5_.refs_13_
  109.9 0.0 collective-permute-done.21
  109.9 0.0 collective-permute-done.24
  109.9 0.5 collective-permute-done.23
  110.4 0.7 collective-permute-done.22
  111.1 0.0 collective-permute-done.17.refs_4_
  111.1 0.1 copy-done.6
  111.2 0.7 copy-done.7
  111.8 0.6 copy-done.8
  112.4 7.8 %final.1 = (f32[128,7168]{1,0:T(8,128)}, f32[224,128]{1,0:T(8,128)}) custom-call(s32[11]{0:T(128)} %stack.47.refs_0_, f32[128,7168]{1,0:T(8,128)} %refs_1_.1, f32[224,128]{1,0:T(8,128)} %bitcast.109, f32[16,224,128]{2,1,0:T(8,128)} %bitcast.89, f32[16,224,128]{2,1,0:T(8,128)} %copy-done.8, f32[16,7296]{1,0:T(8,128)} %pad_maximum_fusion.refs_5_.refs_13_, ...), custom_call_target="tpu_custom_call" | custom-call | flops 4587520 | bytes 14680064 | tf_op jit(solution)/shard_map/final/pallas_call | solution.py:112
  (44 shorter events, 0.5 us)
Async XLA Ops:
  3.8 6.8 %collective-permute-start.1 = (f32[4,8,7168]{2,1,0:T(8,128)}, f32[4,8,7168]{2,1,0:T(8,128)S(1)}, u32[]{:S(2)}, u32[]{:S(2)}) collective-permute-start(f32[4,8,7168]{2,1,0:T(8,128)} %get-tuple-element.11), channel_id=1, source_target_pairs={{0,8},{8,0},{1,9},{9,1},{2,10},{10,2},{3,11},{11,3},{4,12},{12,4},... | collective-permute-start | bytes 2752520 | tf_op jit(solution)/shard_map/ppermute | solution.py:28
  7.0 3.6 %collective-permute-start = (f32[4,8,7168]{2,1,0:T(8,128)S(1)}, f32[4,8,7168]{2,1,0:T(8,128)S(1)}, u32[]{:S(2)}, u32[]{:S(2)}) collective-permute-start(f32[4,8,7168]{2,1,0:T(8,128)S(1)} %get-tuple-element.12), channel_id=1, source_target_pairs={{0,8},{8,0},{1,9},{9,1},{2,10},{10,2},{3,11},{11,3},{4,12},{12,4},... | collective-permute-start | bytes 2752520 | tf_op jit(solution)/shard_map/ppermute | solution.py:28
  7.0 8.8 %copy-start.9 = (f32[128,1,224]{0,2,1:T(8,128)S(1)}, f32[128,1,224]{0,2,1:T(8,128)}, u32[]{:S(2)}) copy-start(f32[128,1,224]{0,2,1:T(8,128)} %param.5) | copy-start | bytes 344068
  12.5 22.9 %collective-permute-start.2 = (f32[2,8,7168]{2,1,0:T(8,128)S(1)}, f32[2,8,7168]{2,1,0:T(8,128)S(1)}, u32[]{:S(2)}, u32[]{:S(2)}) collective-permute-start(f32[2,8,7168]{2,1,0:T(8,128)S(1)} %get-tuple-element.8), channel_id=1, source_target_pairs={{0,192},{64,128},{128,64},{192,0},{1,193},{65,129},{129,65},{193,1... | collective-permute-start | bytes 1376264 | tf_op jit(solution)/shard_map/ppermute | solution.py:28
  13.6 23.2 %collective-permute-start.3 = (f32[2,8,7168]{2,1,0:T(8,128)S(1)}, f32[2,8,7168]{2,1,0:T(8,128)S(1)}, u32[]{:S(2)}, u32[]{:S(2)}) collective-permute-start(f32[2,8,7168]{2,1,0:T(8,128)S(1)} %get-tuple-element.9), channel_id=1, source_target_pairs={{0,128},{64,192},{128,0},{192,64},{1,129},{65,193},{129,1},{193,65... | collective-permute-start | bytes 1376264 | tf_op jit(solution)/shard_map/ppermute | solution.py:28
  13.9 22.8 %collective-permute-start.4 = (f32[2,8,7168]{2,1,0:T(8,128)S(1)}, f32[2,8,7168]{2,1,0:T(8,128)}, u32[]{:S(2)}, u32[]{:S(2)}) collective-permute-start(f32[2,8,7168]{2,1,0:T(8,128)S(1)} %get-tuple-element.10), channel_id=1, source_target_pairs={{0,64},{64,0},{128,192},{192,128},{1,65},{65,1},{129,193},{193,129... | collective-permute-start | bytes 1376264 | tf_op jit(solution)/shard_map/ppermute | solution.py:28
  15.9 35.1 %collective-permute-start.7 = (f32[224,128]{1,0:T(8,128)S(1)}, f32[224,128]{1,0:T(8,128)S(1)}, u32[]{:S(2)}, u32[]{:S(2)}) collective-permute-start(f32[224,128]{1,0:T(8,128)S(1)} %bitcast.110), channel_id=1, source_target_pairs={{0,32},{16,48},{32,0},{48,16},{1,33},{17,49},{33,1},{49,17},{2,34}... | collective-permute-start | bytes 344072 | tf_op jit(solution)/shard_map/ppermute | solution.py:28
  21.2 29.7 %collective-permute-start.6 = (f32[224,128]{1,0:T(8,128)S(1)}, f32[224,128]{1,0:T(8,128)S(1)}, u32[]{:S(2)}, u32[]{:S(2)}) collective-permute-start(f32[224,128]{1,0:T(8,128)S(1)} %bitcast.111), channel_id=1, source_target_pairs={{0,48},{16,32},{32,16},{48,0},{1,49},{17,33},{33,17},{49,1},{2,50}... | collective-permute-start | bytes 344072 | tf_op jit(solution)/shard_map/ppermute | solution.py:28
  35.4 8.4 %collective-permute-start.5 = (f32[224,128]{1,0:T(8,128)S(1)}, f32[224,128]{1,0:T(8,128)S(1)}, u32[]{:S(2)}, u32[]{:S(2)}) collective-permute-start(f32[224,128]{1,0:T(8,128)S(1)} %bitcast.112), channel_id=1, source_target_pairs={{0,16},{16,0},{32,48},{48,32},{1,17},{17,1},{33,49},{49,33},{2,18}... | collective-permute-start | bytes 344072 | tf_op jit(solution)/shard_map/ppermute | solution.py:28
  38.3 16.0 %collective-permute-start.8 = (f32[1,8,3584]{2,1,0:T(8,128)S(1)}, f32[1,8,3584]{2,1,0:T(8,128)S(1)}, u32[]{:S(2)}, u32[]{:S(2)}) collective-permute-start(f32[1,8,3584]{2,1,0:T(8,128)S(1)} %get-tuple-element.15), channel_id=1, source_target_pairs={{0,16},{16,0},{32,48},{48,32},{1,17},{17,1},{33,49},{49,33},{2,18}... | collective-permute-start | bytes 344072 | tf_op jit(solution)/shard_map/ppermute | solution.py:28
  39.3 14.9 %collective-permute-start.9 = (f32[1,8,3584]{2,1,0:T(8,128)S(1)}, f32[1,8,3584]{2,1,0:T(8,128)S(1)}, u32[]{:S(2)}, u32[]{:S(2)}) collective-permute-start(f32[1,8,3584]{2,1,0:T(8,128)S(1)} %get-tuple-element.17), channel_id=1, source_target_pairs={{0,48},{16,32},{32,16},{48,0},{1,49},{17,33},{33,17},{49,1},{2,50}... | collective-permute-start | bytes 344072 | tf_op jit(solution)/shard_map/ppermute | solution.py:28
  43.8 10.4 %collective-permute-start.10 = (f32[1,8,3584]{2,1,0:T(8,128)S(1)}, f32[1,8,3584]{2,1,0:T(8,128)S(1)}, u32[]{:S(2)}, u32[]{:S(2)}) collective-permute-start(f32[1,8,3584]{2,1,0:T(8,128)S(1)} %get-tuple-element.16), channel_id=1, source_target_pairs={{0,32},{16,48},{32,0},{48,16},{1,33},{17,49},{33,1},{49,17},{2,34}... | collective-permute-start | bytes 344072 | tf_op jit(solution)/shard_map/ppermute | solution.py:28
  51.0 29.6 %collective-permute-start.15 = (f32[4,28,8,128]{3,2,1,0:T(8,128)S(1)}, f32[4,28,8,128]{3,2,1,0:T(8,128)S(1)}, u32[]{:S(2)}, u32[]{:S(2)}) collective-permute-start(f32[4,28,8,128]{3,2,1,0:T(8,128)S(1)} %bitcast.82), channel_id=1, source_target_pairs={{0,192},{64,128},{128,64},{192,0},{1,193},{65,129},{129,65},{193,1... | collective-permute-start | bytes 1376264 | tf_op jit(solution)/shard_map/ppermute | solution.py:28
  54.2 26.4 %collective-permute-start.14 = (f32[4,28,8,128]{3,2,1,0:T(8,128)S(1)}, f32[4,28,8,128]{3,2,1,0:T(8,128)S(1)}, u32[]{:S(2)}, u32[]{:S(2)}) collective-permute-start(f32[4,28,8,128]{3,2,1,0:T(8,128)S(1)} %bitcast.83), channel_id=1, source_target_pairs={{0,64},{64,0},{128,192},{192,128},{1,65},{65,1},{129,193},{193,129... | collective-permute-start | bytes 1376264 | tf_op jit(solution)/shard_map/ppermute | solution.py:28
  55.0 19.4 %all-to-all-start = ((f32[32,1,128]{2,1,0:T(1,128)}), f32[32,1,128]{2,1,0:T(1,128)S(1)}, u32[]{:S(2)}, u32[]{:S(2)}) async-start(f32[32,1,128]{2,1,0:T(1,128)} %broadcast_in_dim.54), calls=%async_computation | async-start | bytes 32768 | tf_op jit(solution)/shard_map/all_to_all | solution.py:190
  65.8 8.6 %collective-permute-start.11 = (f32[1,8,3584]{2,1,0:T(8,128)S(1)}, f32[1,8,3584]{2,1,0:T(8,128)S(1)}, u32[]{:S(2)}, u32[]{:S(2)}) collective-permute-start(f32[1,8,3584]{2,1,0:T(8,128)S(1)} %get-tuple-element.7), channel_id=1, source_target_pairs={{0,16},{16,0},{32,48},{48,32},{1,17},{17,1},{33,49},{49,33},{2,18}... | collective-permute-start | bytes 344072 | tf_op jit(solution)/shard_map/ppermute | solution.py:28
  68.0 7.9 %collective-permute-start.13 = (f32[1,8,3584]{2,1,0:T(8,128)S(1)}, f32[1,8,3584]{2,1,0:T(8,128)S(1)}, u32[]{:S(2)}, u32[]{:S(2)}) collective-permute-start(f32[1,8,3584]{2,1,0:T(8,128)S(1)} %get-tuple-element.7), channel_id=1, source_target_pairs={{0,48},{16,32},{32,16},{48,0},{1,49},{17,33},{33,17},{49,1},{2,50}... | collective-permute-start | bytes 344072 | tf_op jit(solution)/shard_map/ppermute | solution.py:28
  71.3 9.0 %collective-permute-start.12 = (f32[1,8,3584]{2,1,0:T(8,128)S(1)}, f32[1,8,3584]{2,1,0:T(8,128)S(1)}, u32[]{:S(2)}, u32[]{:S(2)}) collective-permute-start(f32[1,8,3584]{2,1,0:T(8,128)S(1)} %get-tuple-element.7), channel_id=1, source_target_pairs={{0,32},{16,48},{32,0},{48,16},{1,33},{17,49},{33,1},{49,17},{2,34}... | collective-permute-start | bytes 344072 | tf_op jit(solution)/shard_map/ppermute | solution.py:28
  74.4 9.8 %collective-permute-start.16 = (f32[4,28,8,128]{3,2,1,0:T(8,128)S(1)}, f32[4,28,8,128]{3,2,1,0:T(8,128)S(1)}, u32[]{:S(2)}, u32[]{:S(2)}) collective-permute-start(f32[4,28,8,128]{3,2,1,0:T(8,128)S(1)} %bitcast.84), channel_id=1, source_target_pairs={{0,128},{64,192},{128,0},{192,64},{1,129},{65,193},{129,1},{193,65... | collective-permute-start | bytes 1376264 | tf_op jit(solution)/shard_map/ppermute | solution.py:28
  80.7 14.4 %collective-permute-start.20 = (f32[2,8,7296]{2,1,0:T(8,128)S(1)}, f32[2,8,7296]{2,1,0:T(8,128)S(1)}, u32[]{:S(2)}, u32[]{:S(2)}) collective-permute-start(f32[2,8,7296]{2,1,0:T(8,128)S(1)} %pad_maximum_fusion.1), channel_id=1, source_target_pairs={{0,128},{64,192},{128,0},{192,64},{1,129},{65,193},{129,1},{193,65... | collective-permute-start | bytes 1400840 | tf_op jit(solution)/shard_map/ppermute | solution.py:28
  82.1 26.3 %collective-permute-start.19 = (f32[2,8,7296]{2,1,0:T(8,128)S(1)}, f32[2,8,7296]{2,1,0:T(8,128)S(1)}, u32[]{:S(2)}, u32[]{:S(2)}) collective-permute-start(f32[2,8,7296]{2,1,0:T(8,128)S(1)} %pad_maximum_fusion.1), channel_id=1, source_target_pairs={{0,192},{64,128},{128,64},{192,0},{1,193},{65,129},{129,65},{193,1... | collective-permute-start | bytes 1400840 | tf_op jit(solution)/shard_map/ppermute | solution.py:28
  82.9 26.1 %collective-permute-start.18 = (f32[2,8,7296]{2,1,0:T(8,128)S(1)}, f32[2,8,7296]{2,1,0:T(8,128)S(1)}, u32[]{:S(2)}, u32[]{:S(2)}) collective-permute-start(f32[2,8,7296]{2,1,0:T(8,128)S(1)} %pad_maximum_fusion.1), channel_id=1, source_target_pairs={{0,64},{64,0},{128,192},{192,128},{1,65},{65,1},{129,193},{193,129... | collective-permute-start | bytes 1400840 | tf_op jit(solution)/shard_map/ppermute | solution.py:28
  84.2 26.9 %copy-start = (f32[4,4,28,8,128]{4,3,2,1,0:T(8,128)}, f32[4,4,28,8,128]{4,3,2,1,0:T(8,128)S(1)}, u32[]{:S(2)}) copy-start(f32[4,4,28,8,128]{4,3,2,1,0:T(8,128)S(1)} %bitcast_dynamic-update-slice_fusion) | copy-start | bytes 5505028
  84.2 26.8 %collective-permute-start.17 = (f32[16,224,128]{2,1,0:T(8,128)S(1)}, f32[16,224,128]{2,1,0:T(8,128)S(1)}, u32[]{:S(2)}, u32[]{:S(2)}) collective-permute-start(f32[16,224,128]{2,1,0:T(8,128)S(1)} %bitcast.88), channel_id=1, source_target_pairs={{0,8},{8,0},{1,9},{9,1},{2,10},{10,2},{3,11},{11,3},{4,12},{12,4},... | collective-permute-start | bytes 5505032 | tf_op jit(solution)/shard_map/ppermute | solution.py:28
  92.6 17.2 %collective-permute-start.21 = (f32[2,8,7296]{2,1,0:T(8,128)S(1)}, f32[2,8,7296]{2,1,0:T(8,128)S(1)}, u32[]{:S(2)}, u32[]{:S(2)}) collective-permute-start(f32[2,8,7296]{2,1,0:T(8,128)S(1)} %pad_maximum_fusion.1), channel_id=1, source_target_pairs={{0,8},{8,0},{1,9},{9,1},{2,10},{10,2},{3,11},{11,3},{4,12},{12,4},... | collective-permute-start | bytes 1400840 | tf_op jit(solution)/shard_map/ppermute | solution.py:28
  95.1 15.9 %copy-start.1 = (f32[2,8,7296]{2,1,0:T(8,128)}, f32[2,8,7296]{2,1,0:T(8,128)S(1)}, u32[]{:S(2)}) copy-start(f32[2,8,7296]{2,1,0:T(8,128)S(1)} %collective-permute-done.20) | copy-start | bytes 1400836
  95.1 14.7 %collective-permute-start.24 = (f32[2,8,7296]{2,1,0:T(8,128)S(1)}, f32[2,8,7296]{2,1,0:T(8,128)S(1)}, u32[]{:S(2)}, u32[]{:S(2)}) collective-permute-start(f32[2,8,7296]{2,1,0:T(8,128)S(1)} %collective-permute-done.20), channel_id=1, source_target_pairs={{0,8},{8,0},{1,9},{9,1},{2,10},{10,2},{3,11},{11,3},{4,12},{12,4},... | collective-permute-start | bytes 1400840 | tf_op jit(solution)/shard_map/ppermute | solution.py:28
  108.4 2.6 %copy-start.2 = (f32[2,8,7296]{2,1,0:T(8,128)}, f32[2,8,7296]{2,1,0:T(8,128)S(1)}, u32[]{:S(2)}) copy-start(f32[2,8,7296]{2,1,0:T(8,128)S(1)} %collective-permute-done.19) | copy-start | bytes 1400836
  108.4 1.9 %collective-permute-start.23 = (f32[2,8,7296]{2,1,0:T(8,128)S(1)}, f32[2,8,7296]{2,1,0:T(8,128)S(1)}, u32[]{:S(2)}, u32[]{:S(2)}) collective-permute-start(f32[2,8,7296]{2,1,0:T(8,128)S(1)} %collective-permute-done.19), channel_id=1, source_target_pairs={{0,8},{8,0},{1,9},{9,1},{2,10},{10,2},{3,11},{11,3},{4,12},{12,4},... | collective-permute-start | bytes 1400840 | tf_op jit(solution)/shard_map/ppermute | solution.py:28
  108.9 2.2 %copy-start.3 = (f32[2,8,7296]{2,1,0:T(8,128)}, f32[2,8,7296]{2,1,0:T(8,128)S(1)}, u32[]{:S(2)}) copy-start(f32[2,8,7296]{2,1,0:T(8,128)S(1)} %collective-permute-done.18) | copy-start | bytes 1400836
  108.9 2.1 %collective-permute-start.22 = (f32[2,8,7296]{2,1,0:T(8,128)S(1)}, f32[2,8,7296]{2,1,0:T(8,128)S(1)}, u32[]{:S(2)}, u32[]{:S(2)}) collective-permute-start(f32[2,8,7296]{2,1,0:T(8,128)S(1)} %collective-permute-done.18), channel_id=1, source_target_pairs={{0,8},{8,0},{1,9},{9,1},{2,10},{10,2},{3,11},{11,3},{4,12},{12,4},... | collective-permute-start | bytes 1400840 | tf_op jit(solution)/shard_map/ppermute | solution.py:28
  109.9 1.2 %copy-start.4 = (f32[2,8,7296]{2,1,0:T(8,128)}, f32[2,8,7296]{2,1,0:T(8,128)S(1)}, u32[]{:S(2)}) copy-start(f32[2,8,7296]{2,1,0:T(8,128)S(1)} %collective-permute-done.21) | copy-start | bytes 1400836
  109.9 1.2 %copy-start.5 = (f32[2,8,7296]{2,1,0:T(8,128)}, f32[2,8,7296]{2,1,0:T(8,128)S(1)}, u32[]{:S(2)}) copy-start(f32[2,8,7296]{2,1,0:T(8,128)S(1)} %collective-permute-done.24) | copy-start | bytes 1400836
  110.4 0.8 copy-start.6
  111.1 0.8 copy-start.7
  111.1 1.4 %copy-start.8 = (f32[16,224,128]{2,1,0:T(8,128)}, f32[16,224,128]{2,1,0:T(8,128)S(1)}, u32[]{:S(2)}) copy-start(f32[16,224,128]{2,1,0:T(8,128)S(1)} %collective-permute-done.17.refs_4_) | copy-start | bytes 5505028

commit v5 on v4

--- a/solution.py
+++ b/solution.py
@@ -70,10 +70,10 @@
     pieces, sums, (out_ref, moment_ref, grad) = refs[:8], refs[8:16], refs[16:]
     step = pl.program_id(0)
     high = pieces[0].shape[0]
-    row = sums[0][0:1, :]
-    for part in sums[1:]:
-        row = row + part[0:1, :]
-    scaling = ceiling / jnp.maximum(jnp.sqrt(jnp.sum(row, axis=1, keepdims=True)), ceiling)
+    rows = [part[0:1, :] for part in sums]
+    while len(rows) > 1:
+        rows = [a + b for a, b in zip(rows[::2], rows[1::2])]
+    scaling = ceiling / jnp.maximum(jnp.sqrt(jnp.sum(rows[0], axis=1, keepdims=True)), ceiling)
     factor = (outer_rate * (1.0 + momentum_decay)) * scaling
     swapped = place_ref[8] != 0
     parts = []

time: 121 us -> 121 us (level)
  no operation moved by 1% of the time
where the time goes in v5:
time: 121 us; the launch traced here: 120 us
  starting transfers between devices  66.1 us (55%)
  waiting for transfers between devices  34.7 us (29%)
  Pallas kernels  7.83 us (6%)
  other arithmetic  7.81 us (6%)
  local copies, waits for them, and re-layouts  2.86 us (2%)
    ppermute x25, starting transfers between devices, swap(): lax.ppermute(x, axes, [(i, i ^ mask) for i in range(math.prod(sizes))])  55.3 us
    ppermute x25, waiting for transfers between devices, swap(): lax.ppermute(x, axes, [(i, i ^ mask) for i in range(math.prod(sizes))])  31.8 us
    all_to_all x1, starting transfers between devices, add_squares(): lax.all_to_all(jnp.broadcast_to(row, (n,) + row.shape), axes, 0, 0)  10.8 us
    pallas_call x1, Pallas kernels, final(): pl.pallas_call(lambda *refs: final_kernel(ceiling, *refs), out_shape=(jax...  7.77 us
    sub x1, other arithmetic, drift(): return rows_at(a_rows, start, count) - rows_at(l_rows, start, count)  3.12 us
    all_to_all x1, waiting for transfers between devices, add_squares(): lax.all_to_all(jnp.broadcast_to(row, (n,) + row.shape), axes, 0, 0)  2.83 us
  transfers between devices with their start and end apart: 26, of which 9 were waited for; matrix products, arithmetic and copies ran while one was open for 4% of the time, Pallas kernels for 0%

profile of v5, /device:TPU:1, one launch (start us, length us, event | category | flops | bytes accessed | tf_op | source)
XLA Modules:
  0.0 120.4 jit_solution(15764637282173201947)
XLA Ops:
  0.6 3.1 %dynamic-slice_subtract_fusion = (f32[4,8,7168]{2,1,0:T(8,128)}, f32[4,8,7168]{2,1,0:T(8,128)S(1)}) fusion(f32[16,8,7168]{2,1,0:T(8,128)} %bitcast.90, s32[]{:T(128)S(6)} %select_n.154, f32[16,8,7168]{2,1,0:T(8,128)} %bitcast.85, s32[]{:T(128)S(6)} %select_n.151), kind=kLoop, calls=%fused_computation | loop fusion | flops 458752 | bytes 5505032 | tf_op jit(solution)/shard_map/sub | solution.py:146
  3.8 3.2 %collective-permute-start.1 = (f32[4,8,7168]{2,1,0:T(8,128)}, f32[4,8,7168]{2,1,0:T(8,128)S(1)}, u32[]{:S(2)}, u32[]{:S(2)}) collective-permute-start(f32[4,8,7168]{2,1,0:T(8,128)} %get-tuple-element.11), channel_id=1, source_target_pairs={{0,8},{8,0},{1,9},{9,1},{2,10},{10,2},{3,11},{11,3},{4,12},{12,4},... | collective-permute-start | bytes 2752520 | tf_op jit(solution)/shard_map/ppermute | solution.py:28
  7.0 0.0 collective-permute-start
  7.0 3.6 %collective-permute-done.1 = f32[4,8,7168]{2,1,0:T(8,128)S(1)} collective-permute-done((f32[4,8,7168]{2,1,0:T(8,128)}, f32[4,8,7168]{2,1,0:T(8,128)S(1)}, u32[]{:S(2)}, u32[]{:S(2)}) %collective-permute-start.1) | collective-permute-done | bytes 917536 | tf_op jit(solution)/shard_map/ppermute | solution.py:28
  10.6 0.0 collective-permute-done
  10.6 1.9 %dynamic-slice_add_fusion.2 = (f32[2,8,7168]{2,1,0:T(8,128)S(1)}, f32[2,8,7168]{2,1,0:T(8,128)S(1)}, f32[2,8,7168]{2,1,0:T(8,128)S(1)}) fusion(f32[4,8,7168]{2,1,0:T(8,128)S(1)} %collective-permute-done.1, s32[]{:T(128)S(6)} %select_n.155, f32[16,8,7168]{2,1,0:T(8,128)} %bitcast.91, s32[]{:T(128)S(6)} %select_n.153, f32[16,8,7168]{2,1,0:T(8,128)} %bitcast.86, ...), kind=kLoop, calls=%fused_computation.12 | loop fusion | flops 688128 | bytes 5505048 | tf_op jit(solution)/shard_map/add | solution.py:155
  12.5 1.1 collective-permute-start.2
  13.6 0.3 collective-permute-start.3
  13.9 1.9 %collective-permute-start.4 = (f32[2,8,7168]{2,1,0:T(8,128)S(1)}, f32[2,8,7168]{2,1,0:T(8,128)}, u32[]{:S(2)}, u32[]{:S(2)}) collective-permute-start(f32[2,8,7168]{2,1,0:T(8,128)S(1)} %get-tuple-element.10), channel_id=1, source_target_pairs={{0,64},{64,0},{128,192},{192,128},{1,65},{65,1},{129,193},{193,129... | collective-permute-start | bytes 1376264 | tf_op jit(solution)/shard_map/ppermute | solution.py:28
  15.9 5.3 %collective-permute-start.7 = (f32[224,128]{1,0:T(8,128)S(1)}, f32[224,128]{1,0:T(8,128)S(1)}, u32[]{:S(2)}, u32[]{:S(2)}) collective-permute-start(f32[224,128]{1,0:T(8,128)S(1)} %bitcast.110), channel_id=1, source_target_pairs={{0,32},{16,48},{32,0},{48,16},{1,33},{17,49},{33,1},{49,17},{2,34}... | collective-permute-start | bytes 344072 | tf_op jit(solution)/shard_map/ppermute | solution.py:28
  21.2 0.0 collective-permute-start.6
  21.2 0.7 stack.47.refs_0_
  21.9 13.5 %collective-permute-done.2 = f32[2,8,7168]{2,1,0:T(8,128)S(1)} collective-permute-done((f32[2,8,7168]{2,1,0:T(8,128)S(1)}, f32[2,8,7168]{2,1,0:T(8,128)S(1)}, u32[]{:S(2)}, u32[]{:S(2)}) %collective-permute-start.2) | collective-permute-done | bytes 458784 | tf_op jit(solution)/shard_map/ppermute | solution.py:28
  35.4 1.4 %collective-permute-start.5 = (f32[224,128]{1,0:T(8,128)S(1)}, f32[224,128]{1,0:T(8,128)S(1)}, u32[]{:S(2)}, u32[]{:S(2)}) collective-permute-start(f32[224,128]{1,0:T(8,128)S(1)} %bitcast.112), channel_id=1, source_target_pairs={{0,16},{16,0},{32,48},{48,32},{1,17},{17,1},{33,49},{49,33},{2,18}... | collective-permute-start | bytes 344072 | tf_op jit(solution)/shard_map/ppermute | solution.py:28
  36.8 0.0 collective-permute-done.3
  36.8 0.0 collective-permute-done.4
  36.8 1.4 %add_add_fusion = f32[2,8,7168]{2,1,0:T(8,128)S(1)} fusion(f32[2,8,7168]{2,1,0:T(8,128)} %collective-permute-done.4, f32[2,8,7168]{2,1,0:T(8,128)S(1)} %collective-permute-done.3, f32[2,8,7168]{2,1,0:T(8,128)S(1)} %collective-permute-done.2, f32[4,8,7168]{2,1,0:T(8,128)S(1)} %collective-permute-done, s32[]{:T(128)S(6)} %select_n.152, ...), kind=kLoop, calls=%fused_computation.10 | loop fusion | flops 573440 | bytes 3211272 | tf_op jit(solution)/shard_map/add | solution.py:165
  38.2 0.1 dynamic-slice_select_fusion.2
  38.3 1.1 collective-permute-start.8
  39.3 4.4 %collective-permute-start.9 = (f32[1,8,3584]{2,1,0:T(8,128)S(1)}, f32[1,8,3584]{2,1,0:T(8,128)S(1)}, u32[]{:S(2)}, u32[]{:S(2)}) collective-permute-start(f32[1,8,3584]{2,1,0:T(8,128)S(1)} %get-tuple-element.17), channel_id=1, source_target_pairs={{0,48},{16,32},{32,16},{48,0},{1,49},{17,33},{33,17},{49,1},{2,50}... | collective-permute-start | bytes 344072 | tf_op jit(solution)/shard_map/ppermute | solution.py:28
  43.8 0.0 collective-permute-done.5
  43.8 7.1 %collective-permute-start.10 = (f32[1,8,3584]{2,1,0:T(8,128)S(1)}, f32[1,8,3584]{2,1,0:T(8,128)S(1)}, u32[]{:S(2)}, u32[]{:S(2)}) collective-permute-start(f32[1,8,3584]{2,1,0:T(8,128)S(1)} %get-tuple-element.16), channel_id=1, source_target_pairs={{0,32},{16,48},{32,0},{48,16},{1,33},{17,49},{33,1},{49,17},{2,34}... | collective-permute-start | bytes 344072 | tf_op jit(solution)/shard_map/ppermute | solution.py:28
  50.9 0.0 collective-permute-done.6
  50.9 0.0 collective-permute-done.7
  51.0 3.2 %collective-permute-start.15 = (f32[4,28,8,128]{3,2,1,0:T(8,128)S(1)}, f32[4,28,8,128]{3,2,1,0:T(8,128)S(1)}, u32[]{:S(2)}, u32[]{:S(2)}) collective-permute-start(f32[4,28,8,128]{3,2,1,0:T(8,128)S(1)} %bitcast.82), channel_id=1, source_target_pairs={{0,192},{64,128},{128,64},{192,0},{1,193},{65,129},{129,65},{193,1... | collective-permute-start | bytes 1376264 | tf_op jit(solution)/shard_map/ppermute | solution.py:28
  54.2 0.0 collective-permute-start.14
  54.2 0.0 collective-permute-done.8
  54.2 0.0 collective-permute-done.9
  54.2 0.0 collective-permute-done.10
  54.2 0.1 multiply_reduce_fusion
  54.4 0.6 broadcast_in_dim.54
  55.0 10.8 %all-to-all-start = ((f32[32,1,128]{2,1,0:T(1,128)}), f32[32,1,128]{2,1,0:T(1,128)S(1)}, u32[]{:S(2)}, u32[]{:S(2)}) async-start(f32[32,1,128]{2,1,0:T(1,128)} %broadcast_in_dim.54), calls=%async_computation | async-start | bytes 32768 | tf_op jit(solution)/shard_map/all_to_all | solution.py:190
  65.8 2.2 %collective-permute-start.11 = (f32[1,8,3584]{2,1,0:T(8,128)S(1)}, f32[1,8,3584]{2,1,0:T(8,128)S(1)}, u32[]{:S(2)}, u32[]{:S(2)}) collective-permute-start(f32[1,8,3584]{2,1,0:T(8,128)S(1)} %get-tuple-element.7), channel_id=1, source_target_pairs={{0,16},{16,0},{32,48},{48,32},{1,17},{17,1},{33,49},{49,33},{2,18}... | collective-permute-start | bytes 344072 | tf_op jit(solution)/shard_map/ppermute | solution.py:28
  68.0 3.3 %collective-permute-start.13 = (f32[1,8,3584]{2,1,0:T(8,128)S(1)}, f32[1,8,3584]{2,1,0:T(8,128)S(1)}, u32[]{:S(2)}, u32[]{:S(2)}) collective-permute-start(f32[1,8,3584]{2,1,0:T(8,128)S(1)} %get-tuple-element.7), channel_id=1, source_target_pairs={{0,48},{16,32},{32,16},{48,0},{1,49},{17,33},{33,17},{49,1},{2,50}... | collective-permute-start | bytes 344072 | tf_op jit(solution)/shard_map/ppermute | solution.py:28
  71.3 0.2 collective-permute-start.12
  71.5 2.8 %all-to-all-done = f32[32,1,128]{2,1,0:T(1,128)S(1)} async-done(((f32[32,1,128]{2,1,0:T(1,128)}), f32[32,1,128]{2,1,0:T(1,128)S(1)}, u32[]{:S(2)}, u32[]{:S(2)}) %all-to-all-start) | async-done | bytes 16416 | tf_op jit(solution)/shard_map/all_to_all | solution.py:190
  74.4 0.0 collective-permute-done.11
  74.4 1.4 %collective-permute-start.16 = (f32[4,28,8,128]{3,2,1,0:T(8,128)S(1)}, f32[4,28,8,128]{3,2,1,0:T(8,128)S(1)}, u32[]{:S(2)}, u32[]{:S(2)}) collective-permute-start(f32[4,28,8,128]{3,2,1,0:T(8,128)S(1)} %bitcast.84), channel_id=1, source_target_pairs={{0,128},{64,192},{128,0},{192,64},{1,129},{65,193},{129,1},{193,65... | collective-permute-start | bytes 1376264 | tf_op jit(solution)/shard_map/ppermute | solution.py:28
  75.9 0.0 collective-permute-done.13
  75.9 4.5 %collective-permute-done.12 = f32[1,8,3584]{2,1,0:T(8,128)S(1)} collective-permute-done((f32[1,8,3584]{2,1,0:T(8,128)S(1)}, f32[1,8,3584]{2,1,0:T(8,128)S(1)}, u32[]{:S(2)}, u32[]{:S(2)}) %collective-permute-start.12) | collective-permute-done | bytes 114720 | tf_op jit(solution)/shard_map/ppermute | solution.py:28
  80.4 0.2 broadcast_in_dim.48
  80.6 0.0 collective-permute-done.15
  80.7 0.0 collective-permute-done.14
  80.7 1.4 %collective-permute-start.20 = (f32[2,8,7296]{2,1,0:T(8,128)S(1)}, f32[2,8,7296]{2,1,0:T(8,128)S(1)}, u32[]{:S(2)}, u32[]{:S(2)}) collective-permute-start(f32[2,8,7296]{2,1,0:T(8,128)S(1)} %pad_maximum_fusion.1), channel_id=1, source_target_pairs={{0,128},{64,192},{128,0},{192,64},{1,129},{65,193},{129,1},{193,65... | collective-permute-start | bytes 1400840 | tf_op jit(solution)/shard_map/ppermute | solution.py:28
  82.1 0.8 collective-permute-start.19
  82.9 0.6 collective-permute-start.18
  83.6 0.6 collective-permute-done.16
  84.2 8.4 %collective-permute-start.17 = (f32[16,224,128]{2,1,0:T(8,128)S(1)}, f32[16,224,128]{2,1,0:T(8,128)S(1)}, u32[]{:S(2)}, u32[]{:S(2)}) collective-permute-start(f32[16,224,128]{2,1,0:T(8,128)S(1)} %bitcast.88), channel_id=1, source_target_pairs={{0,8},{8,0},{1,9},{9,1},{2,10},{10,2},{3,11},{11,3},{4,12},{12,4},... | collective-permute-start | bytes 5505032 | tf_op jit(solution)/shard_map/ppermute | solution.py:28
  92.6 0.1 collective-permute-start.21
  92.7 2.4 %collective-permute-done.20 = f32[2,8,7296]{2,1,0:T(8,128)S(1)} collective-permute-done((f32[2,8,7296]{2,1,0:T(8,128)S(1)}, f32[2,8,7296]{2,1,0:T(8,128)S(1)}, u32[]{:S(2)}, u32[]{:S(2)}) %collective-permute-start.20) | collective-permute-done | bytes 466976 | tf_op jit(solution)/shard_map/ppermute | solution.py:28
  95.1 7.3 %collective-permute-start.24 = (f32[2,8,7296]{2,1,0:T(8,128)S(1)}, f32[2,8,7296]{2,1,0:T(8,128)S(1)}, u32[]{:S(2)}, u32[]{:S(2)}) collective-permute-start(f32[2,8,7296]{2,1,0:T(8,128)S(1)} %collective-permute-done.20), channel_id=1, source_target_pairs={{0,8},{8,0},{1,9},{9,1},{2,10},{10,2},{3,11},{11,3},{4,12},{12,4},... | collective-permute-start | bytes 1400840 | tf_op jit(solution)/shard_map/ppermute | solution.py:28
  102.4 6.0 %collective-permute-done.19 = f32[2,8,7296]{2,1,0:T(8,128)S(1)} collective-permute-done((f32[2,8,7296]{2,1,0:T(8,128)S(1)}, f32[2,8,7296]{2,1,0:T(8,128)S(1)}, u32[]{:S(2)}, u32[]{:S(2)}) %collective-permute-start.19) | collective-permute-done | bytes 466976 | tf_op jit(solution)/shard_map/ppermute | solution.py:28
  108.4 0.5 collective-permute-start.23
  108.9 0.0 collective-permute-done.18
  108.9 0.1 collective-permute-start.22
  109.0 0.8 pad_maximum_fusion.refs_5_.refs_13_
  109.9 0.0 collective-permute-done.21
  109.9 0.5 collective-permute-done.23
  110.4 0.7 collective-permute-done.22
  111.1 0.0 collective-permute-done.17.refs_4_
  111.1 0.1 copy-done.6
  111.2 0.7 copy-done.7
  111.8 0.6 copy-done.8
  112.4 7.8 %final.1 = (f32[128,7168]{1,0:T(8,128)}, f32[224,128]{1,0:T(8,128)}) custom-call(s32[11]{0:T(128)} %stack.47.refs_0_, f32[128,7168]{1,0:T(8,128)} %refs_1_.1, f32[224,128]{1,0:T(8,128)} %bitcast.109, f32[16,224,128]{2,1,0:T(8,128)} %bitcast.89, f32[16,224,128]{2,1,0:T(8,128)} %copy-done.8, f32[16,7296]{1,0:T(8,128)} %pad_maximum_fusion.refs_5_.refs_13_, ...), custom_call_target="tpu_custom_call" | custom-call | flops 4587520 | bytes 14680064 | tf_op jit(solution)/shard_map/final/pallas_call | solution.py:112
  (44 shorter events, 0.5 us)
Async XLA Ops:
  3.8 6.8 %collective-permute-start.1 = (f32[4,8,7168]{2,1,0:T(8,128)}, f32[4,8,7168]{2,1,0:T(8,128)S(1)}, u32[]{:S(2)}, u32[]{:S(2)}) collective-permute-start(f32[4,8,7168]{2,1,0:T(8,128)} %get-tuple-element.11), channel_id=1, source_target_pairs={{0,8},{8,0},{1,9},{9,1},{2,10},{10,2},{3,11},{11,3},{4,12},{12,4},... | collective-permute-start | bytes 2752520 | tf_op jit(solution)/shard_map/ppermute | solution.py:28
  7.0 3.6 %collective-permute-start = (f32[4,8,7168]{2,1,0:T(8,128)S(1)}, f32[4,8,7168]{2,1,0:T(8,128)S(1)}, u32[]{:S(2)}, u32[]{:S(2)}) collective-permute-start(f32[4,8,7168]{2,1,0:T(8,128)S(1)} %get-tuple-element.12), channel_id=1, source_target_pairs={{0,8},{8,0},{1,9},{9,1},{2,10},{10,2},{3,11},{11,3},{4,12},{12,4},... | collective-permute-start | bytes 2752520 | tf_op jit(solution)/shard_map/ppermute | solution.py:28
  7.0 8.8 %copy-start.9 = (f32[128,1,224]{0,2,1:T(8,128)S(1)}, f32[128,1,224]{0,2,1:T(8,128)}, u32[]{:S(2)}) copy-start(f32[128,1,224]{0,2,1:T(8,128)} %param.5) | copy-start | bytes 344068
  12.5 22.9 %collective-permute-start.2 = (f32[2,8,7168]{2,1,0:T(8,128)S(1)}, f32[2,8,7168]{2,1,0:T(8,128)S(1)}, u32[]{:S(2)}, u32[]{:S(2)}) collective-permute-start(f32[2,8,7168]{2,1,0:T(8,128)S(1)} %get-tuple-element.8), channel_id=1, source_target_pairs={{0,192},{64,128},{128,64},{192,0},{1,193},{65,129},{129,65},{193,1... | collective-permute-start | bytes 1376264 | tf_op jit(solution)/shard_map/ppermute | solution.py:28
  13.6 23.2 %collective-permute-start.3 = (f32[2,8,7168]{2,1,0:T(8,128)S(1)}, f32[2,8,7168]{2,1,0:T(8,128)S(1)}, u32[]{:S(2)}, u32[]{:S(2)}) collective-permute-start(f32[2,8,7168]{2,1,0:T(8,128)S(1)} %get-tuple-element.9), channel_id=1, source_target_pairs={{0,128},{64,192},{128,0},{192,64},{1,129},{65,193},{129,1},{193,65... | collective-permute-start | bytes 1376264 | tf_op jit(solution)/shard_map/ppermute | solution.py:28
  13.9 22.8 %collective-permute-start.4 = (f32[2,8,7168]{2,1,0:T(8,128)S(1)}, f32[2,8,7168]{2,1,0:T(8,128)}, u32[]{:S(2)}, u32[]{:S(2)}) collective-permute-start(f32[2,8,7168]{2,1,0:T(8,128)S(1)} %get-tuple-element.10), channel_id=1, source_target_pairs={{0,64},{64,0},{128,192},{192,128},{1,65},{65,1},{129,193},{193,129... | collective-permute-start | bytes 1376264 | tf_op jit(solution)/shard_map/ppermute | solution.py:28
  15.9 35.1 %collective-permute-start.7 = (f32[224,128]{1,0:T(8,128)S(1)}, f32[224,128]{1,0:T(8,128)S(1)}, u32[]{:S(2)}, u32[]{:S(2)}) collective-permute-start(f32[224,128]{1,0:T(8,128)S(1)} %bitcast.110), channel_id=1, source_target_pairs={{0,32},{16,48},{32,0},{48,16},{1,33},{17,49},{33,1},{49,17},{2,34}... | collective-permute-start | bytes 344072 | tf_op jit(solution)/shard_map/ppermute | solution.py:28
  21.2 29.7 %collective-permute-start.6 = (f32[224,128]{1,0:T(8,128)S(1)}, f32[224,128]{1,0:T(8,128)S(1)}, u32[]{:S(2)}, u32[]{:S(2)}) collective-permute-start(f32[224,128]{1,0:T(8,128)S(1)} %bitcast.111), channel_id=1, source_target_pairs={{0,48},{16,32},{32,16},{48,0},{1,49},{17,33},{33,17},{49,1},{2,50}... | collective-permute-start | bytes 344072 | tf_op jit(solution)/shard_map/ppermute | solution.py:28
  35.4 8.4 %collective-permute-start.5 = (f32[224,128]{1,0:T(8,128)S(1)}, f32[224,128]{1,0:T(8,128)S(1)}, u32[]{:S(2)}, u32[]{:S(2)}) collective-permute-start(f32[224,128]{1,0:T(8,128)S(1)} %bitcast.112), channel_id=1, source_target_pairs={{0,16},{16,0},{32,48},{48,32},{1,17},{17,1},{33,49},{49,33},{2,18}... | collective-permute-start | bytes 344072 | tf_op jit(solution)/shard_map/ppermute | solution.py:28
  38.3 16.0 %collective-permute-start.8 = (f32[1,8,3584]{2,1,0:T(8,128)S(1)}, f32[1,8,3584]{2,1,0:T(8,128)S(1)}, u32[]{:S(2)}, u32[]{:S(2)}) collective-permute-start(f32[1,8,3584]{2,1,0:T(8,128)S(1)} %get-tuple-element.15), channel_id=1, source_target_pairs={{0,16},{16,0},{32,48},{48,32},{1,17},{17,1},{33,49},{49,33},{2,18}... | collective-permute-start | bytes 344072 | tf_op jit(solution)/shard_map/ppermute | solution.py:28
  39.3 14.9 %collective-permute-start.9 = (f32[1,8,3584]{2,1,0:T(8,128)S(1)}, f32[1,8,3584]{2,1,0:T(8,128)S(1)}, u32[]{:S(2)}, u32[]{:S(2)}) collective-permute-start(f32[1,8,3584]{2,1,0:T(8,128)S(1)} %get-tuple-element.17), channel_id=1, source_target_pairs={{0,48},{16,32},{32,16},{48,0},{1,49},{17,33},{33,17},{49,1},{2,50}... | collective-permute-start | bytes 344072 | tf_op jit(solution)/shard_map/ppermute | solution.py:28
  43.8 10.4 %collective-permute-start.10 = (f32[1,8,3584]{2,1,0:T(8,128)S(1)}, f32[1,8,3584]{2,1,0:T(8,128)S(1)}, u32[]{:S(2)}, u32[]{:S(2)}) collective-permute-start(f32[1,8,3584]{2,1,0:T(8,128)S(1)} %get-tuple-element.16), channel_id=1, source_target_pairs={{0,32},{16,48},{32,0},{48,16},{1,33},{17,49},{33,1},{49,17},{2,34}... | collective-permute-start | bytes 344072 | tf_op jit(solution)/shard_map/ppermute | solution.py:28
  51.0 29.6 %collective-permute-start.15 = (f32[4,28,8,128]{3,2,1,0:T(8,128)S(1)}, f32[4,28,8,128]{3,2,1,0:T(8,128)S(1)}, u32[]{:S(2)}, u32[]{:S(2)}) collective-permute-start(f32[4,28,8,128]{3,2,1,0:T(8,128)S(1)} %bitcast.82), channel_id=1, source_target_pairs={{0,192},{64,128},{128,64},{192,0},{1,193},{65,129},{129,65},{193,1... | collective-permute-start | bytes 1376264 | tf_op jit(solution)/shard_map/ppermute | solution.py:28
  54.2 26.4 %collective-permute-start.14 = (f32[4,28,8,128]{3,2,1,0:T(8,128)S(1)}, f32[4,28,8,128]{3,2,1,0:T(8,128)S(1)}, u32[]{:S(2)}, u32[]{:S(2)}) collective-permute-start(f32[4,28,8,128]{3,2,1,0:T(8,128)S(1)} %bitcast.83), channel_id=1, source_target_pairs={{0,64},{64,0},{128,192},{192,128},{1,65},{65,1},{129,193},{193,129... | collective-permute-start | bytes 1376264 | tf_op jit(solution)/shard_map/ppermute | solution.py:28
  55.0 19.4 %all-to-all-start = ((f32[32,1,128]{2,1,0:T(1,128)}), f32[32,1,128]{2,1,0:T(1,128)S(1)}, u32[]{:S(2)}, u32[]{:S(2)}) async-start(f32[32,1,128]{2,1,0:T(1,128)} %broadcast_in_dim.54), calls=%async_computation | async-start | bytes 32768 | tf_op jit(solution)/shard_map/all_to_all | solution.py:190
  65.8 8.6 %collective-permute-start.11 = (f32[1,8,3584]{2,1,0:T(8,128)S(1)}, f32[1,8,3584]{2,1,0:T(8,128)S(1)}, u32[]{:S(2)}, u32[]{:S(2)}) collective-permute-start(f32[1,8,3584]{2,1,0:T(8,128)S(1)} %get-tuple-element.7), channel_id=1, source_target_pairs={{0,16},{16,0},{32,48},{48,32},{1,17},{17,1},{33,49},{49,33},{2,18}... | collective-permute-start | bytes 344072 | tf_op jit(solution)/shard_map/ppermute | solution.py:28
  68.0 7.9 %collective-permute-start.13 = (f32[1,8,3584]{2,1,0:T(8,128)S(1)}, f32[1,8,3584]{2,1,0:T(8,128)S(1)}, u32[]{:S(2)}, u32[]{:S(2)}) collective-permute-start(f32[1,8,3584]{2,1,0:T(8,128)S(1)} %get-tuple-element.7), channel_id=1, source_target_pairs={{0,48},{16,32},{32,16},{48,0},{1,49},{17,33},{33,17},{49,1},{2,50}... | collective-permute-start | bytes 344072 | tf_op jit(solution)/shard_map/ppermute | solution.py:28
  71.3 9.0 %collective-permute-start.12 = (f32[1,8,3584]{2,1,0:T(8,128)S(1)}, f32[1,8,3584]{2,1,0:T(8,128)S(1)}, u32[]{:S(2)}, u32[]{:S(2)}) collective-permute-start(f32[1,8,3584]{2,1,0:T(8,128)S(1)} %get-tuple-element.7), channel_id=1, source_target_pairs={{0,32},{16,48},{32,0},{48,16},{1,33},{17,49},{33,1},{49,17},{2,34}... | collective-permute-start | bytes 344072 | tf_op jit(solution)/shard_map/ppermute | solution.py:28
  74.4 9.8 %collective-permute-start.16 = (f32[4,28,8,128]{3,2,1,0:T(8,128)S(1)}, f32[4,28,8,128]{3,2,1,0:T(8,128)S(1)}, u32[]{:S(2)}, u32[]{:S(2)}) collective-permute-start(f32[4,28,8,128]{3,2,1,0:T(8,128)S(1)} %bitcast.84), channel_id=1, source_target_pairs={{0,128},{64,192},{128,0},{192,64},{1,129},{65,193},{129,1},{193,65... | collective-permute-start | bytes 1376264 | tf_op jit(solution)/shard_map/ppermute | solution.py:28
  80.7 14.4 %collective-permute-start.20 = (f32[2,8,7296]{2,1,0:T(8,128)S(1)}, f32[2,8,7296]{2,1,0:T(8,128)S(1)}, u32[]{:S(2)}, u32[]{:S(2)}) collective-permute-start(f32[2,8,7296]{2,1,0:T(8,128)S(1)} %pad_maximum_fusion.1), channel_id=1, source_target_pairs={{0,128},{64,192},{128,0},{192,64},{1,129},{65,193},{129,1},{193,65... | collective-permute-start | bytes 1400840 | tf_op jit(solution)/shard_map/ppermute | solution.py:28
  82.1 26.3 %collective-permute-start.19 = (f32[2,8,7296]{2,1,0:T(8,128)S(1)}, f32[2,8,7296]{2,1,0:T(8,128)S(1)}, u32[]{:S(2)}, u32[]{:S(2)}) collective-permute-start(f32[2,8,7296]{2,1,0:T(8,128)S(1)} %pad_maximum_fusion.1), channel_id=1, source_target_pairs={{0,192},{64,128},{128,64},{192,0},{1,193},{65,129},{129,65},{193,1... | collective-permute-start | bytes 1400840 | tf_op jit(solution)/shard_map/ppermute | solution.py:28
  82.9 26.1 %collective-permute-start.18 = (f32[2,8,7296]{2,1,0:T(8,128)S(1)}, f32[2,8,7296]{2,1,0:T(8,128)S(1)}, u32[]{:S(2)}, u32[]{:S(2)}) collective-permute-start(f32[2,8,7296]{2,1,0:T(8,128)S(1)} %pad_maximum_fusion.1), channel_id=1, source_target_pairs={{0,64},{64,0},{128,192},{192,128},{1,65},{65,1},{129,193},{193,129... | collective-permute-start | bytes 1400840 | tf_op jit(solution)/shard_map/ppermute | solution.py:28
  84.2 26.9 %copy-start = (f32[4,4,28,8,128]{4,3,2,1,0:T(8,128)}, f32[4,4,28,8,128]{4,3,2,1,0:T(8,128)S(1)}, u32[]{:S(2)}) copy-start(f32[4,4,28,8,128]{4,3,2,1,0:T(8,128)S(1)} %bitcast_dynamic-update-slice_fusion) | copy-start | bytes 5505028
  84.2 26.8 %collective-permute-start.17 = (f32[16,224,128]{2,1,0:T(8,128)S(1)}, f32[16,224,128]{2,1,0:T(8,128)S(1)}, u32[]{:S(2)}, u32[]{:S(2)}) collective-permute-start(f32[16,224,128]{2,1,0:T(8,128)S(1)} %bitcast.88), channel_id=1, source_target_pairs={{0,8},{8,0},{1,9},{9,1},{2,10},{10,2},{3,11},{11,3},{4,12},{12,4},... | collective-permute-start | bytes 5505032 | tf_op jit(solution)/shard_map/ppermute | solution.py:28
  92.6 17.2 %collective-permute-start.21 = (f32[2,8,7296]{2,1,0:T(8,128)S(1)}, f32[2,8,7296]{2,1,0:T(8,128)S(1)}, u32[]{:S(2)}, u32[]{:S(2)}) collective-permute-start(f32[2,8,7296]{2,1,0:T(8,128)S(1)} %pad_maximum_fusion.1), channel_id=1, source_target_pairs={{0,8},{8,0},{1,9},{9,1},{2,10},{10,2},{3,11},{11,3},{4,12},{12,4},... | collective-permute-start | bytes 1400840 | tf_op jit(solution)/shard_map/ppermute | solution.py:28
  95.1 15.9 %copy-start.1 = (f32[2,8,7296]{2,1,0:T(8,128)}, f32[2,8,7296]{2,1,0:T(8,128)S(1)}, u32[]{:S(2)}) copy-start(f32[2,8,7296]{2,1,0:T(8,128)S(1)} %collective-permute-done.20) | copy-start | bytes 1400836
  95.1 14.7 %collective-permute-start.24 = (f32[2,8,7296]{2,1,0:T(8,128)S(1)}, f32[2,8,7296]{2,1,0:T(8,128)S(1)}, u32[]{:S(2)}, u32[]{:S(2)}) collective-permute-start(f32[2,8,7296]{2,1,0:T(8,128)S(1)} %collective-permute-done.20), channel_id=1, source_target_pairs={{0,8},{8,0},{1,9},{9,1},{2,10},{10,2},{3,11},{11,3},{4,12},{12,4},... | collective-permute-start | bytes 1400840 | tf_op jit(solution)/shard_map/ppermute | solution.py:28
  108.4 2.6 %copy-start.2 = (f32[2,8,7296]{2,1,0:T(8,128)}, f32[2,8,7296]{2,1,0:T(8,128)S(1)}, u32[]{:S(2)}) copy-start(f32[2,8,7296]{2,1,0:T(8,128)S(1)} %collective-permute-done.19) | copy-start | bytes 1400836
  108.4 1.9 %collective-permute-start.23 = (f32[2,8,7296]{2,1,0:T(8,128)S(1)}, f32[2,8,7296]{2,1,0:T(8,128)S(1)}, u32[]{:S(2)}, u32[]{:S(2)}) collective-permute-start(f32[2,8,7296]{2,1,0:T(8,128)S(1)} %collective-permute-done.19), channel_id=1, source_target_pairs={{0,8},{8,0},{1,9},{9,1},{2,10},{10,2},{3,11},{11,3},{4,12},{12,4},... | collective-permute-start | bytes 1400840 | tf_op jit(solution)/shard_map/ppermute | solution.py:28
  108.9 2.2 %copy-start.3 = (f32[2,8,7296]{2,1,0:T(8,128)}, f32[2,8,7296]{2,1,0:T(8,128)S(1)}, u32[]{:S(2)}) copy-start(f32[2,8,7296]{2,1,0:T(8,128)S(1)} %collective-permute-done.18) | copy-start | bytes 1400836
  108.9 2.1 %collective-permute-start.22 = (f32[2,8,7296]{2,1,0:T(8,128)S(1)}, f32[2,8,7296]{2,1,0:T(8,128)S(1)}, u32[]{:S(2)}, u32[]{:S(2)}) collective-permute-start(f32[2,8,7296]{2,1,0:T(8,128)S(1)} %collective-permute-done.18), channel_id=1, source_target_pairs={{0,8},{8,0},{1,9},{9,1},{2,10},{10,2},{3,11},{11,3},{4,12},{12,4},... | collective-permute-start | bytes 1400840 | tf_op jit(solution)/shard_map/ppermute | solution.py:28
  109.9 1.2 %copy-start.4 = (f32[2,8,7296]{2,1,0:T(8,128)}, f32[2,8,7296]{2,1,0:T(8,128)S(1)}, u32[]{:S(2)}) copy-start(f32[2,8,7296]{2,1,0:T(8,128)S(1)} %collective-permute-done.21) | copy-start | bytes 1400836
  109.9 1.2 %copy-start.5 = (f32[2,8,7296]{2,1,0:T(8,128)}, f32[2,8,7296]{2,1,0:T(8,128)S(1)}, u32[]{:S(2)}) copy-start(f32[2,8,7296]{2,1,0:T(8,128)S(1)} %collective-permute-done.24) | copy-start | bytes 1400836
  110.4 0.8 copy-start.6
  111.1 0.8 copy-start.7
  111.1 1.4 %copy-start.8 = (f32[16,224,128]{2,1,0:T(8,128)}, f32[16,224,128]{2,1,0:T(8,128)S(1)}, u32[]{:S(2)}) copy-start(f32[16,224,128]{2,1,0:T(8,128)S(1)} %collective-permute-done.17.refs_4_) | copy-start | bytes 5505028

commit v6 on v5

--- a/solution.py
+++ b/solution.py
@@ -158,7 +158,7 @@
     for mask in (3, 2, 1):
         over_y[mask] = swap(summed(mask), y=mask)
     moments = {0: own_moment}
-    for mask in MASKS:
+    for mask in (2, 3, 1):
         moments[mask] = swap(own_moment, zh=mask)
     total = summed(0)
     for mask in (3, 2, 1):

time: 121 us -> 120 us (level)
  waiting for transfers between devices: 34.7 us -> 31.3 us
  starting transfers between devices: 66.1 us -> 68.3 us
    ppermute x25, starting transfers between devices: 55.3 us -> 58.9 us  [swap(): lax.ppermute(x, axes, [(i, i ^ mask) for i in range(math.prod(sizes))])]
    ppermute x25, waiting for transfers between devices: 31.8 us -> 28.5 us  [swap(): lax.ppermute(x, axes, [(i, i ^ mask) for i in range(math.prod(sizes))])]
    all_to_all x1, starting transfers between devices: 10.8 us -> 9.41 us  [add_squares(): lax.all_to_all(jnp.broadcast_to(row, (n,) + row.shape), axes, 0, 0)]
where the time goes in v6:
time: 120 us; the launch traced here: 119 us
  starting transfers between devices  68.3 us (57%)
  waiting for transfers between devices  31.3 us (26%)
  Pallas kernels  7.83 us (7%)
  other arithmetic  7.79 us (6%)
  local copies, waits for them, and re-layouts  2.86 us (2%)
    ppermute x25, starting transfers between devices, swap(): lax.ppermute(x, axes, [(i, i ^ mask) for i in range(math.prod(sizes))])  58.9 us
    ppermute x25, waiting for transfers between devices, swap(): lax.ppermute(x, axes, [(i, i ^ mask) for i in range(math.prod(sizes))])  28.5 us
    all_to_all x1, starting transfers between devices, add_squares(): lax.all_to_all(jnp.broadcast_to(row, (n,) + row.shape), axes, 0, 0)  9.41 us
    pallas_call x1, Pallas kernels, final(): pl.pallas_call(lambda *refs: final_kernel(ceiling, *refs), out_shape=(jax...  7.77 us
    sub x1, other arithmetic, drift(): return rows_at(a_rows, start, count) - rows_at(l_rows, start, count)  3.12 us
    all_to_all x1, waiting for transfers between devices, add_squares(): lax.all_to_all(jnp.broadcast_to(row, (n,) + row.shape), axes, 0, 0)  2.83 us
  transfers between devices with their start and end apart: 26, of which 9 were waited for; matrix products, arithmetic and copies ran while one was open for 4% of the time, Pallas kernels for 0%

profile of v6, /device:TPU:1, one launch (start us, length us, event | category | flops | bytes accessed | tf_op | source)
XLA Modules:
  0.0 119.2 jit_solution(11667588068474488049)
XLA Ops:
  0.6 3.1 %dynamic-slice_subtract_fusion = (f32[4,8,7168]{2,1,0:T(8,128)}, f32[4,8,7168]{2,1,0:T(8,128)S(1)}) fusion(f32[16,8,7168]{2,1,0:T(8,128)} %bitcast.90, s32[]{:T(128)S(6)} %select_n.154, f32[16,8,7168]{2,1,0:T(8,128)} %bitcast.85, s32[]{:T(128)S(6)} %select_n.151), kind=kLoop, calls=%fused_computation | loop fusion | flops 458752 | bytes 5505032 | tf_op jit(solution)/shard_map/sub | solution.py:146
  3.8 3.2 %collective-permute-start.1 = (f32[4,8,7168]{2,1,0:T(8,128)}, f32[4,8,7168]{2,1,0:T(8,128)S(1)}, u32[]{:S(2)}, u32[]{:S(2)}) collective-permute-start(f32[4,8,7168]{2,1,0:T(8,128)} %get-tuple-element.11), channel_id=1, source_target_pairs={{0,8},{8,0},{1,9},{9,1},{2,10},{10,2},{3,11},{11,3},{4,12},{12,4},... | collective-permute-start | bytes 2752520 | tf_op jit(solution)/shard_map/ppermute | solution.py:28
  7.0 0.0 collective-permute-start
  7.0 3.6 %collective-permute-done.1 = f32[4,8,7168]{2,1,0:T(8,128)S(1)} collective-permute-done((f32[4,8,7168]{2,1,0:T(8,128)}, f32[4,8,7168]{2,1,0:T(8,128)S(1)}, u32[]{:S(2)}, u32[]{:S(2)}) %collective-permute-start.1) | collective-permute-done | bytes 917536 | tf_op jit(solution)/shard_map/ppermute | solution.py:28
  10.6 0.0 collective-permute-done
  10.6 1.9 %dynamic-slice_add_fusion.2 = (f32[2,8,7168]{2,1,0:T(8,128)S(1)}, f32[2,8,7168]{2,1,0:T(8,128)S(1)}, f32[2,8,7168]{2,1,0:T(8,128)S(1)}) fusion(f32[4,8,7168]{2,1,0:T(8,128)S(1)} %collective-permute-done.1, s32[]{:T(128)S(6)} %select_n.155, f32[16,8,7168]{2,1,0:T(8,128)} %bitcast.91, s32[]{:T(128)S(6)} %select_n.153, f32[16,8,7168]{2,1,0:T(8,128)} %bitcast.86, ...), kind=kLoop, calls=%fused_computation.12 | loop fusion | flops 688128 | bytes 5505048 | tf_op jit(solution)/shard_map/add | solution.py:155
  12.5 1.1 collective-permute-start.2
  13.6 0.3 collective-permute-start.3
  13.9 1.9 %collective-permute-start.4 = (f32[2,8,7168]{2,1,0:T(8,128)S(1)}, f32[2,8,7168]{2,1,0:T(8,128)}, u32[]{:S(2)}, u32[]{:S(2)}) collective-permute-start(f32[2,8,7168]{2,1,0:T(8,128)S(1)} %get-tuple-element.10), channel_id=1, source_target_pairs={{0,64},{64,0},{128,192},{192,128},{1,65},{65,1},{129,193},{193,129... | collective-permute-start | bytes 1376264 | tf_op jit(solution)/shard_map/ppermute | solution.py:28
  15.9 1.4 %collective-permute-start.7 = (f32[224,128]{1,0:T(8,128)S(1)}, f32[224,128]{1,0:T(8,128)S(1)}, u32[]{:S(2)}, u32[]{:S(2)}) collective-permute-start(f32[224,128]{1,0:T(8,128)S(1)} %bitcast.110), channel_id=1, source_target_pairs={{0,16},{16,0},{32,48},{48,32},{1,17},{17,1},{33,49},{49,33},{2,18}... | collective-permute-start | bytes 344072 | tf_op jit(solution)/shard_map/ppermute | solution.py:28
  17.3 4.2 %collective-permute-start.6 = (f32[224,128]{1,0:T(8,128)S(1)}, f32[224,128]{1,0:T(8,128)S(1)}, u32[]{:S(2)}, u32[]{:S(2)}) collective-permute-start(f32[224,128]{1,0:T(8,128)S(1)} %bitcast.111), channel_id=1, source_target_pairs={{0,48},{16,32},{32,16},{48,0},{1,49},{17,33},{33,17},{49,1},{2,50}... | collective-permute-start | bytes 344072 | tf_op jit(solution)/shard_map/ppermute | solution.py:28
  21.5 0.7 stack.47.refs_0_
  22.2 13.2 %collective-permute-done.2 = f32[2,8,7168]{2,1,0:T(8,128)S(1)} collective-permute-done((f32[2,8,7168]{2,1,0:T(8,128)S(1)}, f32[2,8,7168]{2,1,0:T(8,128)S(1)}, u32[]{:S(2)}, u32[]{:S(2)}) %collective-permute-start.2) | collective-permute-done | bytes 458784 | tf_op jit(solution)/shard_map/ppermute | solution.py:28
  35.4 5.3 %collective-permute-start.5 = (f32[224,128]{1,0:T(8,128)S(1)}, f32[224,128]{1,0:T(8,128)S(1)}, u32[]{:S(2)}, u32[]{:S(2)}) collective-permute-start(f32[224,128]{1,0:T(8,128)S(1)} %bitcast.112), channel_id=1, source_target_pairs={{0,32},{16,48},{32,0},{48,16},{1,33},{17,49},{33,1},{49,17},{2,34}... | collective-permute-start | bytes 344072 | tf_op jit(solution)/shard_map/ppermute | solution.py:28
  40.7 0.0 collective-permute-done.3
  40.7 0.0 collective-permute-done.4
  40.7 1.4 %add_add_fusion = f32[2,8,7168]{2,1,0:T(8,128)S(1)} fusion(f32[2,8,7168]{2,1,0:T(8,128)} %collective-permute-done.4, f32[2,8,7168]{2,1,0:T(8,128)S(1)} %collective-permute-done.3, f32[2,8,7168]{2,1,0:T(8,128)S(1)} %collective-permute-done.2, f32[4,8,7168]{2,1,0:T(8,128)S(1)} %collective-permute-done, s32[]{:T(128)S(6)} %select_n.152, ...), kind=kLoop, calls=%fused_computation.10 | loop fusion | flops 573440 | bytes 3211272 | tf_op jit(solution)/shard_map/add | solution.py:165
  42.1 0.1 dynamic-slice_select_fusion.2
  42.2 1.3 %collective-permute-start.8 = (f32[1,8,3584]{2,1,0:T(8,128)S(1)}, f32[1,8,3584]{2,1,0:T(8,128)S(1)}, u32[]{:S(2)}, u32[]{:S(2)}) collective-permute-start(f32[1,8,3584]{2,1,0:T(8,128)S(1)} %get-tuple-element.15), channel_id=1, source_target_pairs={{0,16},{16,0},{32,48},{48,32},{1,17},{17,1},{33,49},{49,33},{2,18}... | collective-permute-start | bytes 344072 | tf_op jit(solution)/shard_map/ppermute | solution.py:28
  43.5 0.0 collective-permute-start.9
  43.5 0.0 collective-permute-done.5
  43.5 5.1 %collective-permute-start.10 = (f32[1,8,3584]{2,1,0:T(8,128)S(1)}, f32[1,8,3584]{2,1,0:T(8,128)S(1)}, u32[]{:S(2)}, u32[]{:S(2)}) collective-permute-start(f32[1,8,3584]{2,1,0:T(8,128)S(1)} %get-tuple-element.16), channel_id=1, source_target_pairs={{0,32},{16,48},{32,0},{48,16},{1,33},{17,49},{33,1},{49,17},{2,34}... | collective-permute-start | bytes 344072 | tf_op jit(solution)/shard_map/ppermute | solution.py:28
  48.6 0.0 collective-permute-done.6
  48.7 0.0 collective-permute-done.7
  48.7 2.8 %collective-permute-start.15 = (f32[4,28,8,128]{3,2,1,0:T(8,128)S(1)}, f32[4,28,8,128]{3,2,1,0:T(8,128)S(1)}, u32[]{:S(2)}, u32[]{:S(2)}) collective-permute-start(f32[4,28,8,128]{3,2,1,0:T(8,128)S(1)} %bitcast.82), channel_id=1, source_target_pairs={{0,192},{64,128},{128,64},{192,0},{1,193},{65,129},{129,65},{193,1... | collective-permute-start | bytes 1376264 | tf_op jit(solution)/shard_map/ppermute | solution.py:28
  51.5 0.0 collective-permute-start.14
  51.5 2.9 %collective-permute-done.8 = f32[1,8,3584]{2,1,0:T(8,128)S(1)} collective-permute-done((f32[1,8,3584]{2,1,0:T(8,128)S(1)}, f32[1,8,3584]{2,1,0:T(8,128)S(1)}, u32[]{:S(2)}, u32[]{:S(2)}) %collective-permute-start.8) | collective-permute-done | bytes 114720 | tf_op jit(solution)/shard_map/ppermute | solution.py:28
  54.4 0.0 collective-permute-done.9
  54.4 0.0 collective-permute-done.10
  54.4 0.1 multiply_reduce_fusion
  54.5 0.6 broadcast_in_dim.54
  55.1 9.4 %all-to-all-start = ((f32[32,1,128]{2,1,0:T(1,128)}), f32[32,1,128]{2,1,0:T(1,128)S(1)}, u32[]{:S(2)}, u32[]{:S(2)}) async-start(f32[32,1,128]{2,1,0:T(1,128)} %broadcast_in_dim.54), calls=%async_computation | async-start | bytes 32768 | tf_op jit(solution)/shard_map/all_to_all | solution.py:190
  64.5 2.2 %collective-permute-start.11 = (f32[1,8,3584]{2,1,0:T(8,128)S(1)}, f32[1,8,3584]{2,1,0:T(8,128)S(1)}, u32[]{:S(2)}, u32[]{:S(2)}) collective-permute-start(f32[1,8,3584]{2,1,0:T(8,128)S(1)} %get-tuple-element.7), channel_id=1, source_target_pairs={{0,16},{16,0},{32,48},{48,32},{1,17},{17,1},{33,49},{49,33},{2,18}... | collective-permute-start | bytes 344072 | tf_op jit(solution)/shard_map/ppermute | solution.py:28
  66.7 3.3 %collective-permute-start.13 = (f32[1,8,3584]{2,1,0:T(8,128)S(1)}, f32[1,8,3584]{2,1,0:T(8,128)S(1)}, u32[]{:S(2)}, u32[]{:S(2)}) collective-permute-start(f32[1,8,3584]{2,1,0:T(8,128)S(1)} %get-tuple-element.7), channel_id=1, source_target_pairs={{0,48},{16,32},{32,16},{48,0},{1,49},{17,33},{33,17},{49,1},{2,50}... | collective-permute-start | bytes 344072 | tf_op jit(solution)/shard_map/ppermute | solution.py:28
  70.0 0.2 collective-permute-start.12
  70.3 2.8 %all-to-all-done = f32[32,1,128]{2,1,0:T(1,128)S(1)} async-done(((f32[32,1,128]{2,1,0:T(1,128)}), f32[32,1,128]{2,1,0:T(1,128)S(1)}, u32[]{:S(2)}, u32[]{:S(2)}) %all-to-all-start) | async-done | bytes 16416 | tf_op jit(solution)/shard_map/all_to_all | solution.py:190
  73.2 0.0 collective-permute-done.11
  73.2 2.3 %collective-permute-start.16 = (f32[4,28,8,128]{3,2,1,0:T(8,128)S(1)}, f32[4,28,8,128]{3,2,1,0:T(8,128)S(1)}, u32[]{:S(2)}, u32[]{:S(2)}) collective-permute-start(f32[4,28,8,128]{3,2,1,0:T(8,128)S(1)} %bitcast.84), channel_id=1, source_target_pairs={{0,128},{64,192},{128,0},{192,64},{1,129},{65,193},{129,1},{193,65... | collective-permute-start | bytes 1376264 | tf_op jit(solution)/shard_map/ppermute | solution.py:28
  75.4 0.0 collective-permute-done.13
  75.4 2.3 %collective-permute-done.12 = f32[1,8,3584]{2,1,0:T(8,128)S(1)} collective-permute-done((f32[1,8,3584]{2,1,0:T(8,128)S(1)}, f32[1,8,3584]{2,1,0:T(8,128)S(1)}, u32[]{:S(2)}, u32[]{:S(2)}) %collective-permute-start.12) | collective-permute-done | bytes 114720 | tf_op jit(solution)/shard_map/ppermute | solution.py:28
  77.8 0.2 broadcast_in_dim.48
  78.1 0.0 collective-permute-done.15
  78.1 0.0 collective-permute-done.14
  78.2 3.6 %collective-permute-start.20 = (f32[2,8,7296]{2,1,0:T(8,128)S(1)}, f32[2,8,7296]{2,1,0:T(8,128)S(1)}, u32[]{:S(2)}, u32[]{:S(2)}) collective-permute-start(f32[2,8,7296]{2,1,0:T(8,128)S(1)} %pad_maximum_fusion.1), channel_id=1, source_target_pairs={{0,128},{64,192},{128,0},{192,64},{1,129},{65,193},{129,1},{193,65... | collective-permute-start | bytes 1400840 | tf_op jit(solution)/shard_map/ppermute | solution.py:28
  81.8 0.8 collective-permute-start.19
  82.5 0.0 collective-permute-start.18
  82.7 9.8 %collective-permute-start.17 = (f32[16,224,128]{2,1,0:T(8,128)S(1)}, f32[16,224,128]{2,1,0:T(8,128)S(1)}, u32[]{:S(2)}, u32[]{:S(2)}) collective-permute-start(f32[16,224,128]{2,1,0:T(8,128)S(1)} %bitcast.88), channel_id=1, source_target_pairs={{0,8},{8,0},{1,9},{9,1},{2,10},{10,2},{3,11},{11,3},{4,12},{12,4},... | collective-permute-start | bytes 5505032 | tf_op jit(solution)/shard_map/ppermute | solution.py:28
  92.5 0.1 collective-permute-start.21
  92.6 0.4 collective-permute-done.20
  93.0 9.3 %collective-permute-start.24 = (f32[2,8,7296]{2,1,0:T(8,128)S(1)}, f32[2,8,7296]{2,1,0:T(8,128)S(1)}, u32[]{:S(2)}, u32[]{:S(2)}) collective-permute-start(f32[2,8,7296]{2,1,0:T(8,128)S(1)} %collective-permute-done.20), channel_id=1, source_target_pairs={{0,8},{8,0},{1,9},{9,1},{2,10},{10,2},{3,11},{11,3},{4,12},{12,4},... | collective-permute-start | bytes 1400840 | tf_op jit(solution)/shard_map/ppermute | solution.py:28
  102.3 5.0 %collective-permute-done.19 = f32[2,8,7296]{2,1,0:T(8,128)S(1)} collective-permute-done((f32[2,8,7296]{2,1,0:T(8,128)S(1)}, f32[2,8,7296]{2,1,0:T(8,128)S(1)}, u32[]{:S(2)}, u32[]{:S(2)}) %collective-permute-start.19) | collective-permute-done | bytes 466976 | tf_op jit(solution)/shard_map/ppermute | solution.py:28
  107.3 0.5 collective-permute-start.23
  107.8 0.0 collective-permute-done.18
  107.8 0.3 collective-permute-start.22
  108.1 0.8 pad_maximum_fusion.refs_5_.refs_13_
  108.9 0.0 collective-permute-done.21
  108.9 0.0 collective-permute-done.24
  108.9 0.4 collective-permute-done.23
  109.3 0.7 collective-permute-done.22
  109.9 0.0 collective-permute-done.17.refs_4_
  110.0 0.1 copy-done.6
  110.1 0.7 copy-done.7
  110.7 0.6 copy-done.8
  111.3 7.8 %final.1 = (f32[128,7168]{1,0:T(8,128)}, f32[224,128]{1,0:T(8,128)}) custom-call(s32[11]{0:T(128)} %stack.47.refs_0_, f32[128,7168]{1,0:T(8,128)} %refs_1_.1, f32[224,128]{1,0:T(8,128)} %bitcast.109, f32[16,224,128]{2,1,0:T(8,128)} %bitcast.89, f32[16,224,128]{2,1,0:T(8,128)} %copy-done.8, f32[16,7296]{1,0:T(8,128)} %pad_maximum_fusion.refs_5_.refs_13_, ...), custom_call_target="tpu_custom_call" | custom-call | flops 4587520 | bytes 14680064 | tf_op jit(solution)/shard_map/final/pallas_call | solution.py:112
  (44 shorter events, 0.5 us)
Async XLA Ops:
  3.8 6.8 %collective-permute-start.1 = (f32[4,8,7168]{2,1,0:T(8,128)}, f32[4,8,7168]{2,1,0:T(8,128)S(1)}, u32[]{:S(2)}, u32[]{:S(2)}) collective-permute-start(f32[4,8,7168]{2,1,0:T(8,128)} %get-tuple-element.11), channel_id=1, source_target_pairs={{0,8},{8,0},{1,9},{9,1},{2,10},{10,2},{3,11},{11,3},{4,12},{12,4},... | collective-permute-start | bytes 2752520 | tf_op jit(solution)/shard_map/ppermute | solution.py:28
  7.0 3.6 %collective-permute-start = (f32[4,8,7168]{2,1,0:T(8,128)S(1)}, f32[4,8,7168]{2,1,0:T(8,128)S(1)}, u32[]{:S(2)}, u32[]{:S(2)}) collective-permute-start(f32[4,8,7168]{2,1,0:T(8,128)S(1)} %get-tuple-element.12), channel_id=1, source_target_pairs={{0,8},{8,0},{1,9},{9,1},{2,10},{10,2},{3,11},{11,3},{4,12},{12,4},... | collective-permute-start | bytes 2752520 | tf_op jit(solution)/shard_map/ppermute | solution.py:28
  7.0 8.8 %copy-start.9 = (f32[128,1,224]{0,2,1:T(8,128)S(1)}, f32[128,1,224]{0,2,1:T(8,128)}, u32[]{:S(2)}) copy-start(f32[128,1,224]{0,2,1:T(8,128)} %param.5) | copy-start | bytes 344068
  12.5 22.9 %collective-permute-start.2 = (f32[2,8,7168]{2,1,0:T(8,128)S(1)}, f32[2,8,7168]{2,1,0:T(8,128)S(1)}, u32[]{:S(2)}, u32[]{:S(2)}) collective-permute-start(f32[2,8,7168]{2,1,0:T(8,128)S(1)} %get-tuple-element.8), channel_id=1, source_target_pairs={{0,192},{64,128},{128,64},{192,0},{1,193},{65,129},{129,65},{193,1... | collective-permute-start | bytes 1376264 | tf_op jit(solution)/shard_map/ppermute | solution.py:28
  13.6 27.1 %collective-permute-start.3 = (f32[2,8,7168]{2,1,0:T(8,128)S(1)}, f32[2,8,7168]{2,1,0:T(8,128)S(1)}, u32[]{:S(2)}, u32[]{:S(2)}) collective-permute-start(f32[2,8,7168]{2,1,0:T(8,128)S(1)} %get-tuple-element.9), channel_id=1, source_target_pairs={{0,128},{64,192},{128,0},{192,64},{1,129},{65,193},{129,1},{193,65... | collective-permute-start | bytes 1376264 | tf_op jit(solution)/shard_map/ppermute | solution.py:28
  13.9 26.7 %collective-permute-start.4 = (f32[2,8,7168]{2,1,0:T(8,128)S(1)}, f32[2,8,7168]{2,1,0:T(8,128)}, u32[]{:S(2)}, u32[]{:S(2)}) collective-permute-start(f32[2,8,7168]{2,1,0:T(8,128)S(1)} %get-tuple-element.10), channel_id=1, source_target_pairs={{0,64},{64,0},{128,192},{192,128},{1,65},{65,1},{129,193},{193,129... | collective-permute-start | bytes 1376264 | tf_op jit(solution)/shard_map/ppermute | solution.py:28
  15.9 32.8 %collective-permute-start.7 = (f32[224,128]{1,0:T(8,128)S(1)}, f32[224,128]{1,0:T(8,128)S(1)}, u32[]{:S(2)}, u32[]{:S(2)}) collective-permute-start(f32[224,128]{1,0:T(8,128)S(1)} %bitcast.110), channel_id=1, source_target_pairs={{0,16},{16,0},{32,48},{48,32},{1,17},{17,1},{33,49},{49,33},{2,18}... | collective-permute-start | bytes 344072 | tf_op jit(solution)/shard_map/ppermute | solution.py:28
  17.3 31.4 %collective-permute-start.6 = (f32[224,128]{1,0:T(8,128)S(1)}, f32[224,128]{1,0:T(8,128)S(1)}, u32[]{:S(2)}, u32[]{:S(2)}) collective-permute-start(f32[224,128]{1,0:T(8,128)S(1)} %bitcast.111), channel_id=1, source_target_pairs={{0,48},{16,32},{32,16},{48,0},{1,49},{17,33},{33,17},{49,1},{2,50}... | collective-permute-start | bytes 344072 | tf_op jit(solution)/shard_map/ppermute | solution.py:28
  35.4 8.1 %collective-permute-start.5 = (f32[224,128]{1,0:T(8,128)S(1)}, f32[224,128]{1,0:T(8,128)S(1)}, u32[]{:S(2)}, u32[]{:S(2)}) collective-permute-start(f32[224,128]{1,0:T(8,128)S(1)} %bitcast.112), channel_id=1, source_target_pairs={{0,32},{16,48},{32,0},{48,16},{1,33},{17,49},{33,1},{49,17},{2,34}... | collective-permute-start | bytes 344072 | tf_op jit(solution)/shard_map/ppermute | solution.py:28
  42.2 12.2 %collective-permute-start.8 = (f32[1,8,3584]{2,1,0:T(8,128)S(1)}, f32[1,8,3584]{2,1,0:T(8,128)S(1)}, u32[]{:S(2)}, u32[]{:S(2)}) collective-permute-start(f32[1,8,3584]{2,1,0:T(8,128)S(1)} %get-tuple-element.15), channel_id=1, source_target_pairs={{0,16},{16,0},{32,48},{48,32},{1,17},{17,1},{33,49},{49,33},{2,18}... | collective-permute-start | bytes 344072 | tf_op jit(solution)/shard_map/ppermute | solution.py:28
  43.5 10.9 %collective-permute-start.9 = (f32[1,8,3584]{2,1,0:T(8,128)S(1)}, f32[1,8,3584]{2,1,0:T(8,128)S(1)}, u32[]{:S(2)}, u32[]{:S(2)}) collective-permute-start(f32[1,8,3584]{2,1,0:T(8,128)S(1)} %get-tuple-element.17), channel_id=1, source_target_pairs={{0,48},{16,32},{32,16},{48,0},{1,49},{17,33},{33,17},{49,1},{2,50}... | collective-permute-start | bytes 344072 | tf_op jit(solution)/shard_map/ppermute | solution.py:28
  43.5 10.9 %collective-permute-start.10 = (f32[1,8,3584]{2,1,0:T(8,128)S(1)}, f32[1,8,3584]{2,1,0:T(8,128)S(1)}, u32[]{:S(2)}, u32[]{:S(2)}) collective-permute-start(f32[1,8,3584]{2,1,0:T(8,128)S(1)} %get-tuple-element.16), channel_id=1, source_target_pairs={{0,32},{16,48},{32,0},{48,16},{1,33},{17,49},{33,1},{49,17},{2,34}... | collective-permute-start | bytes 344072 | tf_op jit(solution)/shard_map/ppermute | solution.py:28
  48.7 29.3 %collective-permute-start.15 = (f32[4,28,8,128]{3,2,1,0:T(8,128)S(1)}, f32[4,28,8,128]{3,2,1,0:T(8,128)S(1)}, u32[]{:S(2)}, u32[]{:S(2)}) collective-permute-start(f32[4,28,8,128]{3,2,1,0:T(8,128)S(1)} %bitcast.82), channel_id=1, source_target_pairs={{0,192},{64,128},{128,64},{192,0},{1,193},{65,129},{129,65},{193,1... | collective-permute-start | bytes 1376264 | tf_op jit(solution)/shard_map/ppermute | solution.py:28
  51.5 26.6 %collective-permute-start.14 = (f32[4,28,8,128]{3,2,1,0:T(8,128)S(1)}, f32[4,28,8,128]{3,2,1,0:T(8,128)S(1)}, u32[]{:S(2)}, u32[]{:S(2)}) collective-permute-start(f32[4,28,8,128]{3,2,1,0:T(8,128)S(1)} %bitcast.83), channel_id=1, source_target_pairs={{0,64},{64,0},{128,192},{192,128},{1,65},{65,1},{129,193},{193,129... | collective-permute-start | bytes 1376264 | tf_op jit(solution)/shard_map/ppermute | solution.py:28
  55.1 18.0 %all-to-all-start = ((f32[32,1,128]{2,1,0:T(1,128)}), f32[32,1,128]{2,1,0:T(1,128)S(1)}, u32[]{:S(2)}, u32[]{:S(2)}) async-start(f32[32,1,128]{2,1,0:T(1,128)} %broadcast_in_dim.54), calls=%async_computation | async-start | bytes 32768 | tf_op jit(solution)/shard_map/all_to_all | solution.py:190
  64.5 8.6 %collective-permute-start.11 = (f32[1,8,3584]{2,1,0:T(8,128)S(1)}, f32[1,8,3584]{2,1,0:T(8,128)S(1)}, u32[]{:S(2)}, u32[]{:S(2)}) collective-permute-start(f32[1,8,3584]{2,1,0:T(8,128)S(1)} %get-tuple-element.7), channel_id=1, source_target_pairs={{0,16},{16,0},{32,48},{48,32},{1,17},{17,1},{33,49},{49,33},{2,18}... | collective-permute-start | bytes 344072 | tf_op jit(solution)/shard_map/ppermute | solution.py:28
  66.7 8.7 %collective-permute-start.13 = (f32[1,8,3584]{2,1,0:T(8,128)S(1)}, f32[1,8,3584]{2,1,0:T(8,128)S(1)}, u32[]{:S(2)}, u32[]{:S(2)}) collective-permute-start(f32[1,8,3584]{2,1,0:T(8,128)S(1)} %get-tuple-element.7), channel_id=1, source_target_pairs={{0,48},{16,32},{32,16},{48,0},{1,49},{17,33},{33,17},{49,1},{2,50}... | collective-permute-start | bytes 344072 | tf_op jit(solution)/shard_map/ppermute | solution.py:28
  70.0 7.7 %collective-permute-start.12 = (f32[1,8,3584]{2,1,0:T(8,128)S(1)}, f32[1,8,3584]{2,1,0:T(8,128)S(1)}, u32[]{:S(2)}, u32[]{:S(2)}) collective-permute-start(f32[1,8,3584]{2,1,0:T(8,128)S(1)} %get-tuple-element.7), channel_id=1, source_target_pairs={{0,32},{16,48},{32,0},{48,16},{1,33},{17,49},{33,1},{49,17},{2,34}... | collective-permute-start | bytes 344072 | tf_op jit(solution)/shard_map/ppermute | solution.py:28
  73.2 9.5 %collective-permute-start.16 = (f32[4,28,8,128]{3,2,1,0:T(8,128)S(1)}, f32[4,28,8,128]{3,2,1,0:T(8,128)S(1)}, u32[]{:S(2)}, u32[]{:S(2)}) collective-permute-start(f32[4,28,8,128]{3,2,1,0:T(8,128)S(1)} %bitcast.84), channel_id=1, source_target_pairs={{0,128},{64,192},{128,0},{192,64},{1,129},{65,193},{129,1},{193,65... | collective-permute-start | bytes 1376264 | tf_op jit(solution)/shard_map/ppermute | solution.py:28
  78.2 14.8 %collective-permute-start.20 = (f32[2,8,7296]{2,1,0:T(8,128)S(1)}, f32[2,8,7296]{2,1,0:T(8,128)S(1)}, u32[]{:S(2)}, u32[]{:S(2)}) collective-permute-start(f32[2,8,7296]{2,1,0:T(8,128)S(1)} %pad_maximum_fusion.1), channel_id=1, source_target_pairs={{0,128},{64,192},{128,0},{192,64},{1,129},{65,193},{129,1},{193,65... | collective-permute-start | bytes 1400840 | tf_op jit(solution)/shard_map/ppermute | solution.py:28
  81.8 25.5 %collective-permute-start.19 = (f32[2,8,7296]{2,1,0:T(8,128)S(1)}, f32[2,8,7296]{2,1,0:T(8,128)S(1)}, u32[]{:S(2)}, u32[]{:S(2)}) collective-permute-start(f32[2,8,7296]{2,1,0:T(8,128)S(1)} %pad_maximum_fusion.1), channel_id=1, source_target_pairs={{0,192},{64,128},{128,64},{192,0},{1,193},{65,129},{129,65},{193,1... | collective-permute-start | bytes 1400840 | tf_op jit(solution)/shard_map/ppermute | solution.py:28
  82.5 25.3 %collective-permute-start.18 = (f32[2,8,7296]{2,1,0:T(8,128)S(1)}, f32[2,8,7296]{2,1,0:T(8,128)S(1)}, u32[]{:S(2)}, u32[]{:S(2)}) collective-permute-start(f32[2,8,7296]{2,1,0:T(8,128)S(1)} %pad_maximum_fusion.1), channel_id=1, source_target_pairs={{0,64},{64,0},{128,192},{192,128},{1,65},{65,1},{129,193},{193,129... | collective-permute-start | bytes 1400840 | tf_op jit(solution)/shard_map/ppermute | solution.py:28
  82.7 27.3 %copy-start = (f32[4,4,28,8,128]{4,3,2,1,0:T(8,128)}, f32[4,4,28,8,128]{4,3,2,1,0:T(8,128)S(1)}, u32[]{:S(2)}) copy-start(f32[4,4,28,8,128]{4,3,2,1,0:T(8,128)S(1)} %bitcast_dynamic-update-slice_fusion) | copy-start | bytes 5505028
  82.7 27.2 %collective-permute-start.17 = (f32[16,224,128]{2,1,0:T(8,128)S(1)}, f32[16,224,128]{2,1,0:T(8,128)S(1)}, u32[]{:S(2)}, u32[]{:S(2)}) collective-permute-start(f32[16,224,128]{2,1,0:T(8,128)S(1)} %bitcast.88), channel_id=1, source_target_pairs={{0,8},{8,0},{1,9},{9,1},{2,10},{10,2},{3,11},{11,3},{4,12},{12,4},... | collective-permute-start | bytes 5505032 | tf_op jit(solution)/shard_map/ppermute | solution.py:28
  92.5 16.4 %collective-permute-start.21 = (f32[2,8,7296]{2,1,0:T(8,128)S(1)}, f32[2,8,7296]{2,1,0:T(8,128)S(1)}, u32[]{:S(2)}, u32[]{:S(2)}) collective-permute-start(f32[2,8,7296]{2,1,0:T(8,128)S(1)} %pad_maximum_fusion.1), channel_id=1, source_target_pairs={{0,8},{8,0},{1,9},{9,1},{2,10},{10,2},{3,11},{11,3},{4,12},{12,4},... | collective-permute-start | bytes 1400840 | tf_op jit(solution)/shard_map/ppermute | solution.py:28
  93.0 16.9 %copy-start.1 = (f32[2,8,7296]{2,1,0:T(8,128)}, f32[2,8,7296]{2,1,0:T(8,128)S(1)}, u32[]{:S(2)}) copy-start(f32[2,8,7296]{2,1,0:T(8,128)S(1)} %collective-permute-done.20) | copy-start | bytes 1400836
  93.0 15.9 %collective-permute-start.24 = (f32[2,8,7296]{2,1,0:T(8,128)S(1)}, f32[2,8,7296]{2,1,0:T(8,128)S(1)}, u32[]{:S(2)}, u32[]{:S(2)}) collective-permute-start(f32[2,8,7296]{2,1,0:T(8,128)S(1)} %collective-permute-done.20), channel_id=1, source_target_pairs={{0,8},{8,0},{1,9},{9,1},{2,10},{10,2},{3,11},{11,3},{4,12},{12,4},... | collective-permute-start | bytes 1400840 | tf_op jit(solution)/shard_map/ppermute | solution.py:28
  107.3 2.6 %copy-start.2 = (f32[2,8,7296]{2,1,0:T(8,128)}, f32[2,8,7296]{2,1,0:T(8,128)S(1)}, u32[]{:S(2)}) copy-start(f32[2,8,7296]{2,1,0:T(8,128)S(1)} %collective-permute-done.19) | copy-start | bytes 1400836
  107.3 1.9 %collective-permute-start.23 = (f32[2,8,7296]{2,1,0:T(8,128)S(1)}, f32[2,8,7296]{2,1,0:T(8,128)S(1)}, u32[]{:S(2)}, u32[]{:S(2)}) collective-permute-start(f32[2,8,7296]{2,1,0:T(8,128)S(1)} %collective-permute-done.19), channel_id=1, source_target_pairs={{0,8},{8,0},{1,9},{9,1},{2,10},{10,2},{3,11},{11,3},{4,12},{12,4},... | collective-permute-start | bytes 1400840 | tf_op jit(solution)/shard_map/ppermute | solution.py:28
  107.8 2.2 %copy-start.3 = (f32[2,8,7296]{2,1,0:T(8,128)}, f32[2,8,7296]{2,1,0:T(8,128)S(1)}, u32[]{:S(2)}) copy-start(f32[2,8,7296]{2,1,0:T(8,128)S(1)} %collective-permute-done.18) | copy-start | bytes 1400836
  107.8 2.1 %collective-permute-start.22 = (f32[2,8,7296]{2,1,0:T(8,128)S(1)}, f32[2,8,7296]{2,1,0:T(8,128)S(1)}, u32[]{:S(2)}, u32[]{:S(2)}) collective-permute-start(f32[2,8,7296]{2,1,0:T(8,128)S(1)} %collective-permute-done.18), channel_id=1, source_target_pairs={{0,8},{8,0},{1,9},{9,1},{2,10},{10,2},{3,11},{11,3},{4,12},{12,4},... | collective-permute-start | bytes 1400840 | tf_op jit(solution)/shard_map/ppermute | solution.py:28
  108.9 1.1 copy-start.4
  108.9 1.1 copy-start.5
  109.3 0.8 copy-start.6
  109.9 0.8 copy-start.7
  109.9 1.4 %copy-start.8 = (f32[16,224,128]{2,1,0:T(8,128)}, f32[16,224,128]{2,1,0:T(8,128)S(1)}, u32[]{:S(2)}) copy-start(f32[16,224,128]{2,1,0:T(8,128)S(1)} %collective-permute-done.17.refs_4_) | copy-start | bytes 5505028
